TPU v7x, 32 devices: a whole 2x2x4 slice. The times are simulated.
32 devices in a mesh: rep: 4 (over z), seq: 2 (over x), tp: 4 (over y, core).
Axes of the slice: x: 2, y: 2, z: 4, core: 2. Of those that a mesh axis runs over, the one named last changes fastest.
Arguments:
- hidden_in: float32 [8, 1024, 2048], P('rep', 'seq'), may hold values from -6 to 6
- cotangent: float32 [8, 1024, 2048], P('rep', 'seq'), may hold values from -6 to 6
- w_qkv: bfloat16 [1, 2048, 4, 640], P(None, 'seq', 'tp'), may hold values from -0.125 to 0.125
- w_out: bfloat16 [1, 2048, 2048], P(None, 'tp', 'seq'), may hold values from -0.5 to 0.5
- w_gate_up: bfloat16 [1, 2048, 2, 5632], P(None, 'seq', None, 'tp'), may hold values from -0.125 to 0.125
- w_down: bfloat16 [1, 5632, 2048], P(None, 'tp', 'seq'), may hold values from -0.078125 to 0.078125
- norm_gains: bfloat16 [1, 2, 2048], P(None, None, 'seq'), may hold values from 0.099609375 to 1.8984375
- segments: int32 [8, 1024], P('rep'), may hold values from 0 to 3, never falling along the last dimension, each value on 1 to 512 neighbouring positions
Outputs:
- hidden_out: float32 [8, 1024, 2048], P('rep', 'seq')
- grad_in: float32 [8, 1024, 2048], P('rep', 'seq')
- grad_qkv: float32 [1, 2048, 4, 640], P(None, 'seq', 'tp')
- grad_out: float32 [1, 2048, 2048], P(None, 'tp', 'seq')
- grad_gate_up: float32 [1, 2048, 2, 5632], P(None, 'seq', None, 'tp')
- grad_down: float32 [1, 5632, 2048], P(None, 'tp', 'seq')
- grad_gains: float32 [1, 2, 2048], P(None, None, 'seq')
Inputs may be any that keep to these rules, and one draw needn't show every extreme that they name: `segments`: in each sequence the document number never falls, each of 0 to 3 occurs, a document has 1 to 512 tokens and one has exactly 512.
All inputs are finite; a program needn't handle non-finite values.
Results may differ from a plain program's by a relative error of at most 0.013.
Values may be sent and summed in bfloat16 or wider, within the bound.
No kernel may reach another device: no remote copies, remote signals or barrier semaphores. Data moves between devices by JAX's collectives and lax.ppermute only.
A program may use at most 320 MiB of HBM per device.

v0:
```python
import jax
import jax.numpy as jnp
from jax import lax
from jax.sharding import PartitionSpec as P

HEAD_DIM = 64


NORM_EPS = 1e-05
ROPE_THETA = 10000.0


def doc_positions(seg_ids):
    column_ids = jnp.arange(seg_ids.shape[1], dtype=jnp.int32)
    change = jnp.concatenate(
        [jnp.ones(seg_ids[:, :1].shape, dtype=bool), seg_ids[:, 1:] != seg_ids[:, :-1]], axis=1
    )
    doc_start = lax.cummax(jnp.where(change, column_ids[None, :], 0), axis=1)
    return column_ids[None, :] - doc_start


def rope_tables(positions, half_dim):
    inverse_freq = ROPE_THETA ** (-(jnp.arange(half_dim, dtype=jnp.float32) / half_dim))
    angles = positions.astype(jnp.float32)[..., None] * inverse_freq
    return (jnp.cos(angles), jnp.sin(angles))


def rotate(values, cos_tab, sin_tab):
    half_dim = values.shape[-1] // 2
    first_half = values[..., :half_dim]
    second_half = values[..., half_dim:]
    return jnp.concatenate(
        [
            first_half * cos_tab - second_half * sin_tab,
            second_half * cos_tab + first_half * sin_tab,
        ],
        axis=-1,
    )


def unrotate(upstream, cos_tab, sin_tab):
    half_dim = upstream.shape[-1] // 2
    first_half = upstream[..., :half_dim]
    second_half = upstream[..., half_dim:]
    return jnp.concatenate(
        [
            first_half * cos_tab + second_half * sin_tab,
            second_half * cos_tab - first_half * sin_tab,
        ],
        axis=-1,
    )


def rms_norm(hidden, gain_row):
    inv_rms = lax.rsqrt(jnp.mean(hidden * hidden, axis=-1, keepdims=True) + NORM_EPS)
    return (hidden * inv_rms * gain_row, inv_rms)


def rms_back(hidden, inv_rms, gain_row, upstream):
    weighted = gain_row * upstream
    grad_hidden = inv_rms * weighted - hidden * inv_rms * inv_rms * inv_rms * jnp.mean(
        weighted * hidden, axis=-1, keepdims=True
    )
    grad_gain = jnp.sum(upstream * hidden * inv_rms, axis=0)
    return (grad_hidden, grad_gain)


def per_device(hidden_in, cotangent, w_qkv, w_out, w_gate_up, w_down, norm_gains, segments):
    seq_count, local_len, model_width = hidden_in.shape
    full_len = segments.shape[1]
    kv_local = w_qkv.shape[2]
    qkv_width = w_qkv.shape[3]
    kv_group = qkv_width // HEAD_DIM - 2
    ff_local = w_down.shape[1]
    layer_count = w_qkv.shape[0]
    row_count = seq_count * local_len
    att_scale = float(HEAD_DIM) ** (-0.5)
    first_row = lax.axis_index("seq") * local_len
    all_positions = doc_positions(segments)
    pos_mine = lax.dynamic_slice_in_dim(all_positions, first_row, local_len, 1)
    seg_mine = lax.dynamic_slice_in_dim(segments, first_row, local_len, 1)
    query_ids = first_row + jnp.arange(local_len, dtype=jnp.int32)
    key_ids_all = jnp.arange(full_len, dtype=jnp.int32)
    cos_tab, sin_tab = rope_tables(pos_mine, HEAD_DIM // 2)
    q_cos = cos_tab[:, :, None, None, :]
    q_sin = sin_tab[:, :, None, None, :]
    k_cos = cos_tab[:, :, None, :]
    k_sin = sin_tab[:, :, None, :]
    hidden = hidden_in.reshape(row_count, model_width)
    kept_weights = []
    layer_no = 0
    weights = (
        lax.all_gather(w_qkv[layer_no], "seq", axis=0, tiled=True),
        lax.all_gather(w_out[layer_no], "seq", axis=1, tiled=True),
        lax.all_gather(w_gate_up[layer_no], "seq", axis=0, tiled=True),
        lax.all_gather(w_down[layer_no], "seq", axis=1, tiled=True),
        lax.all_gather(norm_gains[layer_no], "seq", axis=1, tiled=True),
    )
    qkv_full, out_full, gu_full, down_full, gains_half = weights
    gains_full = gains_half.astype(jnp.float32)
    qkv_matrix = qkv_full.reshape(model_width, kv_local * qkv_width)
    normed1, inv_rms1 = rms_norm(hidden, gains_full[0])
    normed1 = normed1.astype(jnp.bfloat16)
    projected = jnp.dot(normed1, qkv_matrix, preferred_element_type=jnp.float32).reshape(
        seq_count, local_len, kv_local, qkv_width
    )
    queries = projected[..., : kv_group * HEAD_DIM].reshape(
        seq_count, local_len, kv_local, kv_group, HEAD_DIM
    )
    keys = projected[..., kv_group * HEAD_DIM : (kv_group + 1) * HEAD_DIM]
    values = projected[..., (kv_group + 1) * HEAD_DIM :]
    q_rot = rotate(queries, q_cos, q_sin).astype(jnp.bfloat16)
    k_rot = rotate(keys, k_cos, k_sin).astype(jnp.bfloat16)
    packed = jnp.concatenate([k_rot, values.astype(jnp.bfloat16)], axis=-1)
    start_top = jnp.full((seq_count, kv_local, kv_group, local_len), -1e30, jnp.float32)
    shard_piece = lax.all_gather(packed, "seq", axis=1, tiled=True)
    top_score = start_top
    key_count = shard_piece.shape[1]
    key_ids = jnp.arange(key_count, dtype=jnp.int32)
    piece_keys = shard_piece[..., :HEAD_DIM]
    piece_vals = shard_piece[..., HEAD_DIM:]
    attend_scores = (
        jnp.einsum("sqkgd,snkd->skgqn", q_rot, piece_keys, preferred_element_type=jnp.float32)
        * att_scale
    )
    attend_allowed = (key_ids[None, None, :] <= query_ids[None, :, None]) & (
        segments[:, None, :] == seg_mine[:, :, None]
    )
    attend_allowed = attend_allowed[:, None, None]
    new_top = jnp.maximum(
        top_score, jnp.max(jnp.where(attend_allowed, attend_scores, -1e30), axis=-1)
    )
    expo = jnp.where(
        attend_allowed,
        jnp.exp(jnp.where(attend_allowed, attend_scores, new_top[..., None]) - new_top[..., None]),
        0.0,
    )
    totals = jnp.sum(expo, axis=-1)
    accum = jnp.einsum(
        "skgqn,snkd->skgqd",
        expo.astype(jnp.bfloat16),
        piece_vals,
        preferred_element_type=jnp.float32,
    )
    top_score, totals, accum = (new_top, totals, accum)
    mixed = jnp.transpose(accum / totals[..., None], (0, 3, 1, 2, 4)).astype(jnp.bfloat16)
    log_total = top_score + jnp.log(totals)
    mixed_rows = mixed.reshape(row_count, kv_local * kv_group * HEAD_DIM)
    hidden2 = hidden + lax.psum(
        jnp.dot(mixed_rows, out_full, preferred_element_type=jnp.float32), "tp"
    )
    normed2, inv_rms2 = rms_norm(hidden2, gains_full[1])
    normed2 = normed2.astype(jnp.bfloat16)
    gate_up = jnp.dot(
        normed2, gu_full.reshape(model_width, 2 * ff_local), preferred_element_type=jnp.float32
    )
    gate_up = gate_up.reshape(row_count, 2, ff_local)
    gate_val = gate_up[:, 0]
    up_val = gate_up[:, 1]
    act_val = (jax.nn.silu(gate_val) * up_val).astype(jnp.bfloat16)
    hidden3 = hidden2 + lax.psum(
        jnp.dot(act_val, down_full, preferred_element_type=jnp.float32), "tp"
    )
    hidden, cache = (
        hidden3,
        (
            hidden,
            inv_rms1,
            normed1,
            q_rot,
            packed,
            mixed,
            mixed_rows,
            log_total,
            hidden2,
            inv_rms2,
            normed2,
            gate_val,
            up_val,
            act_val,
        ),
    )
    caches = [cache]
    kept_weights.append(weights)
    d_hidden = cotangent.reshape(row_count, model_width)
    grads = [None] * layer_count
    for layer_no in reversed(range(layer_count)):
        weights = (
            lax.all_gather(w_qkv[layer_no], "seq", axis=0, tiled=True),
            lax.all_gather(w_out[layer_no], "seq", axis=1, tiled=True),
            lax.all_gather(w_gate_up[layer_no], "seq", axis=0, tiled=True),
            lax.all_gather(w_down[layer_no], "seq", axis=1, tiled=True),
            lax.all_gather(norm_gains[layer_no], "seq", axis=1, tiled=True),
        )
        (
            backward_hidden,
            backward_inv_rms1,
            backward_normed1,
            backward_q_rot,
            backward_packed,
            backward_mixed,
            backward_mixed_rows,
            backward_log_total,
            backward_hidden2,
            backward_inv_rms2,
            backward_normed2,
            backward_gate_val,
            backward_up_val,
            backward_act_val,
        ) = caches[layer_no]
        (
            backward_qkv_full,
            backward_out_full,
            backward_gu_full,
            backward_down_full,
            backward_gains_half,
        ) = weights
        backward_gains_full = backward_gains_half.astype(jnp.float32)
        backward_qkv_matrix = backward_qkv_full.reshape(model_width, kv_local * qkv_width)
        gu_matrix = backward_gu_full.reshape(model_width, 2 * ff_local)
        d_hid_b = d_hidden.astype(jnp.bfloat16)
        g_down = jnp.dot(backward_act_val.T, d_hid_b, preferred_element_type=jnp.float32)
        d_act = jnp.dot(d_hid_b, backward_down_full.T, preferred_element_type=jnp.float32)
        sigm = jax.nn.sigmoid(backward_gate_val)
        d_gate = d_act * backward_up_val * sigm * (1.0 + backward_gate_val * (1.0 - sigm))
        d_up = d_act * backward_gate_val * sigm
        d_gu = (
            jnp.stack([d_gate, d_up], axis=1).astype(jnp.bfloat16).reshape(row_count, 2 * ff_local)
        )
        g_gate_up = jnp.dot(backward_normed2.T, d_gu, preferred_element_type=jnp.float32).reshape(
            model_width, 2, ff_local
        )
        d_normed2 = lax.psum(jnp.dot(d_gu, gu_matrix.T, preferred_element_type=jnp.float32), "tp")
        d_hidden2, g_gain2 = rms_back(
            backward_hidden2, backward_inv_rms2, backward_gains_full[1], d_normed2
        )
        d_hidden2 = d_hidden2 + d_hidden
        d_hid2_b = d_hidden2.astype(jnp.bfloat16)
        g_out = jnp.dot(backward_mixed_rows.T, d_hid2_b, preferred_element_type=jnp.float32)
        d_mixed = jnp.dot(d_hid2_b, backward_out_full.T, preferred_element_type=jnp.float32).astype(
            jnp.bfloat16
        )
        d_mixed = d_mixed.reshape(seq_count, local_len, kv_local, kv_group, HEAD_DIM)
        whole_keys = lax.all_gather(backward_packed, "seq", axis=1, tiled=True)

        def per_sequence(items):
            queries, d_mix, mix_val, log_tot, seg_q, seg_all, key_vals = items
            all_keys = key_vals[..., :HEAD_DIM]
            all_vals = key_vals[..., HEAD_DIM:]
            allowed = (
                (key_ids_all[None, :] <= query_ids[:, None]) & (seg_all[None, :] == seg_q[:, None])
            )[None, None]
            scores = (
                jnp.einsum("qkgd,nkd->kgqn", queries, all_keys, preferred_element_type=jnp.float32)
                * att_scale
            )
            probs = jnp.where(
                allowed,
                jnp.exp(jnp.where(allowed, scores, log_tot[..., None]) - log_tot[..., None]),
                0.0,
            )
            delta = jnp.transpose(
                jnp.sum(d_mix.astype(jnp.float32) * mix_val.astype(jnp.float32), axis=-1), (1, 2, 0)
            )
            d_values = jnp.einsum(
                "kgqn,qkgd->nkd",
                probs.astype(jnp.bfloat16),
                d_mix,
                preferred_element_type=jnp.float32,
            )
            d_probs = jnp.einsum(
                "qkgd,nkd->kgqn", d_mix, all_vals, preferred_element_type=jnp.float32
            )
            d_scores = (probs * (d_probs - delta[..., None]) * att_scale).astype(jnp.bfloat16)
            d_queries = jnp.einsum(
                "kgqn,nkd->qkgd", d_scores, all_keys, preferred_element_type=jnp.float32
            )
            d_keys = jnp.einsum(
                "kgqn,qkgd->nkd", d_scores, queries, preferred_element_type=jnp.float32
            )
            return (d_queries, jnp.concatenate([d_keys, d_values], axis=-1))

        d_queries, d_packed = lax.map(
            per_sequence,
            (
                backward_q_rot,
                d_mixed,
                backward_mixed,
                backward_log_total,
                seg_mine,
                segments,
                whole_keys,
            ),
        )
        d_packed = lax.psum_scatter(d_packed, "seq", scatter_dimension=1, tiled=True)
        d_queries = unrotate(d_queries, q_cos, q_sin)
        d_keys = unrotate(d_packed[..., :HEAD_DIM], k_cos, k_sin)
        d_values = d_packed[..., HEAD_DIM:]
        d_qkv = jnp.concatenate(
            [
                d_queries.reshape(seq_count, local_len, kv_local, kv_group * HEAD_DIM),
                d_keys,
                d_values,
            ],
            axis=-1,
        )
        d_qkv = d_qkv.astype(jnp.bfloat16).reshape(row_count, kv_local * qkv_width)
        g_qkv = jnp.dot(backward_normed1.T, d_qkv, preferred_element_type=jnp.float32).reshape(
            model_width, kv_local, qkv_width
        )
        d_normed1 = lax.psum(
            jnp.dot(d_qkv, backward_qkv_matrix.T, preferred_element_type=jnp.float32), "tp"
        )
        d_prev, g_gain1 = rms_back(
            backward_hidden, backward_inv_rms1, backward_gains_full[0], d_normed1
        )
        d_hidden = d_prev + d_hidden2
        layer_grads = (g_qkv, g_out, g_gate_up, g_down, jnp.stack([g_gain1, g_gain2]))
        grads[layer_no] = lax.psum(
            (
                lax.psum_scatter(layer_grads[0], "seq", scatter_dimension=0, tiled=True),
                lax.psum_scatter(layer_grads[1], "seq", scatter_dimension=1, tiled=True),
                lax.psum_scatter(layer_grads[2], "seq", scatter_dimension=0, tiled=True),
                lax.psum_scatter(layer_grads[3], "seq", scatter_dimension=1, tiled=True),
                lax.psum_scatter(layer_grads[4], "seq", scatter_dimension=1, tiled=True),
            ),
            "rep",
        )
    hidden_out = hidden.reshape(seq_count, local_len, model_width)
    grad_in = d_hidden.reshape(seq_count, local_len, model_width)
    grad_qkv = jnp.stack([item[0] for item in grads])
    grad_out = jnp.stack([item[1] for item in grads])
    grad_gate_up = jnp.stack([item[2] for item in grads])
    grad_down = jnp.stack([item[3] for item in grads])
    grad_gains = jnp.stack([item[4] for item in grads])
    return (hidden_out, grad_in, grad_qkv, grad_out, grad_gate_up, grad_down, grad_gains)


def solution(mesh):
    in_specs = (
        P("rep", "seq", None),
        P("rep", "seq", None),
        P(None, "seq", "tp", None),
        P(None, "tp", "seq"),
        P(None, "seq", None, "tp"),
        P(None, "tp", "seq"),
        P(None, None, "seq"),
        P("rep", None),
    )
    out_specs = (
        P("rep", "seq", None),
        P("rep", "seq", None),
        P(None, "seq", "tp", None),
        P(None, "tp", "seq"),
        P(None, "seq", None, "tp"),
        P(None, "tp", "seq"),
        P(None, None, "seq"),
    )
    return jax.shard_map(
        per_device, mesh=mesh, in_specs=in_specs, out_specs=out_specs, check_vma=False
    )
```

profile of v0, /device:TPU:0, one launch (start us, length us, event | category | flops | bytes accessed | tf_op | source)
XLA Modules:
  0.0 2411.3 jit_solution(18099197908531968922)
XLA Ops:
  16.1 5.2 all-gather
  23.3 28.1 %all-gather.10.cloned.1.call-done = bf16[1,2048,1,640]{3,1,2,0:T(8,128)(2,1)} async-done(((bf16[1,1024,1,640]{3,1,2,0:T(8,128)(2,1)}), bf16[1,2048,1,640]{3,1,2,0:T(8,128)(2,1)}) %all-gather.10.cloned.1.call-update) | async-done | bytes 2621456 | tf_op jit(solution)/shard_map/all_gather | solution.py:93
  51.3 6.5 fusion.102
  58.7 13.9 all_gather.26
  72.9 13.6 fusion.48
  86.6 14.7 fusion.52
  101.3 16.2 divide_convert_fusion
  120.1 7.7 fusion.97
  128.3 6.0 copy.111
  135.0 10.6 fusion.142
  145.6 135.4 %all-reduce.8.cloned.1.call-done = f32[1024,2048]{1,0:T(8,128)} async-done(((f32[1024,2048]{1,0:T(8,128)}), f32[1024,2048]{1,0:T(8,128)}) %all-reduce.8.cloned.1.call-update) | async-done | bytes 8388624 | tf_op jit(solution)/shard_map/psum | solution.py:149
  281.0 11.7 multiply_reduce_fusion.3
  292.7 130.2 %all-gather.14.cloned.1.call-done = bf16[1,2048,2,1408]{3,1,2,0:T(8,128)(2,1)} async-done(((bf16[1,1024,2,1408]{3,1,2,0:T(8,128)(2,1)}), bf16[1,2048,2,1408]{3,1,2,0:T(8,128)(2,1)}) %all-gather.14.cloned.1.call-update) | async-done | bytes 11534352 | tf_op jit(solution)/shard_map/all_gather | solution.py:95
  422.8 15.8 copy.112
  438.7 20.2 fusion.58
  458.9 39.9 %all-gather.16.cloned.1.call-done = bf16[1,1408,2048]{2,1,0:T(8,128)(2,1)} async-done(((bf16[1,1408,1024]{2,1,0:T(8,128)(2,1)}), bf16[1,1408,2048]{2,1,0:T(8,128)(2,1)}) %all-gather.16.cloned.1.call-update) | async-done | bytes 5767184 | tf_op jit(solution)/shard_map/all_gather | solution.py:96
  498.7 14.1 fusion.74
  515.3 16.9 fusion.81
  533.1 152.3 %all-reduce.10.cloned.1.call-done = f32[1024,2048]{1,0:T(8,128)} async-done(((f32[1024,2048]{1,0:T(8,128)}), f32[1024,2048]{1,0:T(8,128)}) %all-reduce.10.cloned.1.call-update) | async-done | bytes 8388624 | tf_op jit(solution)/shard_map/psum | solution.py:233
  685.3 8.0 multiply_reduce_fusion.1
  693.6 7.3 bitcast_add_fusion
  711.8 62.3 %while.13 = (s32[]{:T(128)}, f32[2,512,1,8,64]{1,4,3,2,0:T(8,128)}, f32[2,1024,1,128]{1,3,2,0:T(8,128)}, bf16[2,1024,1,128]{1,3,2,0:T(8,128)(2,1)S(1)}, s32[2,10...) while((s32[]{:T(128)}, f32[2,512,1,8,64]{1,4,3,2,0:T(8,128)}, ...), condition=%wide.region_12.13_spmd.clone, body=%wide.region_10.12_spmd.clone.sunk | while | flops 2741629440 | bytes 126081328 | solution.py:283
  717.4 5.7 fusion.178
  723.1 9.9 fusion.176
  733.1 6.1 fusion.179
  748.4 5.7 fusion.178
  754.1 9.9 fusion.176
  764.0 6.1 fusion.179
  774.3 13.4 fusion.69
  789.6 5.2 reduce-scatter.9.cloned.1.call-done
  797.8 7.9 fusion.93
  806.9 7.7 fusion.99
  814.6 14.3 fusion.89
  829.6 265.1 %all-reduce.12.cloned.1.call-done = (f32[1024,2048]{1,0:T(8,128)}, f32[1024,2048]{1,0:T(8,128)}) async-done(((f32[1024,2048]{1,0:T(8,128)}, f32[1024,2048]{1,0:T(8,128)}), (f32[1024,2048]{1,0:T(8,128)}, f32[1024,2048]{1,0:T(8,128)})) %all-reduce.12.cloned.1.call-update) | async-done | bytes 16777232 | tf_op jit(solution)/shard_map/psum | solution.py:161
  1094.7 7.2 fusion.64
  1102.9 9.8 multiply_convert_fusion
  1112.6 5.2 convolution_bitcast_fusion
  1122.9 8.5 copy.123
  1131.4 21.3 fusion.65
  1154.8 132.5 %reduce-scatter.17.cloned.1.call-done = f32[1408,1024]{1,0:T(8,128)} async-done(((f32[1408,2048]{1,0:T(8,128)}), f32[1408,1024]{1,0:T(8,128)}) %reduce-scatter.17.cloned.1.call-update) | async-done | bytes 5767184 | tf_op jit(solution)/shard_map/reduce_scatter | solution.py:324
  1287.3 68.0 %reduce-scatter.11.cloned.1.call-done = f32[1024,1,640]{2,0,1:T(8,128)} async-done(((f32[2048,1,640]{2,0,1:T(8,128)}), f32[1024,1,640]{2,0,1:T(8,128)}) %reduce-scatter.11.cloned.1.call-update) | async-done | bytes 2621456 | tf_op jit(solution)/shard_map/reduce_scatter | solution.py:321
  1355.3 259.1 %reduce-scatter.15.cloned.1.call-done = f32[1024,2,1408]{2,0,1:T(8,128)} async-done(((f32[2048,2,1408]{2,0,1:T(8,128)}), f32[1024,2,1408]{2,0,1:T(8,128)}) %reduce-scatter.15.cloned.1.call-update) | async-done | bytes 11534352 | tf_op jit(solution)/shard_map/reduce_scatter | solution.py:323
  1614.4 11.9 add.123
  1626.3 11.4 reduce-scatter.19.cloned.1.call-done
  1638.9 12.8 psum.71
  1651.7 722.6 %all-reduce.14.cloned.1.call-done = (f32[1,1024,1,640]{3,1,2,0:T(8,128)}, f32[1,512,1024]{2,1,0:T(8,128)}, f32[1,1024,2,1408]{3,1,2,0:T(8,128)}, f32[1,1408,1024]{2,1,0:T(8,128)}) async-done(((f32[1,1024,1,640]{3,1,2,0:T(8,128)}, f32[1,512,1024]{2,1,0:T(8,128)}, f32[1,1024,2,1408]{3,1,2,0:T(8,128)}, f32[1,1408,1024]{2,1,0:T(8,128)}), (f32[1,1024,1,640]{3,1,2,0:T(8,128)}, f32[1,512,1024]{2,1,0:T(8,128)}, ...) | async-done | bytes 22020112 | tf_op jit(solution)/shard_map/psum | solution.py:319
  2374.3 6.0 copy.125
  2380.3 20.4 copy.126
  (208 shorter events, 68.2 us)
Async XLA Ops:
  7.2 15.1 copy-start.21
  7.2 8.9 copy-start.40
  7.2 44.1 %all-gather.10.cloned.1.call-start = ((), (), s32[]{:S(2)}) async-start(), calls=%async_computation.13 | async-start | bytes 3932160 | tf_op jit(solution)/shard_map/all_gather | solution.py:93
  7.9 112.2 %all-gather.12.cloned.1.call-start = ((), (), s32[]{:S(2)}) async-start(), calls=%async_computation.14 | async-start | bytes 3145728 | tf_op jit(solution)/shard_map/all_gather | solution.py:94
  8.7 272.3 %all-reduce.8.cloned.1.call-start = ((), (), s32[]{:S(2)}) async-start(), calls=%async_computation.6 | async-start | bytes 16777216 | tf_op jit(solution)/shard_map/psum | solution.py:149
  8.7 49.1 %copy-start.38 = (f32[32]{0:T(128)}, f32[32]{0:T(128)S(1)}, u32[]{:S(2)}) copy-start(f32[32]{0:T(128)S(1)} %negate_power_fusion) | copy-start | bytes 388
  10.3 47.5 %copy-start.27 = (s32[2,512]{1,0:T(2,128)}, s32[2,512]{1,0:T(2,128)S(1)}, u32[]{:S(2)}) copy-start(s32[2,512]{1,0:T(2,128)S(1)} %constant_dynamic-slice_fusion.2) | copy-start | bytes 12292
  11.5 46.4 %copy-start.32 = (f32[2,512]{1,0:T(2,128)}, f32[2,512]{1,0:T(2,128)S(1)}, u32[]{:S(2)}) copy-start(f32[2,512]{1,0:T(2,128)S(1)} %fusion.135) | copy-start | bytes 12292
  21.4 36.5 %copy-start.30 = (f32[1,1,2048]{2,1,0:T(1,128)}, f32[1,1,2048]{2,1,0:T(1,128)S(1)}, u32[]{:S(2)}) copy-start(f32[1,1,2048]{2,1,0:T(1,128)S(1)} %get-tuple-element.237) | copy-start | bytes 24580
  21.4 672.0 %copy-start.28 = (f32[1,1,2048]{2,1,0:T(1,128)}, f32[1,1,2048]{2,1,0:T(1,128)S(1)}, u32[]{:S(2)}) copy-start(f32[1,1,2048]{2,1,0:T(1,128)S(1)} %get-tuple-element.236) | copy-start | bytes 24580
  22.3 50.3 %copy-start.9 = (f32[2,512,32]{1,2,0:T(8,128)}, f32[2,512,32]{1,2,0:T(8,128)S(1)}, u32[]{:S(2)}) copy-start(f32[2,512,32]{1,2,0:T(8,128)S(1)} %get-tuple-element.238) | copy-start | bytes 393220
  22.3 50.2 %copy-start.11 = (f32[2,512,32]{1,2,0:T(8,128)}, f32[2,512,32]{1,2,0:T(8,128)S(1)}, u32[]{:S(2)}) copy-start(f32[2,512,32]{1,2,0:T(8,128)S(1)} %get-tuple-element.239) | copy-start | bytes 393220
  86.5 14.7 copy-start.23
  101.3 16.2 copy-start.25
  120.0 7.8 copy-start.13
  127.9 295.0 %all-gather.14.cloned.1.call-start = ((), (), s32[]{:S(2)}) async-start(), calls=%async_computation.15 | async-start | bytes 17301504 | tf_op jit(solution)/shard_map/all_gather | solution.py:95
  134.4 364.4 %all-gather.16.cloned.1.call-start = ((), (), s32[]{:S(2)}) async-start(), calls=%async_computation.16 | async-start | bytes 8650752 | tf_op jit(solution)/shard_map/all_gather | solution.py:96
  135.0 550.4 %all-reduce.10.cloned.1.call-start = ((), (), s32[]{:S(2)}) async-start(), calls=%async_computation.7 | async-start | bytes 16777216 | tf_op jit(solution)/shard_map/psum | solution.py:233
  292.7 400.7 %copy-start.34 = (f32[1024]{0:T(1024)}, f32[1024]{0:T(1024)S(1)}, u32[]{:S(2)}) copy-start(f32[1024]{0:T(1024)S(1)} %add_rsqrt_fusion) | copy-start | bytes 12292
  532.3 262.5 %reduce-scatter.9.cloned.1.call-start = ((), (), s32[]{:S(2)}) async-start(), calls=%async_computation.8 | async-start | bytes 1572864 | tf_op jit(solution)/shard_map/reduce_scatter | solution.py:295
  685.3 8.2 copy-start.2
  693.6 10.5 copy-start.41
  704.1 7.8 copy-start.22
  733.1 8.7 copy-start.15
  733.1 9.7 copy-start.20
  764.0 8.7 copy-start.15
  764.0 9.7 copy-start.20
  774.2 13.5 copy-start.8
  774.2 13.5 copy-start.10
  774.2 13.5 copy-start.12
  774.2 320.4 %all-reduce.12.cloned.1.call-start = ((), (), s32[]{:S(2)}) async-start(), calls=%async_computation.18 | async-start | bytes 33554432 | tf_op jit(solution)/shard_map/psum | solution.py:161
  787.7 8.2 copy-start.33
  787.7 8.2 copy-start.39
  797.8 7.9 copy-start.17
  805.7 349.2 %reduce-scatter.13.cloned.1.call-start = ((), (), s32[]{:S(2)}) async-start(), calls=%async_computation.10 | async-start | bytes 6291456 | tf_op jit(solution)/shard_map/reduce_scatter | solution.py:322
  814.5 472.8 %reduce-scatter.17.cloned.1.call-start = ((), (), s32[]{:S(2)}) async-start(), calls=%async_computation.12 | async-start | bytes 17301504 | tf_op jit(solution)/shard_map/reduce_scatter | solution.py:324
  828.9 265.8 %copy-start.31 = (f32[1,1,2048]{2,1,0:T(1,128)S(1)}, f32[1,1,2048]{2,1,0:T(1,128)}, u32[]{:S(2)}) copy-start(f32[1,1,2048]{2,1,0:T(1,128)} %copy-done.30) | copy-start | bytes 24580
  828.9 526.4 %reduce-scatter.11.cloned.1.call-start = ((), (), s32[]{:S(2)}) async-start(), calls=%async_computation.9 | async-start | bytes 7864320 | tf_op jit(solution)/shard_map/reduce_scatter | solution.py:321
  1094.7 8.2 copy-start.1
  1102.9 9.8 copy-start.18
  1117.9 496.5 %reduce-scatter.15.cloned.1.call-start = ((), (), s32[]{:S(2)}) async-start(), calls=%async_computation.11 | async-start | bytes 34603008 | tf_op jit(solution)/shard_map/reduce_scatter | solution.py:323
  1122.9 8.5 copy-start.29
  1122.9 8.5 copy-start.35
  1152.7 484.9 %reduce-scatter.19.cloned.1.call-start = ((), (), s32[]{:S(2)}) async-start(), calls=%async_computation.17 | async-start | bytes 1572864
  1154.8 1219.5 %all-reduce.14.cloned.1.call-start = ((), (), s32[]{:S(2)}) async-start(), calls=%async_computation.19 | async-start | bytes 44040192 | tf_op jit(solution)/shard_map/psum | solution.py:319
  2374.3 27.8 %slice-start = ((s8[5767168]{0:T(1024)(128)(4,1)}), s8[1572864]{0:T(1024)(128)(4,1)S(1)}, s32[]{:S(2)}) async-start(s8[5767168]{0:T(1024)(128)(4,1)} %bitcast.379), calls=%async_computation.20 | async-start | bytes 3145728
  2380.3 20.4 copy-start.7
  2380.3 21.7 slice-start.1
  (15 other events, 36.4 us)
Sparse Core Ops, SparseCore 0:
  9.6 41.7 all-gather.9
  52.9 37.1 all-gather.11
  128.0 152.9 all-reduce.7
  283.0 139.8 all-gather.13
  424.2 74.4 all-gather.15
  532.4 152.8 all-reduce.9
  774.3 20.4 reduce-scatter.8
  805.8 288.8 all-reduce.11
  1097.1 54.2 reduce-scatter.12
  1154.1 133.1 reduce-scatter.16
  1289.6 65.6 reduce-scatter.10
  1357.6 256.7 reduce-scatter.14
  1617.3 20.3 reduce-scatter.18
  1640.4 733.8 all-reduce.13
where the time goes:
time: 2420 us; the launch traced here: 2410 us
  waiting for transfers between devices  1950 us (81%)
  matrix products  221 us (9%)
  other arithmetic  101 us (4%)
  local copies, waits for them, and re-layouts  89.5 us (4%)
  blocking collectives  31.9 us (1%)
    psum x1, waiting for transfers between devices, per_device(): lax.psum((lax.psum_scatter(layer_grads[0], 'seq', scatter_dimension=0, ti...  723 us
    psum x1, waiting for transfers between devices, per_device(): lax.psum(jnp.dot(act_val, down_full, preferred_element_type=jnp.float32),...  265 us
    reduce_scatter x1, waiting for transfers between devices, per_device(): lax.psum_scatter(layer_grads[2], 'seq', scatter_dimension=0, tiled=True)  259 us
    psum x1, waiting for transfers between devices, per_device(): lax.psum(jnp.dot(d_gu, gu_matrix.T, preferred_element_type=jnp.float32),...  152 us
    psum x1, waiting for transfers between devices, per_device(): lax.psum(jnp.dot(mixed_rows, out_full, preferred_element_type=jnp.float32...  135 us
    reduce_scatter x1, waiting for transfers between devices, per_device(): lax.psum_scatter(layer_grads[3], 'seq', scatter_dimension=1, tiled=True)  132 us
    all_gather x1, waiting for transfers between devices, per_device(): lax.all_gather(w_gate_up[layer_no], 'seq', axis=0, tiled=True)  130 us
    reduce_scatter x1, waiting for transfers between devices, per_device(): lax.psum_scatter(layer_grads[0], 'seq', scatter_dimension=0, tiled=True)  68 us
  transfers between devices with their start and end apart: 14, of which 12 were waited for; matrix products, arithmetic and copies ran while one was open for 10% of the time, Pallas kernels for 0%

commit v1 on v0

v1 whole, which is shorter than its diff:
```python
import functools

import jax
import jax.numpy as jnp
from jax import lax
from jax.experimental import pallas as pl
from jax.experimental.pallas import tpu as pltpu
from jax.sharding import PartitionSpec as P

HEAD_DIM = 64
NORM_EPS = 1e-05
ROPE_THETA = 10000.0
LOG2E = 1.4426950408889634
MASKED = -1e30
F32 = jnp.float32
BF16 = jnp.bfloat16
VMEM_BYTES = 48 * 1024 * 1024


def dot(a, b, ca=1, cb=0):
    return lax.dot_general(a, b, (((ca,), (cb,)), ((), ())), preferred_element_type=F32)


def call(body, grid, ins, outs, shapes, scratch=(), scalars=0, alias=None):
    return pl.pallas_call(
        body,
        out_shape=shapes,
        grid_spec=pltpu.PrefetchScalarGridSpec(
            num_scalar_prefetch=scalars,
            grid=grid,
            in_specs=ins,
            out_specs=outs,
            scratch_shapes=list(scratch),
        ),
        input_output_aliases=alias or {},
        compiler_params=pltpu.CompilerParams(vmem_limit_bytes=VMEM_BYTES),
        cost_estimate=pl.CostEstimate(flops=1, bytes_accessed=1, transcendentals=0),
    )


class Order:
    def __init__(self):
        self.last = ()

    def __call__(self, step, *xs):
        flat, tree = jax.tree.flatten(xs)
        if self.last:
            flat = lax.optimization_barrier((tuple(flat), self.last))[0]
        out = step(*jax.tree.unflatten(tree, flat))
        self.last = tuple(jax.tree.leaves(out))
        return out


def first_norm(hidden, gain, place, block):
    rows, width = hidden.shape
    half = width // 2

    def body(p, a_ref, b_ref, g_ref, n_ref):
        a, b = a_ref[...], b_ref[...]
        total = jnp.sum(a * a, -1, keepdims=True) + jnp.sum(b * b, -1, keepdims=True)
        inv = lax.rsqrt(total * (1.0 / width) + NORM_EPS)
        n_ref[:, :half] = (a * inv * g_ref[:, :half]).astype(BF16)
        n_ref[:, half:] = (b * inv * g_ref[:, half:]).astype(BF16)

    return call(
        body,
        (rows // block,),
        [
            pl.BlockSpec((block, half), lambda i, p: (i, p[1])),
            pl.BlockSpec((block, half), lambda i, p: (i, 1 - p[1])),
            pl.BlockSpec((1, width), lambda i, p: (0, 0)),
        ],
        pl.BlockSpec((block, width), lambda i, p: (i, 0)),
        jax.ShapeDtypeStruct((rows, width), BF16),
        scalars=1,
    )(place, hidden, hidden, gain)


def local_cast(x, place, block):
    rows, width = x.shape
    half = width // 2

    def body(p, a_ref, b_ref, o_ref):
        o_ref[:, :half] = a_ref[...].astype(BF16)
        o_ref[:, half:] = b_ref[...].astype(BF16)

    def row(i, p):
        return (i // 4) * 4 + ((i % 4) ^ p[0])

    return call(
        body,
        (rows // block,),
        [
            pl.BlockSpec((block, half), lambda i, p: (row(i, p), p[1])),
            pl.BlockSpec((block, half), lambda i, p: (row(i, p), 1 - p[1])),
        ],
        pl.BlockSpec((block, width), lambda i, p: (i, 0)),
        jax.ShapeDtypeStruct((rows, width), BF16),
        scalars=1,
    )(place, x, x)


def add_local(x, deltas, place, block):
    rows, width = x.shape
    half = width // 2
    count = len(deltas)

    def body(p, x_ref, *refs):
        o_ref = refs[-1]
        i = pl.program_id(0)
        for k in range(count):

            @pl.when((i // 4) * 4 + ((i % 4) ^ p[0]) == k)
            def _():
                @pl.when(p[1] == 0)
                def _():
                    o_ref[...] = x_ref[...] + refs[k][...].astype(F32)

                @pl.when(p[1] == 1)
                def _():
                    o_ref[:, :half] = x_ref[:, :half] + refs[k][:, half:].astype(F32)
                    o_ref[:, half:] = x_ref[:, half:] + refs[k][:, :half].astype(F32)

    return call(
        body,
        (rows // block,),
        [pl.BlockSpec((block, width), lambda i, p: (i, 0))]
        + [pl.BlockSpec((block, width), lambda i, p: (0, 0))] * count,
        pl.BlockSpec((block, width), lambda i, p: (i, 0)),
        jax.ShapeDtypeStruct((rows, width), F32),
        scalars=1,
    )(place, x, *deltas)


def spread_gate_up(w, place, width, side, pieces, before):
    rows, _, ff = w.shape
    block = min(128, rows)
    steps = rows // block if side is None else rows // block // 2

    def body(p, w_ref, *refs):
        outs = refs[len(before) :]
        for j in range(ff // 128):
            for g in range(2):
                outs[0][:, 256 * j + 128 * g : 256 * j + 128 * (g + 1)] = w_ref[
                    :, g, 128 * j : 128 * (j + 1)
                ]
        for k in range(len(outs) - 1):

            @pl.when(pl.program_id(0) == k)
            def _():
                outs[k + 1][...] = outs[0][...]

    def row(i, p):
        if side is None:
            return i
        return i + steps * (p[2] if side == 0 else 1 - p[2])

    return call(
        body,
        (steps,),
        [pl.BlockSpec((block, 2, ff), lambda i, p: (row(i, p), 0, 0))]
        + [pl.BlockSpec(memory_space=pl.ANY)] * len(before),
        [pl.BlockSpec((block, 2 * ff), lambda i, p: (row(i, p), 0))]
        + [pl.BlockSpec((block, 2 * ff), lambda i, p: (0, 0))] * pieces,
        [jax.ShapeDtypeStruct((width, 2 * ff), BF16)]
        + [jax.ShapeDtypeStruct((block, 2 * ff), BF16)] * pieces,
        scalars=1,
        alias={2 + k: k for k in range(len(before))},
    )(place, w, *before)


def join_gate_up(a, b, middle, at, rows, before):
    count, cols = a.shape
    ff = cols // 2
    block = min(128, count)

    def body(p, a_ref, b_ref, *refs):
        o_ref = refs[-1]

        def put(src):
            for j in range(ff // 128):
                for g in range(2):
                    o_ref[0, :, g, 128 * j : 128 * (j + 1)] = src[
                        :, 256 * j + 128 * g : 256 * j + 128 * (g + 1)
                    ].astype(F32)

        @pl.when(p[0] == 1)
        def _():
            put(a_ref)

        @pl.when(p[0] == 0)
        def _():
            put(b_ref)

    return call(
        body,
        (count // block,),
        [pl.BlockSpec((block, cols), lambda i, p: (i, 0))] * 2
        + [pl.BlockSpec(memory_space=pl.ANY)] * len(before),
        pl.BlockSpec((1, block, 2, ff), lambda i, p: (0, at // block + i, 0, 0)),
        jax.ShapeDtypeStruct((1, rows, 2, ff), F32),
        scalars=1,
        alias={3 + k: k for k in range(len(before))},
    )(middle, a, b, *before)


def project_qkv(normed, weights, cos_t, sin_t, group):
    rows, width = normed.shape
    seqs, half, length = cos_t.shape
    cols = weights[0].shape[1]
    tile = min(256, length)
    per = length // tile
    depth = width // len(weights)
    parts = len(weights)

    def body(n_ref, cos_ref, sin_ref, *refs):
        q_ref, kv_ref = refs[parts:]
        acc = dot(n_ref[:, :depth], refs[0][...])
        for k in range(1, parts):
            acc = acc + dot(n_ref[:, k * depth : (k + 1) * depth], refs[k][...])
        t = acc.T
        cos, sin = cos_ref[0], sin_ref[0]
        for h in range(group + 1):
            a, b = t[2 * half * h : 2 * half * h + half], t[2 * half * h + half : 2 * half * (h + 1)]
            r = jnp.concatenate([a * cos - b * sin, b * cos + a * sin], 0).astype(BF16)
            if h < group:
                q_ref[0, 2 * half * h : 2 * half * (h + 1)] = r
            else:
                kv_ref[0, : 2 * half] = r
        kv_ref[0, 2 * half :] = t[2 * half * (group + 1) :].astype(BF16)

    return call(
        body,
        (seqs, per),
        [
            pl.BlockSpec((tile, width), lambda s, i: (s * per + i, 0)),
            pl.BlockSpec((1, half, tile), lambda s, i: (s, 0, i)),
            pl.BlockSpec((1, half, tile), lambda s, i: (s, 0, i)),
        ]
        + [pl.BlockSpec((depth, cols), lambda s, i: (0, 0))] * parts,
        [
            pl.BlockSpec((1, group * HEAD_DIM, tile), lambda s, i: (s, 0, i)),
            pl.BlockSpec((1, 2 * HEAD_DIM, tile), lambda s, i: (s, 0, i)),
        ],
        [
            jax.ShapeDtypeStruct((seqs, group * HEAD_DIM, length), BF16),
            jax.ShapeDtypeStruct((seqs, 2 * HEAD_DIM, length), BF16),
        ],
    )(normed, cos_t, sin_t, *weights)


def attend(s, q_t, kv_t, starts, bounds, scale, quarter):
    seqs, cols, length = q_t.shape
    total = kv_t.shape[2]
    heads = cols // HEAD_DIM
    tq, tk = min(256, length), min(256, total)

    def body(b_ref, q_ref, kv_ref, st_ref, att_ref, att_t_ref, lse_ref, kn, m, l, acc):
        i = pl.program_id(0)

        @pl.when(i == 0)
        def _():
            kn[...] = kv_ref[0, :HEAD_DIM].astype(F32).T.astype(BF16)

        qid = b_ref[0] + i * tq + lax.broadcasted_iota(jnp.int32, (1, tq), 1)
        start = st_ref[0]
        m[...] = jnp.full_like(m, MASKED)
        l[...] = jnp.zeros_like(l)
        acc[...] = jnp.zeros_like(acc)

        def step(t, _):
            k0 = pl.multiple_of(t * tk, tk)
            kid = k0 + lax.broadcasted_iota(jnp.int32, (tk, 1), 0)
            ok = (kid <= qid) & (kid >= start)
            keys = kn[pl.ds(k0, tk), :]
            vals = kv_ref[0, HEAD_DIM:, pl.ds(k0, tk)]
            for h in range(heads):
                lo = h * HEAD_DIM
                sc = dot(keys, q_ref[0, lo : lo + HEAD_DIM]) * (scale * LOG2E)
                sc = jnp.where(ok, sc, MASKED)
                old = m[h : h + 1]
                new = jnp.maximum(old, jnp.max(sc, 0, keepdims=True))
                e = jnp.exp2(sc - new)
                fade = jnp.exp2(old - new)
                m[h : h + 1] = new
                l[h : h + 1] = l[h : h + 1] * fade + jnp.sum(e, 0, keepdims=True)
                acc[lo : lo + HEAD_DIM] = acc[lo : lo + HEAD_DIM] * fade + dot(vals, e.astype(BF16))
            return 0

        lax.fori_loop(b_ref[2 + 2 * i], b_ref[3 + 2 * i], step, 0)
        for h in range(heads):
            lo = h * HEAD_DIM
            acc[lo : lo + HEAD_DIM] = acc[lo : lo + HEAD_DIM] / l[h : h + 1]
        att_t_ref[...] = acc[...].astype(BF16)
        out = acc[...].T.astype(BF16)
        for q in range(tq // quarter):
            at = ((i * (tq // quarter) + q) ^ b_ref[1]) * quarter
            att_ref[pl.ds(pl.multiple_of(at, quarter), quarter), :] = out[
                q * quarter : (q + 1) * quarter
            ]
        lse_ref[...] = m[...] + jnp.log2(l[...])

    return call(
        body,
        (length // tq,),
        [
            pl.BlockSpec((1, cols, tq), lambda i, b: (s, 0, i)),
            pl.BlockSpec((1, 2 * HEAD_DIM, total), lambda i, b: (s, 0, 0)),
            pl.BlockSpec((1, 1, tq), lambda i, b: (s, 0, i)),
        ],
        [
            pl.BlockSpec((length, cols), lambda i, b: (0, 0)),
            pl.BlockSpec((cols, tq), lambda i, b: (0, i)),
            pl.BlockSpec((heads, tq), lambda i, b: (0, i)),
        ],
        [
            jax.ShapeDtypeStruct((length, cols), BF16),
            jax.ShapeDtypeStruct((cols, length), BF16),
            jax.ShapeDtypeStruct((heads, length), F32),
        ],
        scratch=[
            pltpu.VMEM((total, HEAD_DIM), BF16),
            pltpu.VMEM((heads, tq), F32),
            pltpu.VMEM((heads, tq), F32),
            pltpu.VMEM((cols, tq), F32),
        ],
        scalars=1,
    )(bounds, q_t, kv_t, starts)


def attend_back(s, q_t, kv_t, starts, bounds, att_t, d_att_t, lse, cos_t, sin_t, scale):
    seqs, cols, length = q_t.shape
    total = kv_t.shape[2]
    heads = cols // HEAD_DIM
    half = HEAD_DIM // 2
    tq, tk = min(256, length), min(256, total)

    def body(
        b_ref, q_ref, kv_ref, st_ref, a_ref, d_ref, lse_ref, cos_ref, sin_ref,
        dq_ref, dkv_ref, kn, vn, delta, acc,
    ):
        i = pl.program_id(0)

        @pl.when(i == 0)
        def _():
            kn[...] = kv_ref[0, :HEAD_DIM].astype(F32).T.astype(BF16)
            vn[...] = kv_ref[0, HEAD_DIM:].astype(F32).T.astype(BF16)
            dkv_ref[...] = jnp.zeros_like(dkv_ref)

        qid = b_ref[0] + i * tq + lax.broadcasted_iota(jnp.int32, (1, tq), 1)
        start = st_ref[0]
        for h in range(heads):
            lo = h * HEAD_DIM
            prod = d_ref[lo : lo + HEAD_DIM].astype(F32) * a_ref[lo : lo + HEAD_DIM].astype(F32)
            delta[h : h + 1] = jnp.sum(prod, 0, keepdims=True)
        acc[...] = jnp.zeros_like(acc)

        def step(t, _):
            k0 = pl.multiple_of(t * tk, tk)
            kid = k0 + lax.broadcasted_iota(jnp.int32, (tk, 1), 0)
            ok = (kid <= qid) & (kid >= start)
            keys, vals = kn[pl.ds(k0, tk), :], vn[pl.ds(k0, tk), :]
            keys_t = kv_ref[0, :HEAD_DIM, pl.ds(k0, tk)]
            dk = jnp.zeros((HEAD_DIM, tk), F32)
            dv = jnp.zeros((HEAD_DIM, tk), F32)
            for h in range(heads):
                lo = h * HEAD_DIM
                q, d = q_ref[0, lo : lo + HEAD_DIM], d_ref[lo : lo + HEAD_DIM]
                sc = dot(keys, q) * (scale * LOG2E) - lse_ref[h : h + 1]
                p = jnp.exp2(jnp.where(ok, sc, MASKED))
                dp = dot(vals, d)
                ds = (p * (dp - delta[h : h + 1]) * scale).astype(BF16)
                dv = dv + dot(d, p.astype(BF16), 1, 1)
                dk = dk + dot(q, ds, 1, 1)
                acc[lo : lo + HEAD_DIM] += dot(keys_t, ds)
            dkv_ref[:HEAD_DIM, pl.ds(k0, tk)] += dk
            dkv_ref[HEAD_DIM:, pl.ds(k0, tk)] += dv
            return 0

        lax.fori_loop(b_ref[2 + 2 * i], b_ref[3 + 2 * i], step, 0)
        cos, sin = cos_ref[0], sin_ref[0]
        for h in range(heads):
            lo = h * HEAD_DIM
            c, e = acc[lo : lo + half], acc[lo + half : lo + HEAD_DIM]
            acc[lo : lo + HEAD_DIM] = jnp.concatenate([c * cos + e * sin, e * cos - c * sin], 0)
        dq_ref[...] = acc[...].T.astype(BF16)

    return call(
        body,
        (length // tq,),
        [
            pl.BlockSpec((1, cols, tq), lambda i, b: (s, 0, i)),
            pl.BlockSpec((1, 2 * HEAD_DIM, total), lambda i, b: (s, 0, 0)),
            pl.BlockSpec((1, 1, tq), lambda i, b: (s, 0, i)),
            pl.BlockSpec((cols, tq), lambda i, b: (0, i)),
            pl.BlockSpec((cols, tq), lambda i, b: (0, i)),
            pl.BlockSpec((heads, tq), lambda i, b: (0, i)),
            pl.BlockSpec((1, half, tq), lambda i, b: (s, 0, i)),
            pl.BlockSpec((1, half, tq), lambda i, b: (s, 0, i)),
        ],
        [
            pl.BlockSpec((tq, cols), lambda i, b: (i, 0)),
            pl.BlockSpec((2 * HEAD_DIM, total), lambda i, b: (0, 0)),
        ],
        [
            jax.ShapeDtypeStruct((length, cols), BF16),
            jax.ShapeDtypeStruct((2 * HEAD_DIM, total), F32),
        ],
        scratch=[
            pltpu.VMEM((total, HEAD_DIM), BF16),
            pltpu.VMEM((total, HEAD_DIM), BF16),
            pltpu.VMEM((heads, tq), F32),
            pltpu.VMEM((cols, tq), F32),
        ],
        scalars=1,
    )(bounds, q_t, kv_t, starts, att_t, d_att_t, lse, cos_t, sin_t)


def gate_up(normed, weight):
    rows, width = normed.shape
    ff = weight.shape[1] // 2
    tile = 128

    def body(n_ref, w_ref, act_ref, gu_ref):
        gu = dot(n_ref[...], w_ref[...])
        gate, up = gu[:, :tile], gu[:, tile:]
        sig = 1.0 / (1.0 + jnp.exp2(gate * (-LOG2E)))
        act_ref[...] = (gate * sig * up).astype(BF16)
        gu_ref[...] = gu.astype(BF16)

    return call(
        body,
        (ff // tile,),
        [
            pl.BlockSpec((rows, width), lambda j: (0, 0)),
            pl.BlockSpec((width, 2 * tile), lambda j: (0, j)),
        ],
        [
            pl.BlockSpec((rows, tile), lambda j: (0, j)),
            pl.BlockSpec((rows, 2 * tile), lambda j: (0, j)),
        ],
        [
            jax.ShapeDtypeStruct((rows, ff), BF16),
            jax.ShapeDtypeStruct((rows, 2 * ff), BF16),
        ],
    )(normed, weight)


def gate_back(dhb, w_down, gu):
    rows, width = dhb.shape
    ff = w_down.shape[0]
    tile = 256

    def body(d_ref, w_ref, gu_ref, o_ref):
        d_act = dot(d_ref[...], w_ref[...], 1, 1)
        for k in range(tile // 128):
            d = d_act[:, 128 * k : 128 * (k + 1)]
            gate = gu_ref[:, 256 * k : 256 * k + 128].astype(F32)
            up = gu_ref[:, 256 * k + 128 : 256 * (k + 1)].astype(F32)
            sig = 1.0 / (1.0 + jnp.exp2(gate * (-LOG2E)))
            o_ref[:, 256 * k : 256 * k + 128] = (
                d * up * sig * (1.0 + gate * (1.0 - sig))
            ).astype(BF16)
            o_ref[:, 256 * k + 128 : 256 * (k + 1)] = (d * gate * sig).astype(BF16)

    return call(
        body,
        (pl.cdiv(ff, tile),),
        [
            pl.BlockSpec((rows, width), lambda j: (0, 0)),
            pl.BlockSpec((tile, width), lambda j: (j, 0)),
            pl.BlockSpec((rows, 2 * tile), lambda j: (0, j)),
        ],
        pl.BlockSpec((rows, 2 * tile), lambda j: (0, j)),
        jax.ShapeDtypeStruct((rows, 2 * ff), BF16),
    )(dhb, w_down, gu)


def split_matmul(a, w, transposed, natural, place, seqs):
    rows, depth = a.shape
    cols = w.shape[0] if transposed else w.shape[1]
    tile = min(256, cols)
    length = rows // seqs
    quarter = length // 4

    def body(p, a_ref, w_ref, *refs):
        acc = refs[-1]
        acc[...] = dot(a_ref[...], w_ref[...], 1, 1 if transposed else 0)
        for s in range(seqs):
            send, keep = refs[2 * s], refs[2 * s + 1]
            for j in range(4):
                at = s * length + (j ^ p[0] if natural else j) * quarter
                part = acc[pl.ds(at, quarter), :]
                if j < 2:
                    keep[j * quarter : (j + 1) * quarter] = part
                else:
                    send[(j - 2) * quarter : (j - 1) * quarter] = part.astype(BF16)

    w_spec = (
        pl.BlockSpec((tile, depth), lambda j, p: (j, 0))
        if transposed
        else pl.BlockSpec((depth, tile), lambda j, p: (0, j))
    )
    return call(
        body,
        (cols // tile,),
        [pl.BlockSpec((rows, depth), lambda j, p: (0, 0)), w_spec],
        [pl.BlockSpec((length // 2, tile), lambda j, p: (0, j))] * (2 * seqs),
        [
            jax.ShapeDtypeStruct((length // 2, cols), BF16),
            jax.ShapeDtypeStruct((length // 2, cols), F32),
        ]
        * seqs,
        scratch=[pltpu.VMEM((rows, tile), F32)],
        scalars=1,
    )(place, a, w)


def per_device(
    sizes, hidden_in, cotangent, w_qkv, w_out, w_gate_up, w_down, norm_gains, segments
):
    n_seq, n_tp, n_rep = sizes
    seqs, length, width = hidden_in.shape
    total = segments.shape[1]
    qkv_width = w_qkv.shape[3]
    group = qkv_width // HEAD_DIM - 2
    ff = w_down.shape[1]
    rows = seqs * length
    scale = float(HEAD_DIM) ** (-0.5)
    two = n_seq == 2
    si = lax.axis_index("seq")
    ti = lax.axis_index("tp")
    zi = lax.axis_index("rep")
    core, yi = ti % 2, ti // 2
    half = width // 2
    fourth = width // 4
    quarter = length // 4
    own = core * 2 + yi
    col_swap = si if two else jnp.int32(0) * si
    pz = zi % 2
    place = jnp.stack([own, col_swap, pz]).astype(jnp.int32)
    middle = (zi == 1) | (zi == 2)
    mid_flag = jnp.reshape(middle, (1,)).astype(jnp.int32)
    order = Order()

    def swap_seq(x):
        return lax.ppermute(x, "seq", [(0, 1), (1, 0)])

    def swap_core(x):
        return lax.ppermute(x, "tp", [(0, 1), (1, 0), (2, 3), (3, 2)])

    def swap_y(x):
        return lax.ppermute(x, "tp", [(0, 2), (2, 0), (1, 3), (3, 1)])

    def swap_z(x):
        return lax.ppermute(x, "rep", [(0, 1), (1, 0), (2, 3), (3, 2)])

    def hop_in(x):
        return lax.ppermute(x, "rep", [(0, 1), (3, 2)])

    def hop_mid(x):
        return lax.ppermute(x, "rep", [(1, 2), (2, 1)])

    def hop_out(x):
        return lax.ppermute(x, "rep", [(1, 0), (2, 3)])

    def whole(shard, axis):
        return lax.all_gather(shard, "seq", axis=axis, tiled=True)

    def local_cols(x):
        if not two:
            return x
        return jnp.where(si == 0, x, jnp.concatenate([x[..., half:], x[..., :half]], -1))

    def own_rows(x, s):
        x = lax.dynamic_slice_in_dim(x, s * length + own * quarter, quarter, 0)
        return local_cols(x)

    def join(own_part, x, z, axis):
        first, second = jnp.where(pz == 0, x, z), jnp.where(pz == 0, z, x)
        return jnp.concatenate([own_part, first, second], axis)

    wq, wo, wd, wg = w_qkv[0, :, 0, :], w_out[0], w_down[0], w_gate_up[0]
    if two:
        gains = jnp.concatenate([norm_gains[0], swap_seq(norm_gains[0])], 1).astype(F32)
        qkv_x = swap_seq(lax.dynamic_slice_in_dim(wq, pz * fourth, fourth, 0))
        out_x = swap_seq(lax.dynamic_slice_in_dim(wo, pz * fourth, fourth, 1))
        n_piece = 4
        got = order(lambda w, p: spread_gate_up(w, p, width, 0, n_piece, []), wg, place)
        gu_w, gu_send = got[0], got[1:]
        gu_x = [swap_seq(gu_send[0])]
    else:
        gains = whole(norm_gains[0], 1).astype(F32)
        qkv_w, out_w, down_w = whole(wq, 0), whole(wo, 1), whole(wd, 1)
        gu_w = spread_gate_up(whole(wg, 0), place, width, None, 0, [])[0]

    first_row = si * length
    ids = jnp.arange(total, dtype=jnp.int32)
    change = jnp.concatenate(
        [jnp.ones((seqs, 1), bool), segments[:, 1:] != segments[:, :-1]], axis=1
    )
    doc_start = lax.cummax(jnp.where(change, ids[None, :], 0), axis=1)
    starts = lax.dynamic_slice_in_dim(doc_start, first_row, length, 1)
    pos = first_row + jnp.arange(length, dtype=jnp.int32)[None, :] - starts
    inverse_freq = ROPE_THETA ** (-(jnp.arange(HEAD_DIM // 2, dtype=F32) / (HEAD_DIM // 2)))
    angles = inverse_freq[None, :, None] * pos.astype(F32)[:, None, :]
    cos_t, sin_t = jnp.cos(angles), jnp.sin(angles)
    starts3 = starts[:, None, :]
    tq, tk = min(256, length), min(256, total)
    tiles = jnp.arange(length // tq, dtype=jnp.int32)
    ends = (first_row + (tiles + 1) * tq + tk - 1) // tk
    bounds = [
        jnp.concatenate(
            [
                jnp.stack([first_row, own]),
                jnp.stack([starts[s, ::tq] // tk, ends], axis=1).reshape(-1),
            ]
        ).astype(jnp.int32)
        for s in range(seqs)
    ]

    hidden = hidden_in.reshape(rows, width)
    d_hidden = cotangent.reshape(rows, width)
    normed1 = order(lambda h, g, p: first_norm(h, g, p, 2 * quarter), hidden, gains[:1], place)
    if two:
        qkv_z, out_z = swap_z(qkv_x), swap_z(out_x)
        gu_w = order(lambda w, p, b: spread_gate_up(w, p, width, 1, 0, [b]), wg, place, gu_w)[0]
        qkv_w = order(lambda a, x, z: join(a, x, z, 0), wq, qkv_x, qkv_z)
    q_t, kv_t = order(
        lambda n, w, c, s: project_qkv(n, w, c, s, group), normed1, [qkv_w], cos_t, sin_t
    )
    if two:
        got = lax.ppermute(kv_t, "seq", [(0, 1)])
        *gu_send, wd_late, kv_t = lax.optimization_barrier((*gu_send, wd, kv_t))
        gu_x += [swap_seq(x) for x in gu_send[1:]]
        ff_half = ff // 2
        down_send = lax.dynamic_slice_in_dim(wd_late, pz * fourth, fourth, 1)
        down_x = [swap_seq(down_send[k * ff_half : (k + 1) * ff_half]) for k in range(2)]
        dhb = order(lambda d, p: local_cast(d, p, quarter), d_hidden, place)
        all_kv = order(
            lambda a, g: jnp.concatenate(
                [jnp.where(si == 0, a, g), jnp.where(si == 0, g, a)], axis=2
            ),
            kv_t,
            got,
        )
        gu_z = [swap_z(x) for x in gu_x]
        down_z = [swap_z(x) for x in down_x]
    else:
        dhb = local_cast(d_hidden, place, quarter)
        all_kv = whole(kv_t, 2)

    piece = 128

    def put_gu(w, x, k, parity):
        return lax.dynamic_update_slice(w, x, (half + parity * fourth + k * piece, 0))

    def put_down(w, x, k, parity):
        return lax.dynamic_update_slice(w, x, (k * (ff // 2), half + parity * fourth))

    att, att_t, lse = [None] * seqs, [None] * seqs, [None] * seqs
    hold, keep = [None] * seqs, [None] * seqs

    def first_sum(k, g):
        x = k + g.astype(F32)
        return x[quarter:].astype(BF16), x[:quarter]

    def attention(s):
        att[s], att_t[s], lse[s] = order(
            lambda q, kv, st, b, s=s: attend(s, q, kv, st, b, scale, quarter),
            q_t, all_kv, starts3, bounds[s],
        )

    def out_product(s):
        send, keep[s] = order(
            lambda a, w, p: split_matmul(a, w, False, False, p, 1), att[s], out_w, place
        )
        hold[s] = swap_core(send)

    def summed(s):
        send, keep[s] = order(first_sum, keep[s], hold[s])
        hold[s] = swap_y(send)

    attention(0)
    if two:
        out_w = order(lambda a, x, z: join(a, x, z, 1), wo, out_x, out_z)
    out_product(0)
    for s in range(1, seqs):
        attention(s)
        summed(s - 1)
        out_product(s)
    if two:
        gu_w = order(lambda w, x: put_gu(w, x, 0, pz), gu_w, gu_x[0])
        gu_w = order(lambda w, x: put_gu(w, x, 1, pz), gu_w, gu_x[1])
    summed(seqs - 1)
    if two:
        gu_w = order(lambda w, x: put_gu(w, x, 0, 1 - pz), gu_w, gu_z[0])
    h2, i2, n2 = [None] * seqs, [None] * seqs, [None] * seqs

    def second_norm(h, k, g, gain):
        x = h + k + g.astype(F32)
        inv = lax.rsqrt(jnp.mean(x * x, axis=-1, keepdims=True) + NORM_EPS)
        return x, inv, (x * inv * gain).astype(BF16)

    def share(x):
        far = swap_y(x)
        return [x, far, swap_core(x), swap_core(far)]

    for s in range(seqs):
        h2[s], i2[s], mine = order(
            lambda h, k, g, gain, s=s: second_norm(own_rows(h, s), k, g, gain),
            hidden, keep[s], hold[s], gains[1],
        )
        n2[s] = share(mine)
    if two:
        down_w = order(lambda w: jnp.concatenate([w, w], 1), wd)
        gu_w = order(lambda w, x: put_gu(w, x, 2, pz), gu_w, gu_x[2])
        gu_w = order(lambda w, x: put_gu(w, x, 1, 1 - pz), gu_w, gu_z[1])
    n2_all = order(lambda a: jnp.concatenate([x for b in a for x in b]), n2)
    if two:
        gu_w = order(lambda w, x: put_gu(w, x, 3, pz), gu_w, gu_x[3])
        gu_w = order(lambda w, x: put_gu(w, x, 2, 1 - pz), gu_w, gu_z[2])
        gu_w = order(lambda w, x: put_gu(w, x, 3, 1 - pz), gu_w, gu_z[3])
    act, gu = order(gate_up, n2_all, gu_w)

    def piece_of(x, k, at, size):
        return x[:, k * half + at : k * half + at + size]

    class Chunk:
        def __init__(self, make, finish=None, dtype=BF16):
            self.make, self.finish, self.dtype, self.stage = make, finish, dtype, 0

        def begin(self, *xs):
            self.xs = xs
            self.got = swap_seq(order(lambda *x: self.make(1, *x).astype(self.dtype), *xs))

        def next(self):
            k = self.stage
            self.stage += 1
            if k == 0:
                self.sum = order(
                    lambda g, *x: (self.make(0, *x) + g.astype(F32)).astype(self.dtype),
                    self.got, *self.xs,
                )
                self.got = hop_in(self.sum)
            elif k < 3:
                self.sum = order(
                    lambda a, b: (a.astype(F32) + b.astype(F32)).astype(self.dtype),
                    self.sum, self.got,
                )
                self.got = hop_mid(self.sum) if k == 1 else hop_out(self.sum)
            elif self.finish is not None:
                self.finish(self.sum, self.got)
            else:
                self.out = order(
                    lambda a, b: jnp.where(middle, a, b).astype(F32), self.sum, self.got
                )

    chunks = {}

    def begin(name, make, *xs, finish=None, dtype=BF16):
        if two:
            chunks[name] = Chunk(make, finish, dtype)
            chunks[name].begin(*xs)

    def go(*names):
        for name in names:
            if two:
                chunks[name].next()

    fr = ff // 2
    gu_rows = [256, 256, 256, 128, 128]
    gu_grad = []

    def begin_down(j):
        begin(
            f"d{j}",
            lambda k, a, d: dot(a[:, j * fr : (j + 1) * fr], piece_of(d, k, 0, half), 0, 0),
            act, dhb,
        )

    def begin_gu(j):
        at = sum(gu_rows[:j])

        def finish(a, b):
            gu_grad[:] = [
                order(
                    lambda a, b, m, g: join_gate_up(a, b, m, at, half, g), a, b, mid_flag, gu_grad
                )
            ]

        begin(
            f"g{j}",
            lambda k, n, d: dot(piece_of(n, k, at, gu_rows[j]), d, 0, 0),
            n2_all, dgu, finish=finish,
        )

    begin_down(0)
    begin_down(1)
    if two:
        down_w = order(lambda w, x: put_down(w, x, 0, pz), down_w, down_x[0])
        down_w = order(lambda w, x: put_down(w, x, 1, pz), down_w, down_x[1])
        down_w = order(lambda w, x: put_down(w, x, 0, 1 - pz), down_w, down_z[0])
        down_w = order(lambda w, x: put_down(w, x, 1, 1 - pz), down_w, down_z[1])
    dgu = order(gate_back, dhb, down_w, gu)

    def product(a, w, transposed, natural):
        got = order(lambda a, w, p: split_matmul(a, w, transposed, natural, p, seqs), a, w, place)
        return list(got[1::2]), [swap_core(x) for x in got[::2]]

    keep, hold = product(dgu, gu_w, True, False)
    go("d0")
    for s in range(seqs):
        summed(s)
    begin_gu(0)
    begin_gu(1)
    gain2 = []
    d_h2, d2 = [None] * seqs, [None] * seqs

    def second_back(k, g, x, inv, d, gain):
        mine = k + g.astype(F32)
        w = gain * mine
        back = inv * w - x * (inv * inv * inv) * jnp.mean(w * x, axis=-1, keepdims=True)
        back = back + d
        return back, back.astype(BF16), jnp.sum(mine * x * inv, axis=0)

    for s in range(seqs):
        d_h2[s], mine, g2 = order(
            lambda k, g, x, inv, d, gain, s=s: second_back(k, g, x, inv, own_rows(d, s), gain),
            keep[s], hold[s], h2[s], i2[s], d_hidden, gains[1],
        )
        gain2.append(g2)
        d2[s] = share(mine)
    go("d1", "d0")
    dq, dkv = [None] * seqs, [None] * seqs

    def out_back(w, d):
        x = dot(w, d, 1, 1).astype(BF16).reshape(-1, 2, 2, quarter)
        x = jnp.where(core == 0, x, x[:, ::-1])
        x = jnp.where(yi == 0, x, x[:, :, ::-1])
        return x.reshape(-1, length)

    for s in range(seqs):
        d2[s] = order(lambda a: jnp.concatenate(a), d2[s])
        d_att_t = order(out_back, out_w, d2[s])
        dq[s], dkv[s] = order(
            lambda *x, s=s: attend_back(s, *x, scale),
            q_t, all_kv, starts3, bounds[s], att_t[s], d_att_t, lse[s], cos_t, sin_t,
        )
    dkv_all = order(lambda a: jnp.stack(a), dkv)
    if two:
        dkv_got = lax.ppermute(dkv_all[:, :, :length].astype(BF16), "seq", [(1, 0)])
    begin(
        "out",
        lambda k, a, d: sum(dot(x, piece_of(y, k, 0, half), 0, 0) for x, y in zip(a, d)),
        att, d2,
    )
    go("g0", "d1", "d0")
    keep, hold = product(act, down_w, False, False)
    if two:
        dkv_mine = lax.dynamic_slice_in_dim(dkv_all, first_row, length, 2) + dkv_got.astype(F32)
    else:
        dkv_mine = lax.psum_scatter(dkv_all, "seq", scatter_dimension=2, tiled=True)

    def make_dqkv(q, kv, c, si_):
        lo, hi = kv[:, : HEAD_DIM // 2], kv[:, HEAD_DIM // 2 : HEAD_DIM]
        k = jnp.concatenate([lo * c + hi * si_, hi * c - lo * si_, kv[:, HEAD_DIM:]], 1)
        k = jnp.swapaxes(k.astype(BF16), 1, 2)
        return jnp.concatenate([jnp.stack(q), k], -1).reshape(rows, qkv_width)

    d_qkv = order(make_dqkv, dq, dkv_mine, cos_t, sin_t)
    keep1, hold1 = product(d_qkv, qkv_w, True, True)
    begin("qkv", lambda k, n, d: dot(piece_of(n, k, 0, half), d, 0, 0), normed1, d_qkv)
    begin_gu(2)
    begin_gu(3)
    begin_gu(4)

    def summed_list(keep, hold):
        for s in range(seqs):
            send, keep[s] = order(first_sum, keep[s], hold[s])
            hold[s] = swap_y(send)

    summed_list(keep1, hold1)
    go("g1", "g0", "d1", "d0")
    gain1 = []
    d1 = [None] * seqs

    def first_back(k, g, x, gain, d2, d):
        mine = k + g.astype(F32)
        inv = lax.rsqrt(jnp.mean(x * x, axis=-1, keepdims=True) + NORM_EPS)
        w = gain * mine
        back = inv * w - x * (inv * inv * inv) * jnp.mean(w * x, axis=-1, keepdims=True)
        return (back + (d2 - d)).astype(BF16), jnp.sum(mine * x * inv, axis=0)

    for s in range(seqs):
        mine, g1 = order(
            lambda k, g, h, gain, d2, d, s=s: first_back(
                k, g, own_rows(h, s), gain, d2, own_rows(d, s)
            ),
            keep1[s], hold1[s], hidden, gains[0], d_h2[s], d_hidden,
        )
        gain1.append(g1)
        d1[s] = share(mine)
    gain_sum = order(lambda a, b: jnp.stack([sum(a), sum(b)]), gain1, gain2)
    add = lambda a, b: a + b
    gain_sum = order(add, gain_sum, swap_core(gain_sum))
    gain_sum = order(add, gain_sum, swap_y(gain_sum))
    begin("gain", lambda k, g: piece_of(g, k, 0, half), gain_sum, dtype=F32)
    summed_list(keep, hold)
    go("out", "g1", "g0", "d1")
    grad_in = order(
        lambda d, x, p: add_local(d, x, p, quarter), d_hidden, [x for b in d1 for x in b], place
    )
    hb = [None] * seqs
    for s in range(seqs):
        mine = order(
            lambda k, g, x, h, s=s: (x + k + g.astype(F32) - own_rows(h, s)).astype(BF16),
            keep[s], hold[s], h2[s], hidden,
        )
        hb[s] = share(mine)
    go("qkv", "out", "g1", "g0")
    go("g2", "qkv", "out", "g1")
    hidden_out = order(
        lambda d, x, p: add_local(d, x, p, quarter), hidden, [x for b in hb for x in b], place
    )
    go("g3", "gain", "g2", "qkv", "out")
    go("g4", "g3", "gain", "g2", "qkv")
    go("g4", "g3", "gain", "g2")
    go("g4", "g3", "gain")
    go("g4")
    if two:
        g_qkv, g_out = chunks["qkv"].out, chunks["out"].out
        g_down = jnp.concatenate([chunks["d0"].out, chunks["d1"].out])
        g_gu, gain_own = gu_grad[0], chunks["gain"].out
    else:

        def reduce_rep(x):
            if n_rep != 4:
                return lax.psum(x.astype(F32), "rep").astype(BF16)
            x = x.astype(BF16)
            x = (x.astype(F32) + hop_in(x).astype(F32)).astype(BF16)
            x = (x.astype(F32) + hop_mid(x).astype(F32)).astype(BF16)
            return jnp.where(middle, x, hop_out(x))

        def reduce(x, axis):
            return reduce_rep(lax.psum_scatter(x, "seq", scatter_dimension=axis, tiled=True))

        g_down = reduce(dot(act, dhb, 0, 0), 1).astype(F32)
        g_out = reduce(sum(dot(x, y, 0, 0) for x, y in zip(att, d2)), 1).astype(F32)
        g_qkv = reduce(dot(normed1, d_qkv, 0, 0), 0).astype(F32)
        g_gu = reduce(dot(n2_all, dgu, 0, 0), 0)
        g_gu = join_gate_up(g_gu, g_gu, mid_flag, 0, g_gu.shape[0], [])
        gain_own = lax.psum_scatter(gain_sum, "seq", scatter_dimension=1, tiled=True)
        gain_own = lax.psum(gain_own, "rep")
    return (
        hidden_out.reshape(seqs, length, width),
        grad_in.reshape(seqs, length, width),
        g_qkv[None, :, None, :],
        g_out[None],
        g_gu,
        g_down[None],
        gain_own[None],
    )


def solution(mesh):
    in_specs = (
        P("rep", "seq", None),
        P("rep", "seq", None),
        P(None, "seq", "tp", None),
        P(None, "tp", "seq"),
        P(None, "seq", None, "tp"),
        P(None, "tp", "seq"),
        P(None, None, "seq"),
        P("rep", None),
    )
    out_specs = (
        P("rep", "seq", None),
        P("rep", "seq", None),
        P(None, "seq", "tp", None),
        P(None, "tp", "seq"),
        P(None, "seq", None, "tp"),
        P(None, "tp", "seq"),
        P(None, None, "seq"),
    )
    sizes = (mesh.shape["seq"], mesh.shape["tp"], mesh.shape["rep"])
    return jax.shard_map(
        functools.partial(per_device, sizes),
        mesh=mesh,
        in_specs=in_specs,
        out_specs=out_specs,
        check_vma=False,
    )
```

time: 2420 us -> 803 us (0.33)
  waiting for transfers between devices: 1950 us -> 237 us
  Pallas kernels: 0 us -> 183 us
  matrix products: 221 us -> 66.6 us
  starting transfers between devices: 1.15 us -> 135 us
  blocking collectives: 31.9 us -> 0 us
  other arithmetic: 101 us -> 76.3 us
    psum x4 -> x0, waiting for transfers between devices: 1280 us -> none  [the longest x1 723 us: per_device(): lax.psum((lax.psum_scatter(layer_grads[0], 'seq', scatter_dimension=0, ti...]
    reduce_scatter x5 -> x0, waiting for transfers between devices: 465 us -> none  [the longest x1 259 us: per_device(): lax.psum_scatter(layer_grads[2], 'seq', scatter_dimension=0, tiled=True)]
    ppermute x0 -> x101, waiting for transfers between devices: none -> 237 us  [the longest x10 102 us: hop_out(): return lax.ppermute(x, 'rep', [(1, 0), (2, 3)])]
    all_gather x4 -> x0, waiting for transfers between devices: 198 us -> none  [the longest x1 130 us: per_device(): lax.all_gather(w_gate_up[layer_no], 'seq', axis=0, tiled=True)]
    pallas_call x0 -> x23, Pallas kernels: none -> 183 us  [the longest x5 49.5 us: split_matmul(): call(body, (cols // tile,), [pl.BlockSpec((rows, depth), lambda j, p: (0,...]
    dot_general x24 -> x22, matrix products: 221 us -> 66.6 us  [dot(): lax.dot_general(a, b, (((ca,), (cb,)), ((), ())), preferred_element_type=...]
    ppermute x0 -> x101, starting transfers between devices: none -> 135 us  [the longest x10 44.5 us: hop_in(): return lax.ppermute(x, 'rep', [(0, 1), (3, 2)])]
    reduce_sum x7 -> x8, other arithmetic: 48.3 us -> 5.21 us  [the longest x2 3.35 us: second_norm(): inv = lax.rsqrt(jnp.mean(x * x, axis=-1, keepdims=True) + NORM_EPS)]
  transfers between devices with their start and end apart: 14 -> 101, of which waited for: 12 -> 29; matrix products, arithmetic and copies ran while one was open for 10% -> 26% of each run, Pallas kernels for 0% -> 22%
where the time goes in v1:
time: 803 us; the launch traced here: 793 us
  waiting for transfers between devices  237 us (30%)
  Pallas kernels  183 us (23%)
  starting transfers between devices  135 us (17%)
  local copies, waits for them, and re-layouts  90.9 us (11%)
  other arithmetic  76.3 us (10%)
  matrix products  66.6 us (8%)
    ppermute x10, waiting for transfers between devices, hop_out(): return lax.ppermute(x, 'rep', [(1, 0), (2, 3)])  102 us
    dot_general x22, matrix products, dot(): lax.dot_general(a, b, (((ca,), (cb,)), ((), ())), preferred_element_type=...  66.6 us
    ppermute x17, waiting for transfers between devices, swap_y(): return lax.ppermute(x, 'tp', [(0, 2), (2, 0), (1, 3), (3, 1)])  55.1 us
    pallas_call x5, Pallas kernels, split_matmul(): call(body, (cols // tile,), [pl.BlockSpec((rows, depth), lambda j, p: (0,...  49.5 us
    ppermute x10, starting transfers between devices, hop_in(): return lax.ppermute(x, 'rep', [(0, 1), (3, 2)])  44.5 us
    unnamed x199, local copies, waits for them, and re-layouts  43.8 us
    ppermute x19, waiting for transfers between devices, swap_seq(): return lax.ppermute(x, 'seq', [(0, 1), (1, 0)])  43.7 us
    ppermute x19, starting transfers between devices, swap_seq(): return lax.ppermute(x, 'seq', [(0, 1), (1, 0)])  32.2 us
  transfers between devices with their start and end apart: 101, of which 29 were waited for; matrix products, arithmetic and copies ran while one was open for 26% of the time, Pallas kernels for 22%

profile of v1, /device:TPU:0, one launch (start us, length us, event | category | flops | bytes accessed | tf_op | source)
XLA Modules:
  0.0 792.6 jit_solution(16935206218431644920)
XLA Ops:
  11.6 10.9 %shard_map.135 = (bf16[2048,2816]{1,0:T(8,128)(2,1)}, bf16[128,2816]{1,0:T(8,128)(2,1)}, bf16[128,2816]{1,0:T(8,128)(2,1)S(1)}, bf16[128,2816]{1,0:T(8,128)(2,1)S(1)}, bf16[128,2816]{1,0:T(8,128)(2,1)S(1)}) custom-call(s32[3]{0:T(128)S(1)} %pad_add_fusion.2.p, bf16[1024,2,1408]{2,1,0:T(2,128)(2,1)} %bitcast.93), custom_call_target="tpu_custom_call" | custom-call | flops 1 | bytes 1 | tf_op jit(solution)/shard_map/pallas_call | solution.py:158
  25.2 5.4 shard_map.136.n_ref
  30.7 9.3 %shard_map.137 = bf16[2048,2816]{1,0:T(8,128)(2,1)} custom-call(s32[3]{0:T(128)S(1)} %pad_add_fusion.2.p, bf16[1024,2,1408]{2,1,0:T(2,128)(2,1)S(1)} %bitcast.96, bf16[2048,2816]{1,0:T(8,128)(2,1)} %get-tuple-element.380.refs_0_), custom_call_target="tpu_custom_call", output_to_operand_aliasing={{}: (2, {})} | custom-call | flops 1 | bytes 1 | tf_op jit(solution)/shard_map/pallas_call | solution.py:158
  41.8 6.6 shard_map.138
  52.9 6.2 shard_map.139.d_ref
  62.4 7.8 shard_map.140
  72.0 4.9 shard_map.141
  83.3 7.8 shard_map.142
  95.9 4.9 shard_map.143
  110.2 4.6 collective-permute-done.9
  123.5 8.1 %collective-permute-done.7 = bf16[128,2048]{1,0:T(8,128)(2,1)S(1)} collective-permute-done((bf16[128,2048]{1,0:T(8,128)(2,1)S(1)}, bf16[128,2048]{1,0:T(8,128)(2,1)S(1)}, u32[]{:S(2)}, u32[]{:S(2)}) %collective-permute-start.7) | collective-permute-done | bytes 524320 | tf_op jit(solution)/shard_map/ppermute | solution.py:553
  136.3 7.4 collective-permute-done.15
  151.4 9.7 %collective-permute-done.24 = bf16[704,512]{1,0:T(8,128)(2,1)} collective-permute-done((bf16[704,512]{1,0:T(8,128)(2,1)S(1)}, bf16[704,512]{1,0:T(8,128)(2,1)}, u32[]{:S(2)}, u32[]{:S(2)}) %collective-permute-start.24) | collective-permute-done | bytes 720928 | tf_op jit(solution)/shard_map/ppermute | solution.py:547
  161.7 4.4 collective-permute-done.16
  167.9 8.5 %collective-permute-done.25 = bf16[704,512]{1,0:T(8,128)(2,1)} collective-permute-done((bf16[704,512]{1,0:T(8,128)(2,1)S(1)}, bf16[704,512]{1,0:T(8,128)(2,1)}, u32[]{:S(2)}, u32[]{:S(2)}) %collective-permute-start.25) | collective-permute-done | bytes 720928 | tf_op jit(solution)/shard_map/ppermute | solution.py:547
  188.1 7.3 collective-permute-done.22
  196.3 14.5 %collective-permute-done.23 = bf16[128,2816]{1,0:T(8,128)(2,1)S(1)} collective-permute-done((bf16[128,2816]{1,0:T(8,128)(2,1)S(1)}, bf16[128,2816]{1,0:T(8,128)(2,1)S(1)}, u32[]{:S(2)}, u32[]{:S(2)}) %collective-permute-start.23) | collective-permute-done | bytes 720928 | tf_op jit(solution)/shard_map/ppermute | solution.py:556
  211.7 18.6 %shard_map.144 = (bf16[1024,1408]{1,0:T(8,128)(2,1)S(1)}, bf16[1024,2816]{1,0:T(8,128)(2,1)}) custom-call(bf16[1024,2048]{1,0:T(8,128)(2,1)} %constant_dynamic-update-slice_fusion.2.n_ref, bf16[2048,2816]{1,0:T(8,128)(2,1)} %constant_dynamic-update-slice_fusion.20.w_ref), custom_call_target="tpu_custom_call" | custom-call | flops 1 | bytes 1 | tf_op jit(solution)/shard_map/pallas_call | solution.py:431
  245.5 12.6 %shard_map.145.a_ref = bf16[1024,2816]{1,0:T(8,128)(2,1)} custom-call(bf16[1024,2048]{1,0:T(8,128)(2,1)S(1)} %copy-done.6, bf16[1408,2048]{1,0:T(8,128)(2,1)} %copy-done.45, bf16[1024,2816]{1,0:T(8,128)(2,1)} %get-tuple-element.481.gu_ref), custom_call_target="tpu_custom_call" | custom-call | flops 1 | bytes 1 | tf_op jit(solution)/shard_map/pallas_call | solution.py:466
  258.0 18.1 %shard_map.146 = (bf16[256,2048]{1,0:T(8,128)(2,1)}, f32[256,2048]{1,0:T(8,128)S(1)}, bf16[256,2048]{1,0:T(8,128)(2,1)S(1)}, f32[256,2048]{1,0:T(8,128)}) custom-call(s32[3]{0:T(128)S(1)} %pad_add_fusion.2.p, bf16[1024,2816]{1,0:T(8,128)(2,1)} %shard_map.145.a_ref, bf16[2048,2816]{1,0:T(8,128)(2,1)} %constant_dynamic-update-slice_fusion.20.w_ref), custom_call_target="tpu_custom_call" | custom-call | flops 1 | bytes 1 | tf_op jit(solution)/shard_map/pallas_call | solution.py:504
  296.2 4.3 convolution_convert_fusion.1
  304.4 7.7 collective-permute-done.33
  315.8 7.5 collective-permute-done.38
  329.7 4.3 collective-permute-done.41
  344.5 5.7 rev.13
  358.1 7.8 shard_map.147
  382.9 7.8 shard_map.148
  395.0 6.0 fusion
  401.1 4.4 collective-permute-start.50
  414.4 12.2 %shard_map.149 = (bf16[256,2048]{1,0:T(8,128)(2,1)S(1)}, f32[256,2048]{1,0:T(8,128)S(1)}, bf16[256,2048]{1,0:T(8,128)(2,1)S(1)}, f32[256,2048]{1,0:T(8,128)}) custom-call(s32[3]{0:T(128)S(1)} %pad_add_fusion.2.p, bf16[1024,1408]{1,0:T(8,128)(2,1)} %copy-done.16, bf16[1408,2048]{1,0:T(8,128)(2,1)} %copy-done.45), custom_call_target="tpu_custom_call" | custom-call | flops 1 | bytes 1 | tf_op jit(solution)/shard_map/pallas_call | solution.py:504
  431.0 9.5 %shard_map.150 = (bf16[256,2048]{1,0:T(8,128)(2,1)S(1)}, f32[256,2048]{1,0:T(8,128)S(1)}, bf16[256,2048]{1,0:T(8,128)(2,1)S(1)}, f32[256,2048]{1,0:T(8,128)}) custom-call(s32[3]{0:T(128)S(1)} %pad_add_fusion.2.p, bf16[1024,640]{1,0:T(8,128)(2,1)S(1)} %bitcast.97, bf16[2048,640]{1,0:T(8,128)(2,1)} %copy-done), custom_call_target="tpu_custom_call" | custom-call | flops 1 | bytes 1 | tf_op jit(solution)/shard_map/pallas_call | solution.py:504
  444.0 5.7 convolution_convert_fusion
  470.2 23.4 %collective-permute-done.48 = bf16[704,1024]{1,0:T(8,128)(2,1)S(1)} collective-permute-done((bf16[704,1024]{1,0:T(8,128)(2,1)S(1)}, bf16[704,1024]{1,0:T(8,128)(2,1)S(1)}, u32[]{:S(2)}, u32[]{:S(2)}) %collective-permute-start.48) | collective-permute-done | bytes 1441824 | tf_op jit(solution)/shard_map/ppermute | solution.py:565
  502.6 7.2 collective-permute-start.66
  519.2 13.8 %collective-permute-done.66 = bf16[512,1024]{1,0:T(8,128)(2,1)S(1)} collective-permute-done((bf16[512,1024]{1,0:T(8,128)(2,1)S(1)}, bf16[512,1024]{1,0:T(8,128)(2,1)S(1)}, u32[]{:S(2)}, u32[]{:S(2)}) %collective-permute-start.66) | collective-permute-done | bytes 1048608 | tf_op jit(solution)/shard_map/ppermute | solution.py:547
  536.1 5.8 collective-permute-done.65
  544.4 12.3 %collective-permute-done.57.refs_1_ = bf16[128,2048]{1,0:T(8,128)(2,1)S(1)} collective-permute-done((bf16[128,2048]{1,0:T(8,128)(2,1)S(1)}, bf16[128,2048]{1,0:T(8,128)(2,1)S(1)}, u32[]{:S(2)}, u32[]{:S(2)}) %collective-permute-start.57) | collective-permute-done | bytes 524320 | tf_op jit(solution)/shard_map/ppermute | solution.py:553
  561.8 5.5 collective-permute-start.76
  567.4 9.7 %shard_map.151 = f32[1024,2048]{1,0:T(8,128)} custom-call(s32[3]{0:T(128)S(1)} %pad_add_fusion.2.p, f32[1024,2048]{1,0:T(8,128)} %bitcast.135, bf16[128,2048]{1,0:T(8,128)(2,1)S(1)} %fusion.48.refs_0_, bf16[128,2048]{1,0:T(8,128)(2,1)S(1)} %collective-permute-done.57.refs_1_, bf16[128,2048]{1,0:T(8,128)(2,1)S(1)} %collective-permute-done.58.refs_2_, ...), custom_call_target="tpu_custom_call" | custom-call | flops 1 | bytes 1 | tf_op jit(solution)/shard_map/pallas_call | solution.py:124
  600.1 15.8 %collective-permute-start.81 = (bf16[1024,640]{1,0:T(8,128)(2,1)}, bf16[1024,640]{1,0:T(8,128)(2,1)}, u32[]{:S(2)}, u32[]{:S(2)}) collective-permute-start(bf16[1024,640]{1,0:T(8,128)(2,1)} %add_convert_fusion.14), channel_id=1, source_target_pairs={{0,8},{24,16},{1,9},{25,17},{2,10},{26,18},{3,11},{27,19},{4,12},{... | collective-permute-start | bytes 3932168 | tf_op jit(solution)/shard_map/ppermute | solution.py:559
  629.8 4.9 fusion.2
  637.3 7.0 collective-permute-done.81
  659.1 10.0 %shard_map.154 = f32[1024,2048]{1,0:T(8,128)} custom-call(s32[3]{0:T(128)S(1)} %pad_add_fusion.2.p, f32[1024,2048]{1,0:T(8,128)} %bitcast.126, bf16[128,2048]{1,0:T(8,128)(2,1)S(1)} %copy-done.28, bf16[128,2048]{1,0:T(8,128)(2,1)S(1)} %collective-permute-done.68.refs_1_, bf16[128,2048]{1,0:T(8,128)(2,1)S(1)} %collective-permute-done.69.refs_2_, ...), custom_call_target="tpu_custom_call" | custom-call | flops 1 | bytes 1 | tf_op jit(solution)/shard_map/pallas_call | solution.py:124
  683.2 12.9 %collective-permute-done.92 = bf16[512,1024]{1,0:T(8,128)(2,1)S(1)} collective-permute-done((bf16[512,1024]{1,0:T(8,128)(2,1)S(1)}, bf16[512,1024]{1,0:T(8,128)(2,1)S(1)}, u32[]{:S(2)}, u32[]{:S(2)}) %collective-permute-start.92) | collective-permute-done | bytes 1048608 | tf_op jit(solution)/shard_map/ppermute | solution.py:565
  700.7 4.7 collective-permute-start.93
  708.6 20.1 %collective-permute-done.87 = bf16[1024,640]{1,0:T(8,128)(2,1)S(1)} collective-permute-done((bf16[1024,640]{1,0:T(8,128)(2,1)S(1)}, bf16[1024,640]{1,0:T(8,128)(2,1)S(1)}, u32[]{:S(2)}, u32[]{:S(2)}) %collective-permute-start.87) | collective-permute-done | bytes 1310752 | tf_op jit(solution)/shard_map/ppermute | solution.py:565
  731.6 30.6 %collective-permute-done.95.b_ref = bf16[256,2816]{1,0:T(8,128)(2,1)S(1)} collective-permute-done((bf16[256,2816]{1,0:T(8,128)(2,1)S(1)}, bf16[256,2816]{1,0:T(8,128)(2,1)S(1)}, u32[]{:S(2)}, u32[]{:S(2)}) %collective-permute-start.95) | collective-permute-done | bytes 1441824 | tf_op jit(solution)/shard_map/ppermute | solution.py:565
  779.5 10.2 %collective-permute-done.100 = f32[2,1024]{1,0:T(2,128)S(1)} collective-permute-done((f32[2,1024]{1,0:T(2,128)S(1)}, f32[2,1024]{1,0:T(2,128)S(1)}, u32[]{:S(2)}, u32[]{:S(2)}) %collective-permute-start.100) | collective-permute-done | bytes 8224 | tf_op jit(solution)/shard_map/ppermute | solution.py:565
  (570 shorter events, 334.9 us)
Async XLA Ops:
  7.5 44.5 %collective-permute-start.4 = (bf16[512,512]{1,0:T(8,128)(2,1)}, bf16[512,512]{1,0:T(8,128)(2,1)}, u32[]{:S(2)}, u32[]{:S(2)}) collective-permute-start(bf16[512,512]{1,0:T(8,128)(2,1)} %dynamic-slice_bitcast_fusion.1), channel_id=1, source_target_pairs={{0,4},{4,0},{1,5},{5,1},{2,6},{6,2},{3,7},{7,3},{8,12},{12,8},{9,1... | collective-permute-start | bytes 1572872 | tf_op jit(solution)/shard_map/ppermute | solution.py:547
  82.3 32.5 %collective-permute-start.9 = (bf16[128,2816]{1,0:T(8,128)(2,1)}, bf16[128,2816]{1,0:T(8,128)(2,1)}, u32[]{:S(2)}, u32[]{:S(2)}) collective-permute-start(bf16[128,2816]{1,0:T(8,128)(2,1)} %copy-done.44), channel_id=1, source_target_pairs={{0,4},{4,0},{1,5},{5,1},{2,6},{6,2},{3,7},{7,3},{8,12},{12,8},{9,1... | collective-permute-start | bytes 2162696 | tf_op jit(solution)/shard_map/ppermute | solution.py:547
  102.4 46.2 %collective-permute-start.19 = (bf16[128,2816]{1,0:T(8,128)(2,1)}, bf16[128,2816]{1,0:T(8,128)(2,1)S(1)}, u32[]{:S(2)}, u32[]{:S(2)}) collective-permute-start(bf16[128,2816]{1,0:T(8,128)(2,1)} %copy-done.43), channel_id=1, source_target_pairs={{0,4},{4,0},{1,5},{5,1},{2,6},{6,2},{3,7},{7,3},{8,12},{12,8},{9,1... | collective-permute-start | bytes 2162696 | tf_op jit(solution)/shard_map/ppermute | solution.py:547
  106.6 43.6 %collective-permute-start.21 = (bf16[128,2816]{1,0:T(8,128)(2,1)}, bf16[128,2816]{1,0:T(8,128)(2,1)S(1)}, u32[]{:S(2)}, u32[]{:S(2)}) collective-permute-start(bf16[128,2816]{1,0:T(8,128)(2,1)} %copy-done.42), channel_id=1, source_target_pairs={{0,4},{4,0},{1,5},{5,1},{2,6},{6,2},{3,7},{7,3},{8,12},{12,8},{9,1... | collective-permute-start | bytes 2162696 | tf_op jit(solution)/shard_map/ppermute | solution.py:547
  114.8 46.3 %collective-permute-start.24 = (bf16[704,512]{1,0:T(8,128)(2,1)S(1)}, bf16[704,512]{1,0:T(8,128)(2,1)}, u32[]{:S(2)}, u32[]{:S(2)}) collective-permute-start(bf16[704,512]{1,0:T(8,128)(2,1)S(1)} %get-tuple-element.790), channel_id=1, source_target_pairs={{0,4},{4,0},{1,5},{5,1},{2,6},{6,2},{3,7},{7,3},{8,12},{12,8},{9,1... | collective-permute-start | bytes 2162696 | tf_op jit(solution)/shard_map/ppermute | solution.py:547
  122.0 39.1 %collective-permute-start.20 = (bf16[128,2816]{1,0:T(8,128)(2,1)}, bf16[128,2816]{1,0:T(8,128)(2,1)S(1)}, u32[]{:S(2)}, u32[]{:S(2)}) collective-permute-start(bf16[128,2816]{1,0:T(8,128)(2,1)} %collective-permute-done.9), channel_id=1, source_target_pairs={{0,8},{8,0},{16,24},{24,16},{1,9},{9,1},{17,25},{25,17},{2,10},{10... | collective-permute-start | bytes 2162696 | tf_op jit(solution)/shard_map/ppermute | solution.py:556
  176.4 34.5 %collective-permute-start.23 = (bf16[128,2816]{1,0:T(8,128)(2,1)S(1)}, bf16[128,2816]{1,0:T(8,128)(2,1)S(1)}, u32[]{:S(2)}, u32[]{:S(2)}) collective-permute-start(bf16[128,2816]{1,0:T(8,128)(2,1)S(1)} %collective-permute-done.21), channel_id=1, source_target_pairs={{0,8},{8,0},{16,24},{24,16},{1,9},{9,1},{17,25},{25,17},{2,10},{10... | collective-permute-start | bytes 2162696 | tf_op jit(solution)/shard_map/ppermute | solution.py:556
  178.4 62.1 %collective-permute-start.26 = (bf16[704,512]{1,0:T(8,128)(2,1)}, bf16[704,512]{1,0:T(8,128)(2,1)}, u32[]{:S(2)}, u32[]{:S(2)}) collective-permute-start(bf16[704,512]{1,0:T(8,128)(2,1)} %collective-permute-done.24), channel_id=1, source_target_pairs={{0,8},{8,0},{16,24},{24,16},{1,9},{9,1},{17,25},{25,17},{2,10},{10... | collective-permute-start | bytes 2162696 | tf_op jit(solution)/shard_map/ppermute | solution.py:556
  178.5 63.2 %collective-permute-start.27 = (bf16[704,512]{1,0:T(8,128)(2,1)}, bf16[704,512]{1,0:T(8,128)(2,1)}, u32[]{:S(2)}, u32[]{:S(2)}) collective-permute-start(bf16[704,512]{1,0:T(8,128)(2,1)} %collective-permute-done.25), channel_id=1, source_target_pairs={{0,8},{8,0},{16,24},{24,16},{1,9},{9,1},{17,25},{25,17},{2,10},{10... | collective-permute-start | bytes 2162696 | tf_op jit(solution)/shard_map/ppermute | solution.py:556
  233.2 46.0 %collective-permute-start.28 = (bf16[704,1024]{1,0:T(8,128)(2,1)}, bf16[704,1024]{1,0:T(8,128)(2,1)}, u32[]{:S(2)}, u32[]{:S(2)}) collective-permute-start(bf16[704,1024]{1,0:T(8,128)(2,1)} %fusion.17), channel_id=1, source_target_pairs={{0,4},{4,0},{1,5},{5,1},{2,6},{6,2},{3,7},{7,3},{8,12},{12,8},{9,1... | collective-permute-start | bytes 4325384 | tf_op jit(solution)/shard_map/ppermute | solution.py:547
  278.4 35.8 %collective-permute-start.30 = (bf16[704,1024]{1,0:T(8,128)(2,1)}, bf16[704,1024]{1,0:T(8,128)(2,1)S(1)}, u32[]{:S(2)}, u32[]{:S(2)}) collective-permute-start(bf16[704,1024]{1,0:T(8,128)(2,1)} %fusion.20), channel_id=1, source_target_pairs={{0,4},{4,0},{1,5},{5,1},{2,6},{6,2},{3,7},{7,3},{8,12},{12,8},{9,1... | collective-permute-start | bytes 4325384 | tf_op jit(solution)/shard_map/ppermute | solution.py:547
  287.7 38.7 %collective-permute-start.29 = (bf16[704,1024]{1,0:T(8,128)(2,1)S(1)}, bf16[704,1024]{1,0:T(8,128)(2,1)S(1)}, u32[]{:S(2)}, u32[]{:S(2)}) collective-permute-start(bf16[704,1024]{1,0:T(8,128)(2,1)S(1)} %add_convert_fusion.11), channel_id=1, source_target_pairs={{0,8},{24,16},{1,9},{25,17},{2,10},{26,18},{3,11},{27,19},{4,12},{... | collective-permute-start | bytes 4325384 | tf_op jit(solution)/shard_map/ppermute | solution.py:559
  295.1 99.9 %collective-permute-start.37 = (bf16[256,2816]{1,0:T(8,128)(2,1)}, bf16[256,2816]{1,0:T(8,128)(2,1)}, u32[]{:S(2)}, u32[]{:S(2)}) collective-permute-start(bf16[256,2816]{1,0:T(8,128)(2,1)} %convolution_convert_fusion.2), channel_id=1, source_target_pairs={{0,4},{4,0},{1,5},{5,1},{2,6},{6,2},{3,7},{7,3},{8,12},{12,8},{9,1... | collective-permute-start | bytes 4325384 | tf_op jit(solution)/shard_map/ppermute | solution.py:547
  326.3 133.4 %collective-permute-start.51 = (bf16[256,2816]{1,0:T(8,128)(2,1)}, bf16[256,2816]{1,0:T(8,128)(2,1)}, u32[]{:S(2)}, u32[]{:S(2)}) collective-permute-start(bf16[256,2816]{1,0:T(8,128)(2,1)} %convolution_convert_fusion.1), channel_id=1, source_target_pairs={{0,4},{4,0},{1,5},{5,1},{2,6},{6,2},{3,7},{7,3},{8,12},{12,8},{9,1... | collective-permute-start | bytes 4325384 | tf_op jit(solution)/shard_map/ppermute | solution.py:547
  329.5 36.5 %collective-permute-start.42 = (bf16[128,2048]{1,0:T(8,128)(2,1)}, bf16[128,2048]{1,0:T(8,128)(2,1)}, u32[]{:S(2)}, u32[]{:S(2)}) collective-permute-start(bf16[128,2048]{1,0:T(8,128)(2,1)} %get-tuple-element.534), channel_id=1, source_target_pairs={{0,1},{1,0},{2,3},{3,2},{4,5},{5,4},{6,7},{7,6},{8,9},{9,8},{10,11... | collective-permute-start | bytes 1572872 | tf_op jit(solution)/shard_map/ppermute | solution.py:550
  334.0 71.6 %collective-permute-start.36 = (bf16[704,1024]{1,0:T(8,128)(2,1)}, bf16[704,1024]{1,0:T(8,128)(2,1)}, u32[]{:S(2)}, u32[]{:S(2)}) collective-permute-start(bf16[704,1024]{1,0:T(8,128)(2,1)} %add_convert_fusion.10), channel_id=1, source_target_pairs={{0,8},{24,16},{1,9},{25,17},{2,10},{26,18},{3,11},{27,19},{4,12},{... | collective-permute-start | bytes 4325384 | tf_op jit(solution)/shard_map/ppermute | solution.py:559
  337.5 30.2 %collective-permute-start.43 = (bf16[128,2048]{1,0:T(8,128)(2,1)}, bf16[128,2048]{1,0:T(8,128)(2,1)}, u32[]{:S(2)}, u32[]{:S(2)}) collective-permute-start(bf16[128,2048]{1,0:T(8,128)(2,1)} %collective-permute-done.41), channel_id=1, source_target_pairs={{0,1},{1,0},{2,3},{3,2},{4,5},{5,4},{6,7},{7,6},{8,9},{9,8},{10,11... | collective-permute-start | bytes 1572872 | tf_op jit(solution)/shard_map/ppermute | solution.py:550
  366.0 44.9 %collective-permute-start.35 = (bf16[704,1024]{1,0:T(8,128)(2,1)}, bf16[704,1024]{1,0:T(8,128)(2,1)}, u32[]{:S(2)}, u32[]{:S(2)}) collective-permute-start(bf16[704,1024]{1,0:T(8,128)(2,1)} %add_convert_fusion.9), channel_id=1, source_target_pairs={{8,16},{16,8},{9,17},{17,9},{10,18},{18,10},{11,19},{19,11},{12,20... | collective-permute-start | bytes 4325384 | tf_op jit(solution)/shard_map/ppermute | solution.py:562
  401.1 62.1 %collective-permute-start.50 = (bf16[256,2816]{1,0:T(8,128)(2,1)}, bf16[256,2816]{1,0:T(8,128)(2,1)}, u32[]{:S(2)}, u32[]{:S(2)}) collective-permute-start(bf16[256,2816]{1,0:T(8,128)(2,1)} %fusion), channel_id=1, source_target_pairs={{0,8},{24,16},{1,9},{25,17},{2,10},{26,18},{3,11},{27,19},{4,12},{... | collective-permute-start | bytes 4325384 | tf_op jit(solution)/shard_map/ppermute | solution.py:559
  409.1 58.1 %collective-permute-start.49 = (bf16[704,1024]{1,0:T(8,128)(2,1)}, bf16[704,1024]{1,0:T(8,128)(2,1)}, u32[]{:S(2)}, u32[]{:S(2)}) collective-permute-start(bf16[704,1024]{1,0:T(8,128)(2,1)} %add_convert_fusion.8), channel_id=1, source_target_pairs={{8,16},{16,8},{9,17},{17,9},{10,18},{18,10},{11,19},{19,11},{12,20... | collective-permute-start | bytes 4325384 | tf_op jit(solution)/shard_map/ppermute | solution.py:562
  455.3 38.2 %collective-permute-start.48 = (bf16[704,1024]{1,0:T(8,128)(2,1)S(1)}, bf16[704,1024]{1,0:T(8,128)(2,1)S(1)}, u32[]{:S(2)}, u32[]{:S(2)}) collective-permute-start(bf16[704,1024]{1,0:T(8,128)(2,1)S(1)} %copy-done.59), channel_id=1, source_target_pairs={{8,0},{16,24},{9,1},{17,25},{10,2},{18,26},{11,3},{19,27},{12,4},{... | collective-permute-start | bytes 4325384 | tf_op jit(solution)/shard_map/ppermute | solution.py:565
  458.5 53.6 %collective-permute-start.44 = (bf16[256,2048]{1,0:T(8,128)(2,1)S(1)}, bf16[256,2048]{1,0:T(8,128)(2,1)}, u32[]{:S(2)}, u32[]{:S(2)}) collective-permute-start(bf16[256,2048]{1,0:T(8,128)(2,1)S(1)} %copy-done.40), channel_id=1, source_target_pairs={{0,1},{1,0},{2,3},{3,2},{4,5},{5,4},{6,7},{7,6},{8,9},{9,8},{10,11... | collective-permute-start | bytes 3145736 | tf_op jit(solution)/shard_map/ppermute | solution.py:550
  459.7 56.8 %collective-permute-start.67 = (bf16[256,2048]{1,0:T(8,128)(2,1)S(1)}, bf16[256,2048]{1,0:T(8,128)(2,1)}, u32[]{:S(2)}, u32[]{:S(2)}) collective-permute-start(bf16[256,2048]{1,0:T(8,128)(2,1)S(1)} %get-tuple-element.569), channel_id=1, source_target_pairs={{0,1},{1,0},{2,3},{3,2},{4,5},{5,4},{6,7},{7,6},{8,9},{9,8},{10,11... | collective-permute-start | bytes 3145736 | tf_op jit(solution)/shard_map/ppermute | solution.py:550
  463.2 32.0 %collective-permute-start.47 = (bf16[128,2048]{1,0:T(8,128)(2,1)S(1)}, bf16[128,2048]{1,0:T(8,128)(2,1)S(1)}, u32[]{:S(2)}, u32[]{:S(2)}) collective-permute-start(bf16[128,2048]{1,0:T(8,128)(2,1)S(1)} %slice.433), channel_id=1, source_target_pairs={{0,2},{2,0},{1,3},{3,1},{4,6},{6,4},{5,7},{7,5},{8,10},{10,8},{9,1... | collective-permute-start | bytes 1572872 | tf_op jit(solution)/shard_map/ppermute | solution.py:553
  467.2 30.2 %collective-permute-start.53 = (bf16[128,2048]{1,0:T(8,128)(2,1)S(1)}, bf16[128,2048]{1,0:T(8,128)(2,1)S(1)}, u32[]{:S(2)}, u32[]{:S(2)}) collective-permute-start(bf16[128,2048]{1,0:T(8,128)(2,1)S(1)} %slice.432), channel_id=1, source_target_pairs={{0,2},{2,0},{1,3},{3,1},{4,6},{6,4},{5,7},{7,5},{8,10},{10,8},{9,1... | collective-permute-start | bytes 1572872 | tf_op jit(solution)/shard_map/ppermute | solution.py:553
  502.6 30.4 %collective-permute-start.66 = (bf16[512,1024]{1,0:T(8,128)(2,1)S(1)}, bf16[512,1024]{1,0:T(8,128)(2,1)S(1)}, u32[]{:S(2)}, u32[]{:S(2)}) collective-permute-start(bf16[512,1024]{1,0:T(8,128)(2,1)S(1)} %copy-done.73), channel_id=1, source_target_pairs={{0,4},{4,0},{1,5},{5,1},{2,6},{6,2},{3,7},{7,3},{8,12},{12,8},{9,1... | collective-permute-start | bytes 3145736 | tf_op jit(solution)/shard_map/ppermute | solution.py:547
  509.8 32.2 %collective-permute-start.65 = (bf16[256,2816]{1,0:T(8,128)(2,1)S(1)}, bf16[256,2816]{1,0:T(8,128)(2,1)S(1)}, u32[]{:S(2)}, u32[]{:S(2)}) collective-permute-start(bf16[256,2816]{1,0:T(8,128)(2,1)S(1)} %fusion.1), channel_id=1, source_target_pairs={{0,8},{24,16},{1,9},{25,17},{2,10},{26,18},{3,11},{27,19},{4,12},{... | collective-permute-start | bytes 4325384 | tf_op jit(solution)/shard_map/ppermute | solution.py:559
  511.3 31.4 %collective-permute-start.64 = (bf16[256,2816]{1,0:T(8,128)(2,1)S(1)}, bf16[256,2816]{1,0:T(8,128)(2,1)S(1)}, u32[]{:S(2)}, u32[]{:S(2)}) collective-permute-start(bf16[256,2816]{1,0:T(8,128)(2,1)S(1)} %add_convert_fusion.6), channel_id=1, source_target_pairs={{8,16},{16,8},{9,17},{17,9},{10,18},{18,10},{11,19},{19,11},{12,20... | collective-permute-start | bytes 4325384 | tf_op jit(solution)/shard_map/ppermute | solution.py:562
  512.1 44.7 %collective-permute-start.63 = (bf16[704,1024]{1,0:T(8,128)(2,1)S(1)}, bf16[704,1024]{1,0:T(8,128)(2,1)S(1)}, u32[]{:S(2)}, u32[]{:S(2)}) collective-permute-start(bf16[704,1024]{1,0:T(8,128)(2,1)S(1)} %add_convert_fusion.5), channel_id=1, source_target_pairs={{8,0},{16,24},{9,1},{17,25},{10,2},{18,26},{11,3},{19,27},{12,4},{... | collective-permute-start | bytes 4325384 | tf_op jit(solution)/shard_map/ppermute | solution.py:565
  516.5 26.2 %collective-permute-start.60 = (bf16[128,2048]{1,0:T(8,128)(2,1)S(1)}, bf16[128,2048]{1,0:T(8,128)(2,1)S(1)}, u32[]{:S(2)}, u32[]{:S(2)}) collective-permute-start(bf16[128,2048]{1,0:T(8,128)(2,1)S(1)} %fusion.51.refs_4_), channel_id=1, source_target_pairs={{0,2},{2,0},{1,3},{3,1},{4,6},{6,4},{5,7},{7,5},{8,10},{10,8},{9,1... | collective-permute-start | bytes 1572872 | tf_op jit(solution)/shard_map/ppermute | solution.py:553
  533.0 26.4 %collective-permute-start.61 = (bf16[128,2048]{1,0:T(8,128)(2,1)S(1)}, bf16[128,2048]{1,0:T(8,128)(2,1)S(1)}, u32[]{:S(2)}, u32[]{:S(2)}) collective-permute-start(bf16[128,2048]{1,0:T(8,128)(2,1)S(1)} %fusion.51.refs_4_), channel_id=1, source_target_pairs={{0,1},{1,0},{2,3},{3,2},{4,5},{5,4},{6,7},{7,6},{8,9},{9,8},{10,11... | collective-permute-start | bytes 1572872 | tf_op jit(solution)/shard_map/ppermute | solution.py:550
  542.7 34.4 %collective-permute-start.56 = (bf16[128,2048]{1,0:T(8,128)(2,1)}, bf16[128,2048]{1,0:T(8,128)(2,1)S(1)}, u32[]{:S(2)}, u32[]{:S(2)}) collective-permute-start(bf16[128,2048]{1,0:T(8,128)(2,1)} %slice.431), channel_id=1, source_target_pairs={{0,2},{2,0},{1,3},{3,1},{4,6},{6,4},{5,7},{7,5},{8,10},{10,8},{9,1... | collective-permute-start | bytes 1572872 | tf_op jit(solution)/shard_map/ppermute | solution.py:553
  559.4 32.0 %collective-permute-start.77 = (bf16[1024,640]{1,0:T(8,128)(2,1)}, bf16[1024,640]{1,0:T(8,128)(2,1)}, u32[]{:S(2)}, u32[]{:S(2)}) collective-permute-start(bf16[1024,640]{1,0:T(8,128)(2,1)} %fusion.23), channel_id=1, source_target_pairs={{0,4},{4,0},{1,5},{5,1},{2,6},{6,2},{3,7},{7,3},{8,12},{12,8},{9,1... | collective-permute-start | bytes 3932168 | tf_op jit(solution)/shard_map/ppermute | solution.py:547
  559.7 65.5 %collective-permute-start.82 = (bf16[256,2816]{1,0:T(8,128)(2,1)}, bf16[256,2816]{1,0:T(8,128)(2,1)}, u32[]{:S(2)}, u32[]{:S(2)}) collective-permute-start(bf16[256,2816]{1,0:T(8,128)(2,1)} %convolution_convert_fusion), channel_id=1, source_target_pairs={{0,4},{4,0},{1,5},{5,1},{2,6},{6,2},{3,7},{7,3},{8,12},{12,8},{9,1... | collective-permute-start | bytes 4325384 | tf_op jit(solution)/shard_map/ppermute | solution.py:547
  561.8 33.7 %collective-permute-start.76 = (bf16[512,1024]{1,0:T(8,128)(2,1)}, bf16[512,1024]{1,0:T(8,128)(2,1)}, u32[]{:S(2)}, u32[]{:S(2)}) collective-permute-start(bf16[512,1024]{1,0:T(8,128)(2,1)} %add_convert_fusion.17), channel_id=1, source_target_pairs={{0,8},{24,16},{1,9},{25,17},{2,10},{26,18},{3,11},{27,19},{4,12},{... | collective-permute-start | bytes 3145736 | tf_op jit(solution)/shard_map/ppermute | solution.py:559
  581.8 36.5 %collective-permute-start.79 = (bf16[256,2816]{1,0:T(8,128)(2,1)S(1)}, bf16[256,2816]{1,0:T(8,128)(2,1)S(1)}, u32[]{:S(2)}, u32[]{:S(2)}) collective-permute-start(bf16[256,2816]{1,0:T(8,128)(2,1)S(1)} %add_convert_fusion.3.a_ref), channel_id=1, source_target_pairs={{8,0},{16,24},{9,1},{17,25},{10,2},{18,26},{11,3},{19,27},{12,4},{... | collective-permute-start | bytes 4325384 | tf_op jit(solution)/shard_map/ppermute | solution.py:565
  598.8 48.3 %collective-permute-start.78 = (bf16[256,2816]{1,0:T(8,128)(2,1)S(1)}, bf16[256,2816]{1,0:T(8,128)(2,1)}, u32[]{:S(2)}, u32[]{:S(2)}) collective-permute-start(bf16[256,2816]{1,0:T(8,128)(2,1)S(1)} %add_convert_fusion.2.a_ref), channel_id=1, source_target_pairs={{8,0},{16,24},{9,1},{17,25},{10,2},{18,26},{11,3},{19,27},{12,4},{... | collective-permute-start | bytes 4325384 | tf_op jit(solution)/shard_map/ppermute | solution.py:565
  600.1 44.2 %collective-permute-start.81 = (bf16[1024,640]{1,0:T(8,128)(2,1)}, bf16[1024,640]{1,0:T(8,128)(2,1)}, u32[]{:S(2)}, u32[]{:S(2)}) collective-permute-start(bf16[1024,640]{1,0:T(8,128)(2,1)} %add_convert_fusion.14), channel_id=1, source_target_pairs={{0,8},{24,16},{1,9},{25,17},{2,10},{26,18},{3,11},{27,19},{4,12},{... | collective-permute-start | bytes 3932168 | tf_op jit(solution)/shard_map/ppermute | solution.py:559
  634.7 43.1 %collective-permute-start.84 = (bf16[256,2816]{1,0:T(8,128)(2,1)S(1)}, bf16[256,2816]{1,0:T(8,128)(2,1)}, u32[]{:S(2)}, u32[]{:S(2)}) collective-permute-start(bf16[256,2816]{1,0:T(8,128)(2,1)S(1)} %fusion.2), channel_id=1, source_target_pairs={{0,8},{24,16},{1,9},{25,17},{2,10},{26,18},{3,11},{27,19},{4,12},{... | collective-permute-start | bytes 4325384 | tf_op jit(solution)/shard_map/ppermute | solution.py:559
  656.3 42.5 %collective-permute-start.91 = (bf16[128,2816]{1,0:T(8,128)(2,1)}, bf16[128,2816]{1,0:T(8,128)(2,1)S(1)}, u32[]{:S(2)}, u32[]{:S(2)}) collective-permute-start(bf16[128,2816]{1,0:T(8,128)(2,1)} %convolution_convert_fusion.3), channel_id=1, source_target_pairs={{0,4},{4,0},{1,5},{5,1},{2,6},{6,2},{3,7},{7,3},{8,12},{12,8},{9,1... | collective-permute-start | bytes 2162696 | tf_op jit(solution)/shard_map/ppermute | solution.py:547
  669.2 26.9 %collective-permute-start.92 = (bf16[512,1024]{1,0:T(8,128)(2,1)S(1)}, bf16[512,1024]{1,0:T(8,128)(2,1)S(1)}, u32[]{:S(2)}, u32[]{:S(2)}) collective-permute-start(bf16[512,1024]{1,0:T(8,128)(2,1)S(1)} %add_convert_fusion.15), channel_id=1, source_target_pairs={{8,0},{16,24},{9,1},{17,25},{10,2},{18,26},{11,3},{19,27},{12,4},{... | collective-permute-start | bytes 3145736 | tf_op jit(solution)/shard_map/ppermute | solution.py:565
  675.3 30.1 %collective-permute-start.90 = (bf16[128,2816]{1,0:T(8,128)(2,1)S(1)}, bf16[128,2816]{1,0:T(8,128)(2,1)S(1)}, u32[]{:S(2)}, u32[]{:S(2)}) collective-permute-start(bf16[128,2816]{1,0:T(8,128)(2,1)S(1)} %fusion.3), channel_id=1, source_target_pairs={{0,8},{24,16},{1,9},{25,17},{2,10},{26,18},{3,11},{27,19},{4,12},{... | collective-permute-start | bytes 2162696 | tf_op jit(solution)/shard_map/ppermute | solution.py:559
  677.8 28.5 %collective-permute-start.89 = (f32[2,1024]{1,0:T(2,128)S(1)}, f32[2,1024]{1,0:T(2,128)S(1)}, u32[]{:S(2)}, u32[]{:S(2)}) collective-permute-start(f32[2,1024]{1,0:T(2,128)S(1)} %slice_add_fusion), channel_id=1, source_target_pairs={{0,8},{24,16},{1,9},{25,17},{2,10},{26,18},{3,11},{27,19},{4,12},{... | collective-permute-start | bytes 24584 | tf_op jit(solution)/shard_map/ppermute | solution.py:559
  696.1 32.7 %collective-permute-start.87 = (bf16[1024,640]{1,0:T(8,128)(2,1)S(1)}, bf16[1024,640]{1,0:T(8,128)(2,1)S(1)}, u32[]{:S(2)}, u32[]{:S(2)}) collective-permute-start(bf16[1024,640]{1,0:T(8,128)(2,1)S(1)} %add_convert_fusion.12), channel_id=1, source_target_pairs={{8,0},{16,24},{9,1},{17,25},{10,2},{18,26},{11,3},{19,27},{12,4},{... | collective-permute-start | bytes 3932168 | tf_op jit(solution)/shard_map/ppermute | solution.py:565
  700.7 28.2 %collective-permute-start.93 = (bf16[128,2816]{1,0:T(8,128)(2,1)S(1)}, bf16[128,2816]{1,0:T(8,128)(2,1)S(1)}, u32[]{:S(2)}, u32[]{:S(2)}) collective-permute-start(bf16[128,2816]{1,0:T(8,128)(2,1)S(1)} %fusion.4), channel_id=1, source_target_pairs={{0,8},{24,16},{1,9},{25,17},{2,10},{26,18},{3,11},{27,19},{4,12},{... | collective-permute-start | bytes 2162696 | tf_op jit(solution)/shard_map/ppermute | solution.py:559
  707.3 54.8 %collective-permute-start.95 = (bf16[256,2816]{1,0:T(8,128)(2,1)S(1)}, bf16[256,2816]{1,0:T(8,128)(2,1)S(1)}, u32[]{:S(2)}, u32[]{:S(2)}) collective-permute-start(bf16[256,2816]{1,0:T(8,128)(2,1)S(1)} %add_convert_fusion.a_ref), channel_id=1, source_target_pairs={{8,0},{16,24},{9,1},{17,25},{10,2},{18,26},{11,3},{19,27},{12,4},{... | collective-permute-start | bytes 4325384 | tf_op jit(solution)/shard_map/ppermute | solution.py:565
  729.1 35.8 %collective-permute-start.94 = (bf16[128,2816]{1,0:T(8,128)(2,1)S(1)}, bf16[128,2816]{1,0:T(8,128)(2,1)S(1)}, u32[]{:S(2)}, u32[]{:S(2)}) collective-permute-start(bf16[128,2816]{1,0:T(8,128)(2,1)S(1)} %add_convert_fusion.21), channel_id=1, source_target_pairs={{8,16},{16,8},{9,17},{17,9},{10,18},{18,10},{11,19},{19,11},{12,20... | collective-permute-start | bytes 2162696 | tf_op jit(solution)/shard_map/ppermute | solution.py:562
  730.0 47.6 %collective-permute-start.99 = (bf16[128,2816]{1,0:T(8,128)(2,1)S(1)}, bf16[128,2816]{1,0:T(8,128)(2,1)S(1)}, u32[]{:S(2)}, u32[]{:S(2)}) collective-permute-start(bf16[128,2816]{1,0:T(8,128)(2,1)S(1)} %add_convert_fusion.20.a_ref), channel_id=1, source_target_pairs={{8,0},{16,24},{9,1},{17,25},{10,2},{18,26},{11,3},{19,27},{12,4},{... | collective-permute-start | bytes 2162696 | tf_op jit(solution)/shard_map/ppermute | solution.py:565
  (148 other events, 1522.6 us)

commit v2 on v1

v2 whole, which is shorter than its diff:
```python
import dataclasses
import functools
from typing import Any

import jax
import jax.numpy as jnp
from jax import lax
from jax.experimental import pallas as pl
from jax.experimental.pallas import tpu as pltpu
from jax.sharding import PartitionSpec as P

HEAD_DIM = 64
NORM_EPS = 1e-05
ROPE_THETA = 10000.0
LOG2E = 1.4426950408889634
MASKED = -1e30
F32 = jnp.float32
BF16 = jnp.bfloat16
MIB = 1024 * 1024


def touch(order, *xs):
    order.last = (*order.last, *xs)


def dot(a, b, ca=1, cb=0):
    return lax.dot_general(a, b, (((ca,), (cb,)), ((), ())), preferred_element_type=F32)


def call(body, grid, ins, outs, shapes, scratch=(), scalars=0, alias=None, vmem=20):
    return pl.pallas_call(
        body,
        out_shape=shapes,
        grid_spec=pltpu.PrefetchScalarGridSpec(
            num_scalar_prefetch=scalars,
            grid=grid,
            in_specs=ins,
            out_specs=outs,
            scratch_shapes=list(scratch),
        ),
        input_output_aliases=alias or {},
        compiler_params=pltpu.CompilerParams(vmem_limit_bytes=vmem * MIB),
        cost_estimate=pl.CostEstimate(flops=3000000000, bytes_accessed=8000000, transcendentals=0),
    )


@functools.partial(
    jax.tree_util.register_dataclass, data_fields=["array"], meta_fields=["base", "late"]
)
@dataclasses.dataclass(frozen=True)
class Part:
    array: Any
    base: int = 0
    late: Any = None

    def start(self, width, p):
        if self.late is None:
            return self.base
        return width // 2 + (p ^ self.late) * (width // 4) + self.base


class Order:
    def __init__(self):
        self.last = ()

    def __call__(self, step, *xs):
        flat, tree = jax.tree.flatten(xs)
        if self.last:
            flat = lax.optimization_barrier((tuple(flat), self.last))[0]
        out = step(*jax.tree.unflatten(tree, flat))
        self.last = tuple(jax.tree.leaves(out))
        return out


def first_norm(hidden, gain, place, block):
    rows, width = hidden.shape
    half = width // 2

    def body(p, a_ref, b_ref, g_ref, n_ref):
        a, b = a_ref[...], b_ref[...]
        total = jnp.sum(a * a, -1, keepdims=True) + jnp.sum(b * b, -1, keepdims=True)
        inv = lax.rsqrt(total * (1.0 / width) + NORM_EPS)
        n_ref[:, :half] = (a * inv * g_ref[:, :half]).astype(BF16)
        n_ref[:, half:] = (b * inv * g_ref[:, half:]).astype(BF16)

    return call(
        body,
        (rows // block,),
        [
            pl.BlockSpec((block, half), lambda i, p: (i, p[1])),
            pl.BlockSpec((block, half), lambda i, p: (i, 1 - p[1])),
            pl.BlockSpec((1, width), lambda i, p: (0, 0)),
        ],
        pl.BlockSpec((block, width), lambda i, p: (i, 0)),
        jax.ShapeDtypeStruct((rows, width), BF16),
        scalars=1,
    )(place, hidden, hidden, gain)


def local_cast(x, place, block):
    rows, width = x.shape
    half = width // 2

    def body(p, a_ref, b_ref, o_ref):
        o_ref[:, :half] = a_ref[...].astype(BF16)
        o_ref[:, half:] = b_ref[...].astype(BF16)

    def row(i, p):
        return (i // 4) * 4 + ((i % 4) ^ p[0])

    return call(
        body,
        (rows // block,),
        [
            pl.BlockSpec((block, half), lambda i, p: (row(i, p), p[1])),
            pl.BlockSpec((block, half), lambda i, p: (row(i, p), 1 - p[1])),
        ],
        pl.BlockSpec((block, width), lambda i, p: (i, 0)),
        jax.ShapeDtypeStruct((rows, width), BF16),
        scalars=1,
    )(place, x, x)


def join_gate_up(a, b, middle, at, rows, before):
    count, cols = a.shape
    ff = cols // 2
    block = min(128, count)

    def body(p, a_ref, b_ref, *refs):
        o_ref = refs[-1]

        def put(src):
            for j in range(ff // 128):
                for g in range(2):
                    o_ref[0, :, g, 128 * j : 128 * (j + 1)] = src[
                        :, 256 * j + 128 * g : 256 * j + 128 * (g + 1)
                    ].astype(F32)

        @pl.when(p[0] == 1)
        def _():
            put(a_ref)

        @pl.when(p[0] == 0)
        def _():
            put(b_ref)

    return call(
        body,
        (count // block,),
        [pl.BlockSpec((block, cols), lambda i, p: (i, 0))] * 2
        + [pl.BlockSpec(memory_space=pl.ANY)] * len(before),
        pl.BlockSpec((1, block, 2, ff), lambda i, p: (0, at // block + i, 0, 0)),
        jax.ShapeDtypeStruct((1, rows, 2, ff), F32),
        scalars=1,
        alias={3 + k: k for k in range(len(before))},
    )(middle, a, b, *before)


def project_qkv(normed, weights, cos_t, sin_t, group):
    rows, width = normed.shape
    seqs, half, length = cos_t.shape
    cols = weights[0].shape[1]
    tile = min(256, length)
    per = length // tile
    depth = width // len(weights)
    parts = len(weights)

    def body(n_ref, cos_ref, sin_ref, *refs):
        q_ref, kv_ref = refs[parts:]
        acc = dot(n_ref[:, :depth], refs[0][...])
        for k in range(1, parts):
            acc = acc + dot(n_ref[:, k * depth : (k + 1) * depth], refs[k][...])
        t = acc.T
        cos, sin = cos_ref[0], sin_ref[0]
        for h in range(group + 1):
            a, b = t[2 * half * h : 2 * half * h + half], t[2 * half * h + half : 2 * half * (h + 1)]
            r = jnp.concatenate([a * cos - b * sin, b * cos + a * sin], 0).astype(BF16)
            if h < group:
                q_ref[0, 2 * half * h : 2 * half * (h + 1)] = r
            else:
                kv_ref[0, : 2 * half] = r
        kv_ref[0, 2 * half :] = t[2 * half * (group + 1) :].astype(BF16)

    return call(
        body,
        (seqs, per),
        [
            pl.BlockSpec((tile, width), lambda s, i: (s * per + i, 0)),
            pl.BlockSpec((1, half, tile), lambda s, i: (s, 0, i)),
            pl.BlockSpec((1, half, tile), lambda s, i: (s, 0, i)),
        ]
        + [pl.BlockSpec((depth, cols), lambda s, i: (0, 0))] * parts,
        [
            pl.BlockSpec((1, group * HEAD_DIM, tile), lambda s, i: (s, 0, i)),
            pl.BlockSpec((1, 2 * HEAD_DIM, tile), lambda s, i: (s, 0, i)),
        ],
        [
            jax.ShapeDtypeStruct((seqs, group * HEAD_DIM, length), BF16),
            jax.ShapeDtypeStruct((seqs, 2 * HEAD_DIM, length), BF16),
        ],
    )(normed, cos_t, sin_t, *weights)


def attend(s, q_t, kv_t, starts, bounds, scale):
    seqs, cols, length = q_t.shape
    total = kv_t.shape[2]
    heads = cols // HEAD_DIM
    tq, tk = min(256, length), min(256, total)

    def body(b_ref, q_ref, kv_ref, st_ref, att_ref, att_t_ref, lse_ref, kn, m, l, acc):
        i = pl.program_id(0)

        @pl.when(i == 0)
        def _():
            kn[...] = kv_ref[0, :HEAD_DIM].astype(F32).T.astype(BF16)

        qid = b_ref[0] + i * tq + lax.broadcasted_iota(jnp.int32, (1, tq), 1)
        start = st_ref[0]
        m[...] = jnp.full_like(m, MASKED)
        l[...] = jnp.zeros_like(l)
        acc[...] = jnp.zeros_like(acc)

        def step(t, _):
            k0 = pl.multiple_of(t * tk, tk)
            kid = k0 + lax.broadcasted_iota(jnp.int32, (tk, 1), 0)
            ok = (kid <= qid) & (kid >= start)
            keys = kn[pl.ds(k0, tk), :]
            vals = kv_ref[0, HEAD_DIM:, pl.ds(k0, tk)]
            for h in range(heads):
                lo = h * HEAD_DIM
                sc = dot(keys, q_ref[0, lo : lo + HEAD_DIM]) * (scale * LOG2E)
                sc = jnp.where(ok, sc, MASKED)
                old = m[h : h + 1]
                new = jnp.maximum(old, jnp.max(sc, 0, keepdims=True))
                e = jnp.exp2(sc - new)
                fade = jnp.exp2(old - new)
                m[h : h + 1] = new
                l[h : h + 1] = l[h : h + 1] * fade + jnp.sum(e, 0, keepdims=True)
                acc[lo : lo + HEAD_DIM] = acc[lo : lo + HEAD_DIM] * fade + dot(vals, e.astype(BF16))
            return 0

        lax.fori_loop(b_ref[2 + 2 * i], b_ref[3 + 2 * i], step, 0)
        for h in range(heads):
            lo = h * HEAD_DIM
            acc[lo : lo + HEAD_DIM] = acc[lo : lo + HEAD_DIM] / l[h : h + 1]
        att_t_ref[...] = acc[...].astype(BF16)
        att_ref[...] = acc[...].T.astype(BF16)
        lse_ref[...] = m[...] + jnp.log2(l[...])

    return call(
        body,
        (length // tq,),
        [
            pl.BlockSpec((1, cols, tq), lambda i, b: (s, 0, i)),
            pl.BlockSpec((1, 2 * HEAD_DIM, total), lambda i, b: (s, 0, 0)),
            pl.BlockSpec((1, 1, tq), lambda i, b: (s, 0, i)),
        ],
        [
            pl.BlockSpec((tq, cols), lambda i, b: (i, 0)),
            pl.BlockSpec((cols, tq), lambda i, b: (0, i)),
            pl.BlockSpec((heads, tq), lambda i, b: (0, i)),
        ],
        [
            jax.ShapeDtypeStruct((length, cols), BF16),
            jax.ShapeDtypeStruct((cols, length), BF16),
            jax.ShapeDtypeStruct((heads, length), F32),
        ],
        scratch=[
            pltpu.VMEM((total, HEAD_DIM), BF16),
            pltpu.VMEM((heads, tq), F32),
            pltpu.VMEM((heads, tq), F32),
            pltpu.VMEM((cols, tq), F32),
        ],
        scalars=1,
    )(bounds, q_t, kv_t, starts)


def attend_back(s, q_t, kv_t, starts, bounds, att_t, out_parts, d2, lse, cos_t, sin_t, scale):
    seqs, cols, length = q_t.shape
    width = d2.shape[1]
    parts = len(out_parts)
    total = kv_t.shape[2]
    heads = cols // HEAD_DIM
    half = HEAD_DIM // 2
    tq, tk = min(256, length), min(256, total)

    def body(
        b_ref, q_ref, kv_ref, st_ref, a_ref, d2_ref, lse_ref, cos_ref, sin_ref, *refs
    ):
        w_refs = refs[:parts]
        dq_ref, dkv_ref, early_ref, kn, vn, delta, acc, d_ref = refs[parts:]
        i = pl.program_id(0)

        @pl.when(i == 0)
        def _():
            kn[...] = kv_ref[0, :HEAD_DIM].astype(F32).T.astype(BF16)
            vn[...] = kv_ref[0, HEAD_DIM:].astype(F32).T.astype(BF16)
            dkv_ref[...] = jnp.zeros_like(dkv_ref)

        d_att = 0.0
        for part, w_ref in zip(out_parts, w_refs):
            size = part.array.shape[1]
            at = part.start(width, b_ref[1])
            if part.late is not None:
                at = pl.multiple_of(at, 128)
            d_att = d_att + dot(w_ref[...], d2_ref[:, pl.ds(at, size)], 1, 1)
        d_ref[...] = d_att.astype(BF16)
        qid = b_ref[0] + i * tq + lax.broadcasted_iota(jnp.int32, (1, tq), 1)
        start = st_ref[0]
        for h in range(heads):
            lo = h * HEAD_DIM
            prod = d_ref[lo : lo + HEAD_DIM].astype(F32) * a_ref[lo : lo + HEAD_DIM].astype(F32)
            delta[h : h + 1] = jnp.sum(prod, 0, keepdims=True)
        acc[...] = jnp.zeros_like(acc)

        def step(t, _):
            k0 = pl.multiple_of(t * tk, tk)
            kid = k0 + lax.broadcasted_iota(jnp.int32, (tk, 1), 0)
            ok = (kid <= qid) & (kid >= start)
            keys, vals = kn[pl.ds(k0, tk), :], vn[pl.ds(k0, tk), :]
            keys_t = kv_ref[0, :HEAD_DIM, pl.ds(k0, tk)]
            dk = jnp.zeros((HEAD_DIM, tk), F32)
            dv = jnp.zeros((HEAD_DIM, tk), F32)
            for h in range(heads):
                lo = h * HEAD_DIM
                q, d = q_ref[0, lo : lo + HEAD_DIM], d_ref[lo : lo + HEAD_DIM]
                sc = dot(keys, q) * (scale * LOG2E) - lse_ref[h : h + 1]
                p = jnp.exp2(jnp.where(ok, sc, MASKED))
                dp = dot(vals, d)
                ds = (p * (dp - delta[h : h + 1]) * scale).astype(BF16)
                dv = dv + dot(d, p.astype(BF16), 1, 1)
                dk = dk + dot(q, ds, 1, 1)
                acc[lo : lo + HEAD_DIM] += dot(keys_t, ds)
            dkv_ref[:HEAD_DIM, pl.ds(k0, tk)] += dk
            dkv_ref[HEAD_DIM:, pl.ds(k0, tk)] += dv
            return 0

        lax.fori_loop(b_ref[2 + 2 * i], b_ref[3 + 2 * i], step, 0)
        cos, sin = cos_ref[0], sin_ref[0]
        for h in range(heads):
            lo = h * HEAD_DIM
            c, e = acc[lo : lo + half], acc[lo + half : lo + HEAD_DIM]
            acc[lo : lo + HEAD_DIM] = jnp.concatenate([c * cos + e * sin, e * cos - c * sin], 0)
        dq_ref[...] = acc[...].T.astype(BF16)
        early_ref[...] = dkv_ref[:, :length].astype(BF16)

    return call(
        body,
        (length // tq,),
        [
            pl.BlockSpec((1, cols, tq), lambda i, b: (s, 0, i)),
            pl.BlockSpec((1, 2 * HEAD_DIM, total), lambda i, b: (s, 0, 0)),
            pl.BlockSpec((1, 1, tq), lambda i, b: (s, 0, i)),
            pl.BlockSpec((cols, tq), lambda i, b: (0, i)),
            pl.BlockSpec((tq, d2.shape[1]), lambda i, b: (i, 0)),
            pl.BlockSpec((heads, tq), lambda i, b: (0, i)),
            pl.BlockSpec((1, half, tq), lambda i, b: (s, 0, i)),
            pl.BlockSpec((1, half, tq), lambda i, b: (s, 0, i)),
        ]
        + [pl.BlockSpec(p.array.shape, lambda i, b: (0, 0)) for p in out_parts],
        [
            pl.BlockSpec((tq, cols), lambda i, b: (i, 0)),
            pl.BlockSpec((2 * HEAD_DIM, total), lambda i, b: (0, 0)),
            pl.BlockSpec((2 * HEAD_DIM, length), lambda i, b: (0, 0)),
        ],
        [
            jax.ShapeDtypeStruct((length, cols), BF16),
            jax.ShapeDtypeStruct((2 * HEAD_DIM, total), F32),
            jax.ShapeDtypeStruct((2 * HEAD_DIM, length), BF16),
        ],
        scratch=[
            pltpu.VMEM((total, HEAD_DIM), BF16),
            pltpu.VMEM((total, HEAD_DIM), BF16),
            pltpu.VMEM((heads, tq), F32),
            pltpu.VMEM((cols, tq), F32),
            pltpu.VMEM((cols, tq), BF16),
        ],
        scalars=1,
    )(
        bounds, q_t, kv_t, starts, att_t, d2, lse, cos_t, sin_t, *[p.array for p in out_parts]
    )


def join_kv(mine, other, place):
    seqs, cols, length = mine.shape

    def body(p, m_ref, o_ref, out_ref):
        @pl.when(pl.program_id(0) == 0)
        def _():
            out_ref[...] = m_ref[...]

        @pl.when(pl.program_id(0) == 1)
        def _():
            out_ref[...] = o_ref[...]

    spec = pl.BlockSpec(mine.shape, lambda i, p: (0, 0, 0))
    return call(
        body,
        (2,),
        [spec, spec],
        pl.BlockSpec(mine.shape, lambda i, p: (0, 0, i ^ p[1])),
        jax.ShapeDtypeStruct((seqs, cols, 2 * length), mine.dtype),
        scalars=1,
    )(place, mine, other)


def stack(pieces, place):
    quarter, width = pieces[0].shape
    count = len(pieces)

    def body(p, *refs):
        for k in range(count):

            @pl.when(pl.program_id(0) == k)
            def _():
                refs[-1][...] = refs[k][...]

    return call(
        body,
        (count,),
        [pl.BlockSpec((quarter, width), lambda i, p: (0, 0))] * count,
        pl.BlockSpec((quarter, width), lambda i, p: ((i // 4) * 4 + ((i % 4) ^ p[0]), 0)),
        jax.ShapeDtypeStruct((count * quarter, width), BF16),
        scalars=1,
    )(place, *pieces)


def first_sum(keep, got):
    rows, width = keep.shape
    half = rows // 2
    tile = width // 4

    def body(k_ref, g_ref, send_ref, keep_ref):
        send_ref[...] = (k_ref[half:] + g_ref[half:].astype(F32)).astype(BF16)
        keep_ref[...] = k_ref[:half] + g_ref[:half].astype(F32)

    return call(
        body,
        (4,),
        [pl.BlockSpec((rows, tile), lambda j: (0, j))] * 2,
        [pl.BlockSpec((half, tile), lambda j: (0, j))] * 2,
        [jax.ShapeDtypeStruct((half, width), BF16), jax.ShapeDtypeStruct((half, width), F32)],
    )(keep, got)


def by_rows(step, place, s, quarter, owned, blocks, vectors, outs, sums=0):
    width = owned[0].shape[1]
    half = width // 2
    tile = min(32, quarter)
    per = quarter // tile
    seqs = owned[0].shape[0] // (4 * quarter) if s is None else 1
    n_in = 2 * len(owned) + len(blocks) + len(vectors)

    def body(p, *refs):
        vals = [
            jnp.concatenate([refs[2 * k][...], refs[2 * k + 1][...]], 1) for k in range(len(owned))
        ]
        vals += [r[...].astype(F32) for r in refs[2 * len(owned) : n_in]]
        got = step(*vals)
        for k in range(len(outs)):
            refs[n_in + k][...] = got[k].astype(outs[k])
        for k in range(sums):
            o_ref, x = refs[n_in + len(outs) + k], got[len(outs) + k]

            @pl.when(pl.program_id(0) == 0)
            def _():
                o_ref[...] = x

            @pl.when(pl.program_id(0) > 0)
            def _():
                o_ref[...] += x

    def at(i, p):
        if s is None:
            return ((i // per) * 4 + p[0]) * per + i % per
        return (s * 4 + p[0]) * per + i

    own_specs = [
        pl.BlockSpec((tile, half), lambda i, p: (at(i, p), p[1])),
        pl.BlockSpec((tile, half), lambda i, p: (at(i, p), 1 - p[1])),
    ]
    return call(
        body,
        (seqs * per,),
        own_specs * len(owned)
        + [pl.BlockSpec((tile, width), lambda i, p: (i, 0))] * len(blocks)
        + [pl.BlockSpec((1, width), lambda i, p: (0, 0))] * len(vectors),
        [pl.BlockSpec((tile, width), lambda i, p: (i, 0))] * len(outs)
        + [pl.BlockSpec((1, width), lambda i, p: (0, 0))] * sums,
        [jax.ShapeDtypeStruct((seqs * quarter, width), d) for d in outs]
        + [jax.ShapeDtypeStruct((1, width), F32)] * sums,
        scalars=1,
    )(place, *[x for a in owned for x in (a, a)], *blocks, *vectors)


def pack_dqkv(dqs, dkvs, others, cos_t, sin_t, place, seq_block):
    seqs = len(dqs)
    length, cols = dqs[0].shape
    half = HEAD_DIM // 2
    wide = cols + 2 * HEAD_DIM

    def body(p, cos_ref, sin_ref, *refs):
        o_ref = refs[-1]
        for s in range(seqs):

            @pl.when(pl.program_id(0) == s)
            def _():
                kv = refs[seqs + s][...]
                if others:
                    kv = kv + refs[2 * seqs + s][...].astype(F32)
                c, e = kv[:half], kv[half:HEAD_DIM]
                cos, sin = cos_ref[0], sin_ref[0]
                kv = jnp.concatenate([c * cos + e * sin, e * cos - c * sin, kv[HEAD_DIM:]], 0)
                o_ref[:, :cols] = refs[s][...]
                o_ref[:, cols:] = kv.T.astype(BF16)

    const = lambda i, p: (0, 0)
    return call(
        body,
        (seqs,),
        [pl.BlockSpec((1, half, length), lambda i, p: (i, 0, 0))] * 2
        + [pl.BlockSpec((length, cols), const)] * seqs
        + [
            pl.BlockSpec((2 * HEAD_DIM, length), lambda i, p: (0, p[1] if seq_block else 0))
        ]
        * seqs
        + [pl.BlockSpec((2 * HEAD_DIM, length), const)] * len(others),
        pl.BlockSpec((length, wide), lambda i, p: (i, 0)),
        jax.ShapeDtypeStruct((seqs * length, wide), BF16),
        scalars=1,
    )(place, cos_t, sin_t, *dqs, *dkvs, *others)


def add_pair(a, b):
    rows, cols = a.shape
    block = rows // 4

    def body(a_ref, b_ref, o_ref):
        o_ref[...] = (a_ref[...].astype(F32) + b_ref[...].astype(F32)).astype(BF16)

    spec = pl.BlockSpec((block, cols), lambda i: (i, 0))
    return call(body, (4,), [spec, spec], spec, jax.ShapeDtypeStruct((rows, cols), BF16))(a, b)


def place_rows(a, b, middle, at, rows, before):
    count, cols = a.shape
    block = 128

    def body(p, a_ref, b_ref, *refs):
        o_ref = refs[-1]

        @pl.when(p[0] == 1)
        def _():
            o_ref[...] = a_ref[...].astype(F32)

        @pl.when(p[0] == 0)
        def _():
            o_ref[...] = b_ref[...].astype(F32)

    return call(
        body,
        (count // block,),
        [pl.BlockSpec((block, cols), lambda i, p: (i, 0))] * 2
        + [pl.BlockSpec(memory_space=pl.ANY)] * len(before),
        pl.BlockSpec((block, cols), lambda i, p: (at // block + i, 0)),
        jax.ShapeDtypeStruct((rows, cols), F32),
        scalars=1,
        alias={3 + k: k for k in range(len(before))},
    )(middle, a, b, *before)


def spread_gate_up(w, place, blocks, apart, before):
    rows, _, ff = w.shape
    block = min(128, rows)
    steps = rows // block if blocks is None else len(blocks)

    def body(p, w_ref, *refs):
        outs = refs[len(before) :]
        for j in range(ff // 128):
            for g in range(2):
                outs[0][:, 256 * j + 128 * g : 256 * j + 128 * (g + 1)] = w_ref[
                    :, g, 128 * j : 128 * (j + 1)
                ]
        if apart:
            outs[1][...] = outs[0][...]

    def row(i, p):
        if blocks is None:
            return i
        r = blocks[0](p)
        for k in range(1, steps):
            r = jnp.where(i == k, blocks[k](p), r)
        return r

    return call(
        body,
        (steps,),
        [pl.BlockSpec((block, 2, ff), lambda i, p: (row(i, p), 0, 0))]
        + [pl.BlockSpec(memory_space=pl.ANY)] * len(before),
        [pl.BlockSpec((block, 2 * ff), lambda i, p: (row(i, p), 0))]
        + [pl.BlockSpec((block, 2 * ff), lambda i, p: (i, 0))] * apart,
        [jax.ShapeDtypeStruct((rows, 2 * ff), BF16)]
        + [jax.ShapeDtypeStruct((steps * block, 2 * ff), BF16)] * apart,
        scalars=1,
        alias={2 + k: k for k in range(len(before))},
    )(place, w, *before)


def gate_up(pieces, parts, place):
    quarter, width = pieces[0].shape
    count = len(pieces)
    rows = count * quarter
    own, rest = parts[0].array, parts[1:]
    depth = own.shape[0]
    ff = own.shape[1] // 2
    tile = 128

    def body(p, *refs):
        own_ref, *rest_refs = refs[count : count + len(parts)]
        n_ref, act_ref, gu_ref, w_ref = refs[count + len(parts) :]

        @pl.when(pl.program_id(0) == 0)
        def _():
            for k in range(count):
                n_ref[k * quarter : (k + 1) * quarter] = refs[k][...]

        gu = dot(n_ref[:, :depth], own_ref[...])
        if rest:
            for part, ref in zip(rest, rest_refs):
                size = part.array.shape[0]
                at = pl.multiple_of(part.start(width, p[2]) - depth, 128)
                w_ref[pl.ds(at, size), :] = ref[...]
            gu = gu + dot(n_ref[:, depth:], w_ref[...])
        gate, up = gu[:, :tile], gu[:, tile:]
        sig = 1.0 / (1.0 + jnp.exp2(gate * (-LOG2E)))
        act_ref[...] = (gate * sig * up).astype(BF16)
        gu_ref[...] = gu.astype(BF16)

    return call(
        body,
        (ff // tile,),
        [pl.BlockSpec((quarter, width), lambda j, p: (0, 0), pipeline_mode=pl.Buffered(1))] * count
        + [pl.BlockSpec((x.array.shape[0], 2 * tile), lambda j, p: (0, j)) for x in parts],
        [
            pl.BlockSpec((rows, width), lambda j, p: (0, 0)),
            pl.BlockSpec((rows, tile), lambda j, p: (0, j)),
            pl.BlockSpec((rows, 2 * tile), lambda j, p: (0, j)),
        ],
        [
            jax.ShapeDtypeStruct((rows, width), BF16),
            jax.ShapeDtypeStruct((rows, ff), BF16),
            jax.ShapeDtypeStruct((rows, 2 * ff), BF16),
        ],
        scratch=[pltpu.VMEM((max(width - depth, 8), 2 * tile), BF16)],
        scalars=1,
        vmem=30,
    )(place, *pieces, *[x.array for x in parts])


def gate_back(dhb, parts, gu, place):
    rows, width = dhb.shape
    ff = parts[0].array.shape[0]
    tile = 256

    def body(p, d_ref, gu_ref, *refs):
        o_ref = refs[-1]
        d_act = 0.0
        for part, ref in zip(parts, refs):
            at = part.start(width, p[2])
            if part.late is not None:
                at = pl.multiple_of(at, 128)
            d_act = d_act + dot(d_ref[:, pl.ds(at, part.array.shape[1])], ref[...], 1, 1)
        for k in range(tile // 128):
            d = d_act[:, 128 * k : 128 * (k + 1)]
            gate = gu_ref[:, 256 * k : 256 * k + 128].astype(F32)
            up = gu_ref[:, 256 * k + 128 : 256 * (k + 1)].astype(F32)
            sig = 1.0 / (1.0 + jnp.exp2(gate * (-LOG2E)))
            o_ref[:, 256 * k : 256 * k + 128] = (
                d * up * sig * (1.0 + gate * (1.0 - sig))
            ).astype(BF16)
            o_ref[:, 256 * k + 128 : 256 * (k + 1)] = (d * gate * sig).astype(BF16)

    return call(
        body,
        (pl.cdiv(ff, tile),),
        [
            pl.BlockSpec((rows, width), lambda j, p: (0, 0)),
            pl.BlockSpec((rows, 2 * tile), lambda j, p: (0, j)),
        ]
        + [pl.BlockSpec((tile, x.array.shape[1]), lambda j, p: (j, 0)) for x in parts],
        pl.BlockSpec((rows, 2 * tile), lambda j, p: (0, j)),
        jax.ShapeDtypeStruct((rows, 2 * ff), BF16),
        scalars=1,
    )(place, dhb, gu, *[x.array for x in parts])


def split_matmul(a, parts, transposed, natural, place, seqs):
    rows, depth = a.shape
    axis = 0 if transposed else 1
    tile = 256
    counts = [x.array.shape[axis] // tile for x in parts]
    bases = [sum(counts[:k]) for k in range(len(parts))]
    cols = tile * sum(counts)
    length = rows // seqs
    quarter = length // 4

    def body(p, a_ref, *refs):
        w_refs, outs, acc = refs[: len(parts)], refs[len(parts) : -1], refs[-1]
        j = pl.program_id(0)
        for k, w_ref in enumerate(w_refs):

            @pl.when((j >= bases[k]) & (j < bases[k] + counts[k]))
            def _():
                acc[...] = dot(a_ref[...], w_ref[...], 1, 1 - axis)

        for s in range(seqs):
            send, keep = outs[2 * s], outs[2 * s + 1]
            for b in range(4):
                at = s * length + (b ^ p[0] if natural else b) * quarter
                part = acc[pl.ds(at, quarter), :]
                to = (b % 2) * quarter
                if b < 2:
                    keep[to : to + quarter] = part
                else:
                    send[to : to + quarter] = part.astype(BF16)

    def w_spec(k):
        def index(j, p):
            t = jnp.clip(j - bases[k], 0, counts[k] - 1)
            return (t, 0) if transposed else (0, t)

        shape = (tile, depth) if transposed else (depth, tile)
        once = {"pipeline_mode": pl.Buffered(1)} if counts[k] == 1 else {}
        return pl.BlockSpec(shape, index, **once)

    def column(j, p):
        c = j
        for k in range(1, len(parts)):
            at = parts[k].start(cols, p[2]) // tile + j - bases[k]
            c = jnp.where(j >= bases[k], at, c)
        return (0, c)

    return call(
        body,
        (sum(counts),),
        [pl.BlockSpec((rows, depth), lambda j, p: (0, 0), pipeline_mode=pl.Buffered(1))]
        + [w_spec(k) for k in range(len(parts))],
        [pl.BlockSpec((length // 2, tile), column)] * (2 * seqs),
        [
            jax.ShapeDtypeStruct((length // 2, cols), BF16),
            jax.ShapeDtypeStruct((length // 2, cols), F32),
        ]
        * seqs,
        scratch=[pltpu.VMEM((rows, tile), F32)],
        scalars=1,
    )(place, a, *[x.array for x in parts])


def full_matmul(a, parts, transposed, place, seqs, extras):
    rows, depth = a.shape
    axis = 0 if transposed else 1
    tile = 256
    counts = [x.array.shape[axis] // tile for x in parts]
    bases = [sum(counts[:k]) for k in range(len(parts))]
    cols = tile * sum(counts)
    length = rows // seqs
    quarter = length // 4

    def body(p, a_ref, *refs):
        w_refs, o_ref, acc = refs[: len(parts)], refs[-2], refs[-1]
        j = pl.program_id(0)
        for k, w_ref in enumerate(w_refs):

            @pl.when((j >= bases[k]) & (j < bases[k] + counts[k]))
            def _():
                acc[...] = dot(a_ref[...], w_ref[...], 1, 1 - axis)

        if not extras:
            o_ref[...] = acc[...].astype(BF16)
        for s in range(len(extras)):
            for b in range(4):
                part = acc[s * length + b * quarter : s * length + (b + 1) * quarter]
                if b == 0:
                    part = part + refs[len(parts) + s][...].astype(F32)
                at = pl.multiple_of(s * length + (b ^ p[0]) * quarter, quarter)
                o_ref[pl.ds(at, quarter), :] = part.astype(BF16)

    def w_spec(k):
        def index(j, p):
            t = jnp.clip(j - bases[k], 0, counts[k] - 1)
            return (t, 0) if transposed else (0, t)

        return pl.BlockSpec((tile, depth) if transposed else (depth, tile), index)

    def column(j, p):
        c = j
        for k in range(1, len(parts)):
            c = jnp.where(j >= bases[k], parts[k].start(cols, p[2]) // tile + j - bases[k], c)
        return (0, c)

    return call(
        body,
        (sum(counts),),
        [pl.BlockSpec((rows, depth), lambda j, p: (0, 0), pipeline_mode=pl.Buffered(1))]
        + [w_spec(k) for k in range(len(parts))]
        + [pl.BlockSpec((quarter, tile), column)] * len(extras),
        pl.BlockSpec((rows, tile), column),
        jax.ShapeDtypeStruct((rows, cols), BF16),
        scratch=[pltpu.VMEM((rows, tile), F32)],
        scalars=1,
    )(place, a, *[x.array for x in parts], *extras)


def put_columns(o_ref, x, swapped, half):
    @pl.when(swapped == 0)
    def _():
        o_ref[...] = x

    @pl.when(swapped == 1)
    def _():
        o_ref[:, :half] = x[:, half:]
        o_ref[:, half:] = x[:, :half]


def add_columns(x, delta, place, block):
    rows, width = x.shape
    half = width // 2

    def body(p, a_ref, b_ref, d_ref, o_ref):
        mine = jnp.concatenate([a_ref[...], b_ref[...]], 1) + d_ref[...].astype(F32)
        put_columns(o_ref, mine, p[1], half)

    return call(
        body,
        (rows // block,),
        [
            pl.BlockSpec((block, half), lambda i, p: (i, p[1])),
            pl.BlockSpec((block, half), lambda i, p: (i, 1 - p[1])),
            pl.BlockSpec((block, width), lambda i, p: (i, 0)),
        ],
        pl.BlockSpec((block, width), lambda i, p: (i, 0)),
        jax.ShapeDtypeStruct((rows, width), F32),
        scalars=1,
    )(place, x, x, delta)


def first_norm_back(x, upstream, d2, gain, place, block):
    rows, width = x.shape
    half = width // 2
    per = d2[0].shape[0] // block
    count = len(d2)

    def body(p, a_ref, b_ref, u_ref, g_ref, *refs):
        o_ref, sum_ref = refs[count:]
        i = pl.program_id(0)
        h = jnp.concatenate([a_ref[...], b_ref[...]], 1)
        inv = lax.rsqrt(jnp.mean(h * h, axis=-1, keepdims=True) + NORM_EPS)
        mine = u_ref[...].astype(F32)
        w = g_ref[...] * mine
        back = inv * w - h * (inv * inv * inv) * jnp.mean(w * h, axis=-1, keepdims=True)
        for s in range(count):

            @pl.when(i // per == s)
            def _():
                put_columns(o_ref, back + refs[s][...].astype(F32), p[1], half)

        total = jnp.sum(mine * h * inv, axis=0, keepdims=True)

        @pl.when(i == 0)
        def _():
            sum_ref[...] = total

        @pl.when(i > 0)
        def _():
            sum_ref[...] += total

    def spec(s):
        return pl.BlockSpec((block, width), lambda i, p: (jnp.clip(i - s * per, 0, per - 1), 0))

    return call(
        body,
        (rows // block,),
        [
            pl.BlockSpec((block, half), lambda i, p: (i, p[1])),
            pl.BlockSpec((block, half), lambda i, p: (i, 1 - p[1])),
            pl.BlockSpec((block, width), lambda i, p: (i, 0)),
            pl.BlockSpec((1, width), lambda i, p: (0, 0)),
        ]
        + [spec(s) for s in range(count)],
        [
            pl.BlockSpec((block, width), lambda i, p: (i, 0)),
            pl.BlockSpec((1, width), lambda i, p: (0, 0)),
        ],
        [jax.ShapeDtypeStruct((rows, width), F32), jax.ShapeDtypeStruct((1, width), F32)],
        scalars=1,
    )(place, x, x, upstream, gain, *d2)


def per_device(
    sizes, hidden_in, cotangent, w_qkv, w_out, w_gate_up, w_down, norm_gains, segments
):
    n_seq, n_tp, n_rep = sizes
    seqs, length, width = hidden_in.shape
    total = segments.shape[1]
    qkv_width = w_qkv.shape[3]
    group = qkv_width // HEAD_DIM - 2
    ff = w_down.shape[1]
    rows = seqs * length
    scale = float(HEAD_DIM) ** (-0.5)
    two = n_seq == 2
    si = lax.axis_index("seq")
    ti = lax.axis_index("tp")
    zi = lax.axis_index("rep")
    core, yi = ti % 2, ti // 2
    half = width // 2
    fourth = width // 4
    quarter = length // 4
    own = core * 2 + yi
    col_swap = si if two else jnp.int32(0) * si
    pz = zi % 2
    place = jnp.stack([own, col_swap, pz]).astype(jnp.int32)
    middle = (zi == 1) | (zi == 2)
    mid_flag = jnp.reshape(middle, (1,)).astype(jnp.int32)
    order = Order()

    def swap_seq(x):
        return lax.ppermute(x, "seq", [(0, 1), (1, 0)])

    def swap_core(x):
        return lax.ppermute(x, "tp", [(0, 1), (1, 0), (2, 3), (3, 2)])

    def swap_y(x):
        return lax.ppermute(x, "tp", [(0, 2), (2, 0), (1, 3), (3, 1)])

    def swap_z(x):
        return lax.ppermute(x, "rep", [(0, 1), (1, 0), (2, 3), (3, 2)])

    def hop_in(x):
        return lax.ppermute(x, "rep", [(0, 1), (3, 2)])

    def hop_mid(x):
        return lax.ppermute(x, "rep", [(1, 2), (2, 1)])

    def hop_out(x):
        return lax.ppermute(x, "rep", [(1, 0), (2, 3)])

    def whole(shard, axis):
        return lax.all_gather(shard, "seq", axis=axis, tiled=True)

    def now(*xs):
        return lax.optimization_barrier((xs, order.last))[0]

    def share(x):
        far = swap_y(x)
        return [x, far, swap_core(x), swap_core(far)]

    wq, wo, wd, wg = w_qkv[0, :, 0, :], w_out[0], w_down[0], w_gate_up[0]
    if two:
        gains = jnp.concatenate([norm_gains[0], swap_seq(norm_gains[0])], 1).astype(F32)
        qkv_parts = [Part(wq), Part(swap_seq(wq), half)]
        out_x = swap_seq(lax.dynamic_slice_in_dim(wo, pz * fourth, fourth, 1))
        gu_own, gu_a = order(
            lambda w, p: spread_gate_up(w, p, [lambda p: 4 * p[2]], 1, []), wg, place
        )
    else:
        gains = whole(norm_gains[0], 1).astype(F32)
        qkv_parts, out_parts = [Part(whole(wq, 0))], [Part(whole(wo, 1))]
        down_parts = [Part(whole(wd, 1))]
        gu_parts = [Part(spread_gate_up(whole(wg, 0), place, None, 0, [])[0])]

    first_row = si * length
    ids = jnp.arange(total, dtype=jnp.int32)
    change = jnp.concatenate(
        [jnp.ones((seqs, 1), bool), segments[:, 1:] != segments[:, :-1]], axis=1
    )
    doc_start = lax.cummax(jnp.where(change, ids[None, :], 0), axis=1)
    starts = lax.dynamic_slice_in_dim(doc_start, first_row, length, 1)
    pos = first_row + jnp.arange(length, dtype=jnp.int32)[None, :] - starts
    inverse_freq = ROPE_THETA ** (-(jnp.arange(HEAD_DIM // 2, dtype=F32) / (HEAD_DIM // 2)))
    angles = inverse_freq[None, :, None] * pos.astype(F32)[:, None, :]
    cos_t, sin_t = jnp.cos(angles), jnp.sin(angles)
    starts3 = starts[:, None, :]
    tq, tk = min(256, length), min(256, total)
    tiles = jnp.arange(length // tq, dtype=jnp.int32)
    ends = (first_row + (tiles + 1) * tq + tk - 1) // tk
    bounds = [
        jnp.concatenate(
            [
                jnp.stack([first_row, pz]),
                jnp.stack([starts[s, ::tq] // tk, ends], axis=1).reshape(-1),
            ]
        ).astype(jnp.int32)
        for s in range(seqs)
    ]

    hidden = hidden_in.reshape(rows, width)
    d_hidden = cotangent.reshape(rows, width)
    late_blocks = [lambda p, k=k: 4 * (1 - p[2]) + k for k in (0, 2, 3)]
    normed1 = order(lambda h, g, p: first_norm(h, g, p, 2 * quarter), hidden, gains[:1], place)
    if two:
        gu_own = order(lambda w, p, b: spread_gate_up(w, p, late_blocks, 0, [b]), wg, place, gu_own)[0]
    dhb = order(lambda d, p: local_cast(d, p, quarter), d_hidden, place)
    q_t, kv_t = order(
        lambda n, w, c, s: project_qkv(n, w, c, s, group),
        normed1, [x.array for x in qkv_parts], cos_t, sin_t,
    )
    if two:
        kv_got = lax.ppermute(kv_t, "seq", [(0, 1)])
        gu_x = [swap_seq(*now(gu_a))]
        blocks_b = [lambda p, k=k: 4 * p[2] + k for k in (2, 3)]
        gu_own, gu_b = order(
            lambda w, p, b: spread_gate_up(w, p, blocks_b, 1, [b]), wg, place, gu_own
        )
        out_z = swap_z(*now(out_x))
        all_kv = order(join_kv, kv_t, kv_got, place)
        out_parts = [Part(wo), Part(out_x, 0, 0), Part(out_z, 0, 1)]
    else:
        all_kv = whole(kv_t, 2)

    att, att_t, lse = [None] * seqs, [None] * seqs, [None] * seqs
    hold, keep = [None] * seqs, [None] * seqs

    def attention(s):
        att[s], att_t[s], lse[s] = order(
            lambda q, kv, st, b, s=s: attend(s, q, kv, st, b, scale),
            q_t, all_kv, starts3, bounds[s],
        )

    def out_product(s):
        send, keep[s] = order(
            lambda a, w, p: split_matmul(a, w, False, True, p, 1), att[s], out_parts, place
        )
        hold[s] = swap_core(send)

    def summed(keep, hold, s):
        send, keep[s] = order(first_sum, keep[s], hold[s])
        hold[s] = swap_y(send)

    attention(0)
    if two:
        touch(order, gu_x[0])
        gu_z = [swap_z(*now(gu_x[0]))]
        gu_x += [swap_seq(*now(gu_b))]
    out_product(0)
    for s in range(1, seqs):
        attention(s)
        summed(keep, hold, s - 1)
        out_product(s)
    if two:
        blocks_c = [lambda p: 1, lambda p: 5]
        gu_own, gu_c = order(
            lambda w, p, b: spread_gate_up(w, p, blocks_c, 1, [b]), wg, place, gu_own
        )
        gu_c = [swap_seq(gu_c[k * 128 : (k + 1) * 128]) for k in range(2)]
        touch(order, gu_z[0])
    summed(keep, hold, seqs - 1)
    if two:
        touch(order, gu_x[1])
        gu_z += [swap_z(*now(gu_x[1]))]
        piece = fourth // 2
        down_send = order(
            lambda w: (
                lax.dynamic_slice_in_dim(w, pz * fourth, piece, 1),
                w[:, piece : 2 * piece],
                w[:, 3 * piece :],
            ),
            wd,
        )
    h2, n2, extra = [None] * seqs, [None] * seqs, [None] * seqs

    def second_norm(h, k, g, gain):
        x = h + k + g
        inv = lax.rsqrt(jnp.mean(x * x, axis=-1, keepdims=True) + NORM_EPS)
        return x, x * inv * gain, k + g

    for s in range(seqs):
        h2[s], mine, extra[s] = order(
            lambda h, k, g, gain, p, s=s: by_rows(
                second_norm, p, s, quarter, [h], [k, g], [gain], [F32, BF16, BF16]
            ),
            hidden, keep[s], hold[s], gains[1:], place,
        )
        n2[s] = share(mine)
        if two and s == 0:
            touch(order, gu_c[0])
            down_send = now(*down_send)
            down_x = swap_seq(down_send[0])
            down_c = [swap_seq(x) for x in down_send[1:]]
    if two:
        gu_parts = [Part(gu_own)]
        gu_parts += [Part(gu_x[k], k * 256, 0) for k in range(2)]
        gu_parts += [Part(gu_z[k], k * 256, 1) for k in range(2)]
        gu_parts += [Part(gu_c[k], half + k * fourth + 128) for k in range(2)]
        touch(order, down_x)
        down_z = swap_z(*now(down_x))
        down_parts = [Part(wd), Part(down_x, 0, 0), Part(down_z, 0, 1)]
        down_parts += [Part(down_c[k], half + k * fourth + piece) for k in range(2)]
    n2_all, act, gu = order(gate_up, [x for b in n2 for x in b], gu_parts, place)

    class Chunk:
        def __init__(self, finish):
            self.finish, self.stage = finish, 0

        def begin(self, make, *xs):
            self.make, self.xs = make, xs
            self.got = swap_seq(order(lambda *x: make(1, *x), *xs))

        def next(self):
            k = self.stage
            self.stage += 1
            assert k < 4
            if k == 0:
                self.sum = order(
                    lambda g, *x: (self.make(0, *x) + g.astype(F32)).astype(g.dtype),
                    self.got, *self.xs,
                )
            elif k < 3:
                self.sum = order(self.add, self.sum, self.got)
            else:
                self.finish(self.sum, self.got)
            if k < 3:
                self.got = (hop_in, hop_mid, hop_out)[k](self.sum)

        def add(self, a, b):
            return a + b if a.dtype == F32 else add_pair(a, b)

    chunks, results = {}, {}

    def begin(name, finish, make, *xs):
        if two:
            chunks[name] = Chunk(finish)
            chunks[name].begin(make, *xs)

    def go(*names):
        for name in names:
            if two:
                chunks[name].next()

    def into(name, writer):
        def finish(a, b):
            results[name] = [
                order(lambda a, b, m, r: writer(a, b, m, r), a, b, mid_flag, results.get(name, []))
            ]

        return finish

    def piece_of(x, k, at, size):
        return x[:, k * half + at : k * half + at + size]

    def tdot(a, b, k):
        x = dot(a, b, 0, 0)
        return x.astype(BF16) if k else x

    cuts = [0, 768, ff]
    gu_rows = [256, 256, 256, 128, 128]

    def begin_down(j):
        begin(
            f"d{j}",
            into("down", lambda a, b, m, r: place_rows(a, b, m, cuts[j], ff, r)),
            lambda k, a, d: tdot(a[:, cuts[j] : cuts[j + 1]], piece_of(d, k, 0, half), k),
            act, dhb,
        )

    def begin_gu(j):
        at = sum(gu_rows[:j])
        begin(
            f"g{j}",
            into("gu", lambda a, b, m, r: join_gate_up(a, b, m, at, half, r)),
            lambda k, n, d: tdot(piece_of(n, k, at, gu_rows[j]), d, k),
            n2_all, dgu,
        )

    begin_down(0)
    if two:

        def pair(a, c, first):
            return jnp.concatenate([a, jnp.where(first, c[0], c[1])])

        begin_down(1)
        pair_x = order(lambda a, c: pair(a, c, pz == 0), gu_x[0], gu_c)
        pair_z = order(lambda a, c: pair(a, c, pz == 1), gu_z[0], gu_c)
        gu_parts = [Part(gu_own), Part(pair_x, 0, 0), Part(gu_x[1], 256, 0)]
        gu_parts += [Part(pair_z, 0, 1), Part(gu_z[1], 256, 1)]
    dgu = order(gate_back, dhb, down_parts, gu, place)
    got = order(
        lambda a, w, p: split_matmul(a, w, True, False, p, seqs), dgu, gu_parts, place
    )
    keep, hold = list(got[1::2]), [swap_core(x) for x in got[::2]]
    go("d0")
    for s in range(seqs):
        summed(keep, hold, s)
    begin_gu(0)
    delta = order(
        lambda a, w, p, x: full_matmul(a, w, False, p, seqs, x), act, down_parts, place, extra
    )
    d2, gain2 = [None] * seqs, []

    def second_back(d, k, g, x, gain):
        mine = k + g
        inv = lax.rsqrt(jnp.mean(x * x, axis=-1, keepdims=True) + NORM_EPS)
        w = gain * mine
        back = inv * w - x * (inv * inv * inv) * jnp.mean(w * x, axis=-1, keepdims=True)
        return back + d, jnp.sum(mine * x * inv, axis=0, keepdims=True)

    for s in range(seqs):
        mine, g2 = order(
            lambda d, k, g, x, gain, p, s=s: by_rows(
                second_back, p, s, quarter, [d], [k, g, x], [gain], [BF16], 1
            ),
            d_hidden, keep[s], hold[s], h2[s], gains[1:], place,
        )
        gain2.append(g2)
        d2[s] = share(mine)
        if s == 0:
            go("d1")
    go("d0")
    dq, dkv, early = [None] * seqs, [None] * seqs, [None] * seqs
    dkv_got = []
    for s in range(seqs):
        d2[s] = order(stack, d2[s], place)
        dq[s], dkv[s], early[s] = order(
            lambda q, kv, st, b, a, w, *x, s=s: attend_back(s, q, kv, st, b, a, w, *x, scale),
            q_t, all_kv, starts3, bounds[s], att_t[s], out_parts, d2[s], lse[s], cos_t, sin_t,
        )
        if two:
            dkv_got.append(lax.ppermute(early[s], "seq", [(1, 0)]))
        if s == 0:
            go("g0")
    delta = lax.psum(lax.optimization_barrier((delta, d2[-1]))[0], "tp")
    begin(
        "out",
        into("out", lambda a, b, m, r: place_rows(a, b, m, 0, a.shape[0], r)),
        lambda k, a, d: sum(
            dot(x, piece_of(y, k, 0, half), 0, 0) for x, y in zip(a, d)
        ).astype(BF16 if k else F32),
        att, d2,
    )
    go("d0", "d1")
    if not two:
        dkv = [lax.psum_scatter(x, "seq", scatter_dimension=1, tiled=True) for x in dkv]
    d_qkv = order(
        lambda q, kv, g, c, s, p: pack_dqkv(q, kv, g, c, s, p, two),
        dq, dkv, dkv_got, cos_t, sin_t, place,
    )
    begin_gu(1)
    d_n1 = order(lambda a, w, p: full_matmul(a, w, True, p, seqs, []), d_qkv, qkv_parts, place)
    d_n1 = lax.psum(lax.optimization_barrier((d_n1, delta))[0], "tp")
    go("g0", "out")
    begin(
        "qkv",
        into("qkv", lambda a, b, m, r: place_rows(a, b, m, 0, half, r)),
        lambda k, n, d: tdot(piece_of(n, k, 0, half), d, k),
        normed1, d_qkv,
    )
    go("d1")
    gain2 = order(lambda g: sum(g), gain2)
    gain2 = order(lambda a, b: a + b, gain2, swap_core(gain2))
    gain2 = order(lambda a, b: a + b, gain2, swap_y(gain2))
    go("g1", "out", "g0")
    begin_gu(2)
    go("qkv", "g1", "d0")
    begin_gu(3)
    go("out", "g2", "qkv", "g0", "d1")
    begin_gu(4)
    go("g1", "g3", "g2", "qkv")
    hidden_out = order(lambda h, d, p: add_columns(h, d, p, quarter), hidden, delta, place)
    go("g4", "g3", "g2", "out")
    go("g4", "g3", "g1")
    grad_in, gain1 = order(
        lambda h, u, d, g, p: first_norm_back(h, u, d, g, p, quarter),
        hidden, d_n1, d2, gains[:1], place,
    )
    gain_sum = order(lambda a, b: jnp.concatenate([a, b]), gain1, gain2)

    def gain_finish(a, b):
        results["gain"] = [order(lambda a, b: jnp.where(middle, a, b), a, b)]

    begin("gain", gain_finish, lambda k, g: piece_of(g, k, 0, half), gain_sum)
    go("g4", "gain", "qkv", "gain", "g2", "gain", "g3", "g4", "gain")
    if two:
        g_qkv, g_out, g_down = results["qkv"][0], results["out"][0], results["down"][0]
        g_gu, gain_own = results["gu"][0], results["gain"][0]
    else:

        def reduce_rep(x):
            if n_rep != 4:
                return lax.psum(x.astype(F32), "rep").astype(BF16)
            x = x.astype(BF16)
            x = (x.astype(F32) + hop_in(x).astype(F32)).astype(BF16)
            x = (x.astype(F32) + hop_mid(x).astype(F32)).astype(BF16)
            return jnp.where(middle, x, hop_out(x))

        def reduce(x, axis):
            return reduce_rep(lax.psum_scatter(x, "seq", scatter_dimension=axis, tiled=True))

        g_down = reduce(dot(act, dhb, 0, 0), 1).astype(F32)
        g_out = reduce(sum(dot(x, y, 0, 0) for x, y in zip(att, d2)), 1).astype(F32)
        g_qkv = reduce(dot(normed1, d_qkv, 0, 0), 0).astype(F32)
        g_gu = reduce(dot(n2_all, dgu, 0, 0), 0)
        g_gu = join_gate_up(g_gu, g_gu, mid_flag, 0, g_gu.shape[0], [])
        gain_own = lax.psum_scatter(gain_sum, "seq", scatter_dimension=1, tiled=True)
        gain_own = lax.psum(gain_own, "rep")
    return (
        hidden_out.reshape(seqs, length, width),
        grad_in.reshape(seqs, length, width),
        g_qkv[None, :, None, :],
        g_out[None],
        g_gu,
        g_down[None],
        gain_own[None],
    )


def solution(mesh):
    in_specs = (
        P("rep", "seq", None),
        P("rep", "seq", None),
        P(None, "seq", "tp", None),
        P(None, "tp", "seq"),
        P(None, "seq", None, "tp"),
        P(None, "tp", "seq"),
        P(None, None, "seq"),
        P("rep", None),
    )
    out_specs = (
        P("rep", "seq", None),
        P("rep", "seq", None),
        P(None, "seq", "tp", None),
        P(None, "tp", "seq"),
        P(None, "seq", None, "tp"),
        P(None, "tp", "seq"),
        P(None, None, "seq"),
    )
    sizes = (mesh.shape["seq"], mesh.shape["tp"], mesh.shape["rep"])
    return jax.shard_map(
        functools.partial(per_device, sizes),
        mesh=mesh,
        in_specs=in_specs,
        out_specs=out_specs,
        check_vma=False,
    )
```

time: 803 us -> 671 us (0.84)
  waiting for transfers between devices: 237 us -> 144 us
  other arithmetic: 76.3 us -> 8.61 us
  Pallas kernels: 183 us -> 246 us
  local copies, waits for them, and re-layouts: 90.9 us -> 52.2 us
  matrix products: 66.6 us -> 49.3 us
  between operations: 3.29 us -> 16.5 us
  starting transfers between devices: 135 us -> 146 us
    ppermute x10, waiting for transfers between devices: 102 us -> 25 us  [hop_out(): return lax.ppermute(x, 'rep', [(1, 0), (2, 3)])]
    pallas_call x9 -> x43, Pallas kernels: 100 us -> 162 us  [the longest x18 36.5 us: add_pair(): call(body, (4,), [spec, spec], spec, jax.ShapeDtypeStruct((rows, cols), B...]
    ppermute x17 -> x9, waiting for transfers between devices: 55.1 us -> 12.2 us  [swap_y(): return lax.ppermute(x, 'tp', [(0, 2), (2, 0), (1, 3), (3, 1)])]
    convert_element_type x31 -> x1, other arithmetic: 43.2 us -> 3.12 us  [next(): (self.make(0, *x) + g.astype(F32)).astype(g.dtype)]
    psum x0 -> x2, waiting for transfers between devices: none -> 22.4 us  [the longest x1 22.4 us: per_device(): d_n1 = lax.psum(lax.optimization_barrier((d_n1, delta))[0], 'tp')]
    ppermute x8 -> x4, waiting for transfers between devices: 21.9 us -> 1.7 us  [swap_z(): return lax.ppermute(x, 'rep', [(0, 1), (1, 0), (2, 3), (3, 2)])]
    dot_general x22 -> x20, matrix products: 66.6 us -> 49.3 us  [dot(): lax.dot_general(a, b, (((ca,), (cb,)), ((), ())), preferred_element_type=...]
    dynamic_update_slice x12 -> x0, local copies, waits for them, and re-layouts: 14.4 us -> none  [the longest x8 9.62 us: put_gu(): lax.dynamic_update_slice(w, x, (half + parity * fourth + k * piece, 0))]
  transfers between devices with their start and end apart: 101 -> 81, of which waited for: 29 -> 25; matrix products, arithmetic and copies ran while one was open for 26% -> 10% of each run, Pallas kernels for 22% -> 36%
where the time goes in v2:
time: 671 us; the launch traced here: 663 us
  Pallas kernels  246 us (37%)
  starting transfers between devices  146 us (22%)
  waiting for transfers between devices  144 us (21%)
  local copies, waits for them, and re-layouts  52.2 us (8%)
  matrix products  49.3 us (7%)
  between operations  16.5 us (2%)
  other arithmetic  8.61 us (1%)
    ppermute x20, waiting for transfers between devices, swap_seq(): return lax.ppermute(x, 'seq', [(0, 1), (1, 0)])  57.6 us
    ppermute x10, starting transfers between devices, hop_in(): return lax.ppermute(x, 'rep', [(0, 1), (3, 2)])  56.6 us
    dot_general x20, matrix products, dot(): lax.dot_general(a, b, (((ca,), (cb,)), ((), ())), preferred_element_type=...  49.3 us
    unnamed x235, local copies, waits for them, and re-layouts  49 us
    ppermute x20, starting transfers between devices, swap_seq(): return lax.ppermute(x, 'seq', [(0, 1), (1, 0)])  40.6 us
    pallas_call x18, Pallas kernels, add_pair(): call(body, (4,), [spec, spec], spec, jax.ShapeDtypeStruct((rows, cols), B...  36.5 us
    pallas_call x3, Pallas kernels, split_matmul(): call(body, (sum(counts),), [pl.BlockSpec((rows, depth), lambda j, p: (0,...  29.6 us
    pallas_call x4, Pallas kernels, spread_gate_up(): call(body, (steps,), [pl.BlockSpec((block, 2, ff), lambda i, p: (row(i, p...  26.8 us
  transfers between devices with their start and end apart: 81, of which 25 were waited for; matrix products, arithmetic and copies ran while one was open for 10% of the time, Pallas kernels for 36%

profile of v2, /device:TPU:0, one launch (start us, length us, event | category | flops | bytes accessed | tf_op | source)
XLA Modules:
  0.0 663.1 jit_solution(1348728226845104868)
XLA Ops:
  26.0 6.5 shard_map.137.refs_0_
  34.4 7.7 %collective-permute-done.1.refs_1_ = bf16[1024,640]{1,0:T(8,128)(2,1)S(1)} collective-permute-done((bf16[1024,640]{1,0:T(8,128)(2,1)}, bf16[1024,640]{1,0:T(8,128)(2,1)S(1)}, u32[]{:S(2)}, u32[]{:S(2)}) %collective-permute-start.1) | collective-permute-done | bytes 1310752 | tf_op jit(solution)/shard_map/ppermute | solution.py:927
  42.2 4.4 shard_map.139
  48.9 8.4 %shard_map.140 = (bf16[1024,2816]{1,0:T(8,128)(2,1)S(1)}, bf16[256,2816]{1,0:T(8,128)(2,1)}) custom-call(s32[3]{0:T(128)S(1)} %pad_add_fusion.2.p, bf16[1024,2,1408]{2,1,0:T(2,128)(2,1)S(1)} %bitcast.98, bf16[1024,2816]{1,0:T(8,128)(2,1)S(1)} %shard_map.137.refs_0_), custom_call_target="tpu_custom_call", output_to_operand_aliasing={{0}: (2, {})} | custom-call | flops 3000000000 | bytes 8000000 | tf_op jit(solution)/shard_map/pallas_call | solution.py:595
  60.2 7.8 %shard_map.142 = (bf16[512,512]{1,0:T(8,128)(2,1)S(1)}, bf16[512,512]{1,0:T(8,128)(2,1)S(1)}, f32[8,512]{1,0:T(8,128)S(1)}) custom-call(s32[6]{0:T(128)S(1)} %pad_add_fusion.3.b_ref, bf16[2,512,512]{2,1,0:T(8,128)(2,1)S(1)} %get-tuple-element.589.q_ref, bf16[2,128,1024]{2,1,0:T(8,128)(2,1)S(1)} %shard_map.141.kv_ref, s32[2,1,512]{2,1,0:T(1,128)S(1)} %broadcast_in_dim.33.st_ref), custom_call_target="tpu_custom_call" | custom-call | flops 3000000000 | bytes 8000000 | tf_op jit(solution)/shard_map/pallas_call | solution.py:250
  70.9 5.2 shard_map.143
  83.6 7.8 %shard_map.144 = (bf16[512,512]{1,0:T(8,128)(2,1)S(1)}, bf16[512,512]{1,0:T(8,128)(2,1)S(1)}, f32[8,512]{1,0:T(8,128)S(1)}) custom-call(s32[6]{0:T(128)S(1)} %pad_add_fusion.5.b_ref, bf16[2,512,512]{2,1,0:T(8,128)(2,1)S(1)} %copy-done.81, bf16[2,128,1024]{2,1,0:T(8,128)(2,1)S(1)} %copy-done.86, s32[2,1,512]{2,1,0:T(1,128)S(1)} %broadcast_in_dim.33.st_ref), custom_call_target="tpu_custom_call" | custom-call | flops 3000000000 | bytes 8000000 | tf_op jit(solution)/shard_map/pallas_call | solution.py:250
  93.5 4.5 shard_map.146
  100.6 7.9 %shard_map.147 = (bf16[1024,2816]{1,0:T(8,128)(2,1)S(1)}, bf16[256,2816]{1,0:T(8,128)(2,1)S(1)}) custom-call(s32[3]{0:T(128)S(1)} %pad_add_fusion.2.p, bf16[1024,2,1408]{2,1,0:T(2,128)(2,1)S(1)} %bitcast.101, bf16[1024,2816]{1,0:T(8,128)(2,1)S(1)} %bitcast.91), custom_call_target="tpu_custom_call", output_to_operand_aliasing={{0}: (2, {})} | custom-call | flops 3000000000 | bytes 8000000 | tf_op jit(solution)/shard_map/pallas_call | solution.py:595
  111.1 4.8 collective-permute-start.15
  117.7 4.5 collective-permute-start.20
  143.6 4.7 collective-permute-done.20.refs_14_
  149.7 13.0 %collective-permute-done.21.refs_1_ = bf16[1408,256]{1,0:T(8,128)(2,1)} collective-permute-done((bf16[1408,256]{1,0:T(8,128)(2,1)S(1)}, bf16[1408,256]{1,0:T(8,128)(2,1)}, u32[]{:S(2)}, u32[]{:S(2)}) %collective-permute-start.21) | collective-permute-done | bytes 720928 | tf_op jit(solution)/shard_map/ppermute | solution.py:927
  170.1 18.9 %shard_map.151 = (bf16[1024,2048]{1,0:T(8,128)(2,1)S(1)}, bf16[1024,1408]{1,0:T(8,128)(2,1)S(1)}, bf16[1024,2816]{1,0:T(8,128)(2,1)S(1)}) custom-call(s32[3]{0:T(128)S(1)} %pad_add_fusion.2.p, bf16[128,2048]{1,0:T(8,128)(2,1)} %get-tuple-element.466.refs_0_, bf16[128,2048]{1,0:T(8,128)(2,1)} %collective-permute-done.11.refs_1_, ...), custom_call_target="tpu_custom_call" | custom-call | flops 3000000000 | bytes 8000000 | tf_op jit(solution)/shard_map/pallas_call | solution.py:639
  200.0 12.1 %shard_map.152.a_ref = bf16[1024,2816]{1,0:T(8,128)(2,1)S(1)} custom-call(s32[3]{0:T(128)S(1)} %pad_add_fusion.2.p, bf16[1024,2048]{1,0:T(8,128)(2,1)S(1)} %copy-done.12, bf16[1024,2816]{1,0:T(8,128)(2,1)S(1)} %copy-done.24, bf16[1408,1024]{1,0:T(8,128)(2,1)S(1)} %bitcast.103, bf16[1408,256]{1,0:T(8,128)(2,1)} %collective-permute-done.21.refs_1_, ...), custom_call_target="tpu_custom_call" | custom-call | flops 3000000000 | bytes 8000000 | tf_op jit(solution)/shard_map/pallas_call | solution.py:683
  212.2 19.9 %shard_map.153 = (bf16[256,2048]{1,0:T(8,128)(2,1)S(1)}, f32[256,2048]{1,0:T(8,128)S(1)}, bf16[256,2048]{1,0:T(8,128)(2,1)S(1)}, f32[256,2048]{1,0:T(8,128)S(1)}) custom-call(s32[3]{0:T(128)S(1)} %pad_add_fusion.2.p, bf16[1024,2816]{1,0:T(8,128)(2,1)S(1)} %shard_map.152.a_ref, bf16[1024,2816]{1,0:T(8,128)(2,1)S(1)} %bitcast.93, ...), custom_call_target="tpu_custom_call" | custom-call | flops 3000000000 | bytes 8000000 | tf_op jit(solution)/shard_map/pallas_call | solution.py:743
  233.0 4.4 add_convert_fusion.a_ref
  252.3 12.1 %shard_map.156 = bf16[1024,2048]{1,0:T(8,128)(2,1)S(1)} custom-call(s32[3]{0:T(128)S(1)} %pad_add_fusion.2.p, bf16[1024,1408]{1,0:T(8,128)(2,1)S(1)} %get-tuple-element.546.a_ref, bf16[1408,1024]{1,0:T(8,128)(2,1)S(1)} %bitcast.104, bf16[1408,256]{1,0:T(8,128)(2,1)} %collective-permute-done.21.refs_1_, bf16[1408,256]{1,0:T(8,128)(2,1)} %collective-permute-done.22.refs_2_, ...), custom_call_target="tpu_custom_call" | custom-call | flops 3000000000 | bytes 8000000 | tf_op jit(solution)/shard_map/pallas_call | solution.py:801
  292.4 7.2 %collective-permute-done.31.refs_1_ = bf16[128,2048]{1,0:T(8,128)(2,1)S(1)} collective-permute-done((bf16[128,2048]{1,0:T(8,128)(2,1)S(1)}, bf16[128,2048]{1,0:T(8,128)(2,1)S(1)}, u32[]{:S(2)}, u32[]{:S(2)}) %collective-permute-start.31) | collective-permute-done | bytes 524320 | tf_op jit(solution)/shard_map/ppermute | solution.py:933
  302.9 9.2 %shard_map.161 = (bf16[512,512]{1,0:T(8,128)(2,1)S(1)}, f32[128,1024]{1,0:T(8,128)S(1)}, bf16[128,512]{1,0:T(8,128)(2,1)S(1)}) custom-call(s32[6]{0:T(128)S(1)} %copy-done.61, bf16[2,512,512]{2,1,0:T(8,128)(2,1)S(1)} %copy-done.82, bf16[2,128,1024]{2,1,0:T(8,128)(2,1)S(1)} %copy-done.87, s32[2,1,512]{2,1,0:T(1,128)S(1)} %broadcast_in_dim.33.st_ref, ...), custom_call_target="tpu_custom_call" | custom-call | flops 3000000000 | bytes 8000000 | tf_op jit(solution)/shard_map/pallas_call | solution.py:347
  313.9 4.4 fusion.a_ref
  318.2 5.2 collective-permute-start.44
  324.4 9.3 %shard_map.163 = (bf16[512,512]{1,0:T(8,128)(2,1)S(1)}, f32[128,1024]{1,0:T(8,128)S(1)}, bf16[128,512]{1,0:T(8,128)(2,1)S(1)}) custom-call(s32[6]{0:T(128)S(1)} %copy-done.63, bf16[2,512,512]{2,1,0:T(8,128)(2,1)S(1)} %copy-done.82, bf16[2,128,1024]{2,1,0:T(8,128)(2,1)S(1)} %copy-done.87, s32[2,1,512]{2,1,0:T(1,128)S(1)} %broadcast_in_dim.33.st_ref, ...), custom_call_target="tpu_custom_call" | custom-call | flops 3000000000 | bytes 8000000 | tf_op jit(solution)/shard_map/pallas_call | solution.py:347
  337.6 7.0 %collective-permute-start.43 = (bf16[512,1024]{1,0:T(8,128)(2,1)}, bf16[512,1024]{1,0:T(8,128)(2,1)}, u32[]{:S(2)}, u32[]{:S(2)}) collective-permute-start(bf16[512,1024]{1,0:T(8,128)(2,1)} %add_convert_fusion.4), channel_id=1, source_target_pairs={{0,4},{4,0},{1,5},{5,1},{2,6},{6,2},{3,7},{7,3},{8,12},{12,8},{9,1... | collective-permute-start | bytes 3145736 | tf_op jit(solution)/shard_map/ppermute | solution.py:927
  349.6 4.4 convolution_convert_fusion.1
  354.0 6.5 shard_map.167
  389.7 10.0 %collective-permute-done.48 = bf16[256,2816]{1,0:T(8,128)(2,1)} collective-permute-done((bf16[256,2816]{1,0:T(8,128)(2,1)}, bf16[256,2816]{1,0:T(8,128)(2,1)}, u32[]{:S(2)}, u32[]{:S(2)}) %collective-permute-start.48) | collective-permute-done | bytes 1441824 | tf_op jit(solution)/shard_map/ppermute | solution.py:927
  401.0 5.0 fusion.1.a_ref
  406.0 4.7 collective-permute-start.56
  419.2 7.8 %collective-permute-done.45 = bf16[1024,640]{1,0:T(8,128)(2,1)S(1)} collective-permute-done((bf16[1024,640]{1,0:T(8,128)(2,1)}, bf16[1024,640]{1,0:T(8,128)(2,1)S(1)}, u32[]{:S(2)}, u32[]{:S(2)}) %collective-permute-start.45) | collective-permute-done | bytes 1310752 | tf_op jit(solution)/shard_map/ppermute | solution.py:927
  430.6 9.5 %collective-permute-done.56.b_ref = bf16[256,2816]{1,0:T(8,128)(2,1)S(1)} collective-permute-done((bf16[256,2816]{1,0:T(8,128)(2,1)S(1)}, bf16[256,2816]{1,0:T(8,128)(2,1)S(1)}, u32[]{:S(2)}, u32[]{:S(2)}) %collective-permute-start.56) | collective-permute-done | bytes 1441824 | tf_op jit(solution)/shard_map/ppermute | solution.py:939
  440.1 4.5 collective-permute-start.52
  451.6 9.9 %collective-permute-done.53 = bf16[256,2816]{1,0:T(8,128)(2,1)S(1)} collective-permute-done((bf16[256,2816]{1,0:T(8,128)(2,1)S(1)}, bf16[256,2816]{1,0:T(8,128)(2,1)S(1)}, u32[]{:S(2)}, u32[]{:S(2)}) %collective-permute-start.53) | collective-permute-done | bytes 1441824 | tf_op jit(solution)/shard_map/ppermute | solution.py:927
  464.1 6.3 collective-permute-done.52.b_ref
  470.4 4.7 collective-permute-start.58
  476.8 7.8 %collective-permute-done.62.b_ref = bf16[256,2816]{1,0:T(8,128)(2,1)S(1)} collective-permute-done((bf16[256,2816]{1,0:T(8,128)(2,1)S(1)}, bf16[256,2816]{1,0:T(8,128)(2,1)S(1)}, u32[]{:S(2)}, u32[]{:S(2)}) %collective-permute-start.62) | collective-permute-done | bytes 1441824 | tf_op jit(solution)/shard_map/ppermute | solution.py:945
  496.9 5.7 collective-permute-done.58.b_ref
  508.8 17.9 %collective-permute-start.64 = (bf16[128,2816]{1,0:T(8,128)(2,1)}, bf16[128,2816]{1,0:T(8,128)(2,1)S(1)}, u32[]{:S(2)}, u32[]{:S(2)}) collective-permute-start(bf16[128,2816]{1,0:T(8,128)(2,1)} %fusion.3.a_ref), channel_id=1, source_target_pairs={{0,8},{24,16},{1,9},{25,17},{2,10},{26,18},{3,11},{27,19},{4,12},{... | collective-permute-start | bytes 2162696 | tf_op jit(solution)/shard_map/ppermute | solution.py:939
  526.8 5.0 shard_map.180.a_ref
  535.2 5.9 shard_map.181
  544.8 5.6 collective-permute-start.67
  569.6 22.4 %all-reduce.6.cloned.1.call-done.u_ref = bf16[1024,2048]{1,0:T(8,128)(2,1)} async-done(((bf16[1024,2048]{1,0:T(8,128)(2,1)}), bf16[1024,2048]{1,0:T(8,128)(2,1)}) %all-reduce.6.cloned.1.call-update) | async-done | bytes 4194320 | tf_op jit(solution)/shard_map/psum | solution.py:1248
  599.2 9.0 %shard_map.188 = (f32[1024,2048]{1,0:T(8,128)}, f32[1,2048]{1,0:T(1,128)S(1)}) custom-call(s32[3]{0:T(128)S(1)} %pad_add_fusion.2.p, f32[1024,2048]{1,0:T(8,128)S(1)} %bitcast.80, f32[1024,2048]{1,0:T(8,128)S(1)} %bitcast.81, bf16[1024,2048]{1,0:T(8,128)(2,1)S(1)} %copy-done.25, f32[1,2048]{1,0:T(1,128)S(1)} %copy-done.57, ...), custom_call_target="tpu_custom_call" | custom-call | flops 3000000000 | bytes 8000000 | tf_op jit(solution)/shard_map/pallas_call | solution.py:880
  613.5 4.8 collective-permute-start.76
  618.3 4.4 shard_map.190
  622.7 4.2 copy.28
  632.9 8.5 %collective-permute-done.74.b_ref = bf16[128,2816]{1,0:T(8,128)(2,1)} collective-permute-done((bf16[128,2816]{1,0:T(8,128)(2,1)}, bf16[128,2816]{1,0:T(8,128)(2,1)}, u32[]{:S(2)}, u32[]{:S(2)}) %collective-permute-start.74) | collective-permute-done | bytes 720928 | tf_op jit(solution)/shard_map/ppermute | solution.py:945
  644.7 8.6 %collective-permute-done.73.b_ref = bf16[128,2816]{1,0:T(8,128)(2,1)S(1)} collective-permute-done((bf16[128,2816]{1,0:T(8,128)(2,1)S(1)}, bf16[128,2816]{1,0:T(8,128)(2,1)S(1)}, u32[]{:S(2)}, u32[]{:S(2)}) %collective-permute-start.73) | collective-permute-done | bytes 720928 | tf_op jit(solution)/shard_map/ppermute | solution.py:945
  (481 shorter events, 266.5 us)
Async XLA Ops:
  7.2 499.0 %all-reduce.4.cloned.1.call-start = ((), (), s32[]{:S(2)}) async-start(), calls=%async_computation | async-start | bytes 8388608 | tf_op jit(solution)/shard_map/psum | solution.py:1230
  10.2 31.9 %collective-permute-start.1 = (bf16[1024,640]{1,0:T(8,128)(2,1)}, bf16[1024,640]{1,0:T(8,128)(2,1)S(1)}, u32[]{:S(2)}, u32[]{:S(2)}) collective-permute-start(bf16[1024,640]{1,0:T(8,128)(2,1)} %bitcast.110), channel_id=1, source_target_pairs={{0,4},{4,0},{1,5},{5,1},{2,6},{6,2},{3,7},{7,3},{8,12},{12,8},{9,1... | collective-permute-start | bytes 3932168 | tf_op jit(solution)/shard_map/ppermute | solution.py:927
  11.4 45.9 %collective-permute-start.3 = (bf16[512,512]{1,0:T(8,128)(2,1)S(1)}, bf16[512,512]{1,0:T(8,128)(2,1)S(1)}, u32[]{:S(2)}, u32[]{:S(2)}) collective-permute-start(bf16[512,512]{1,0:T(8,128)(2,1)S(1)} %dynamic-slice_bitcast_fusion), channel_id=1, source_target_pairs={{0,4},{4,0},{1,5},{5,1},{2,6},{6,2},{3,7},{7,3},{8,12},{12,8},{9,1... | collective-permute-start | bytes 1572872 | tf_op jit(solution)/shard_map/ppermute | solution.py:927
  77.7 46.8 %collective-permute-start.10 = (bf16[256,2816]{1,0:T(8,128)(2,1)}, bf16[256,2816]{1,0:T(8,128)(2,1)}, u32[]{:S(2)}, u32[]{:S(2)}) collective-permute-start(bf16[256,2816]{1,0:T(8,128)(2,1)} %get-tuple-element.445), channel_id=1, source_target_pairs={{0,4},{4,0},{1,5},{5,1},{2,6},{6,2},{3,7},{7,3},{8,12},{12,8},{9,1... | collective-permute-start | bytes 4325384 | tf_op jit(solution)/shard_map/ppermute | solution.py:927
  99.0 26.8 %collective-permute-start.7 = (bf16[128,2048]{1,0:T(8,128)(2,1)S(1)}, bf16[128,2048]{1,0:T(8,128)(2,1)S(1)}, u32[]{:S(2)}, u32[]{:S(2)}) collective-permute-start(bf16[128,2048]{1,0:T(8,128)(2,1)S(1)} %get-tuple-element.427), channel_id=1, source_target_pairs={{0,2},{2,0},{1,3},{3,1},{4,6},{6,4},{5,7},{7,5},{8,10},{10,8},{9,1... | collective-permute-start | bytes 1572872 | tf_op jit(solution)/shard_map/ppermute | solution.py:933
  117.7 30.7 %collective-permute-start.20 = (bf16[128,2816]{1,0:T(8,128)(2,1)S(1)}, bf16[128,2816]{1,0:T(8,128)(2,1)S(1)}, u32[]{:S(2)}, u32[]{:S(2)}) collective-permute-start(bf16[128,2816]{1,0:T(8,128)(2,1)S(1)} %get-tuple-element.764), channel_id=1, source_target_pairs={{0,4},{4,0},{1,5},{5,1},{2,6},{6,2},{3,7},{7,3},{8,12},{12,8},{9,1... | collective-permute-start | bytes 2162696 | tf_op jit(solution)/shard_map/ppermute | solution.py:927
  125.8 40.9 %collective-permute-start.19 = (bf16[256,2816]{1,0:T(8,128)(2,1)}, bf16[256,2816]{1,0:T(8,128)(2,1)}, u32[]{:S(2)}, u32[]{:S(2)}) collective-permute-start(bf16[256,2816]{1,0:T(8,128)(2,1)} %collective-permute-done.10.refs_10_.refs_2_), channel_id=1, source_target_pairs={{0,8},{8,0},{16,24},{24,16},{1,9},{9,1},{17,25},{25,17},{2,10},{10... | collective-permute-start | bytes 4325384 | tf_op jit(solution)/shard_map/ppermute | solution.py:936
  132.9 29.8 %collective-permute-start.21 = (bf16[1408,256]{1,0:T(8,128)(2,1)S(1)}, bf16[1408,256]{1,0:T(8,128)(2,1)}, u32[]{:S(2)}, u32[]{:S(2)}) collective-permute-start(bf16[1408,256]{1,0:T(8,128)(2,1)S(1)} %get-tuple-element.464), channel_id=1, source_target_pairs={{0,4},{4,0},{1,5},{5,1},{2,6},{6,2},{3,7},{7,3},{8,12},{12,8},{9,1... | collective-permute-start | bytes 2162696 | tf_op jit(solution)/shard_map/ppermute | solution.py:927
  163.3 35.5 %collective-permute-start.23 = (bf16[1408,256]{1,0:T(8,128)(2,1)}, bf16[1408,256]{1,0:T(8,128)(2,1)S(1)}, u32[]{:S(2)}, u32[]{:S(2)}) collective-permute-start(bf16[1408,256]{1,0:T(8,128)(2,1)} %get-tuple-element.483), channel_id=1, source_target_pairs={{0,4},{4,0},{1,5},{5,1},{2,6},{6,2},{3,7},{7,3},{8,12},{12,8},{9,1... | collective-permute-start | bytes 2162696 | tf_op jit(solution)/shard_map/ppermute | solution.py:927
  165.0 33.7 %collective-permute-start.24 = (bf16[1408,256]{1,0:T(8,128)(2,1)}, bf16[1408,256]{1,0:T(8,128)(2,1)S(1)}, u32[]{:S(2)}, u32[]{:S(2)}) collective-permute-start(bf16[1408,256]{1,0:T(8,128)(2,1)} %get-tuple-element.484), channel_id=1, source_target_pairs={{0,4},{4,0},{1,5},{5,1},{2,6},{6,2},{3,7},{7,3},{8,12},{12,8},{9,1... | collective-permute-start | bytes 2162696 | tf_op jit(solution)/shard_map/ppermute | solution.py:927
  165.3 33.5 %collective-permute-start.22 = (bf16[1408,256]{1,0:T(8,128)(2,1)}, bf16[1408,256]{1,0:T(8,128)(2,1)}, u32[]{:S(2)}, u32[]{:S(2)}) collective-permute-start(bf16[1408,256]{1,0:T(8,128)(2,1)} %collective-permute-done.21.refs_1_), channel_id=1, source_target_pairs={{0,8},{8,0},{16,24},{24,16},{1,9},{9,1},{17,25},{25,17},{2,10},{10... | collective-permute-start | bytes 2162696 | tf_op jit(solution)/shard_map/ppermute | solution.py:936
  192.7 40.3 %collective-permute-start.27 = (bf16[768,1024]{1,0:T(8,128)(2,1)}, bf16[768,1024]{1,0:T(8,128)(2,1)}, u32[]{:S(2)}, u32[]{:S(2)}) collective-permute-start(bf16[768,1024]{1,0:T(8,128)(2,1)} %fusion.17), channel_id=1, source_target_pairs={{0,4},{4,0},{1,5},{5,1},{2,6},{6,2},{3,7},{7,3},{8,12},{12,8},{9,1... | collective-permute-start | bytes 4718600 | tf_op jit(solution)/shard_map/ppermute | solution.py:927
  232.7 43.8 %collective-permute-start.29 = (bf16[640,1024]{1,0:T(8,128)(2,1)}, bf16[640,1024]{1,0:T(8,128)(2,1)}, u32[]{:S(2)}, u32[]{:S(2)}) collective-permute-start(bf16[640,1024]{1,0:T(8,128)(2,1)} %fusion.20), channel_id=1, source_target_pairs={{0,4},{4,0},{1,5},{5,1},{2,6},{6,2},{3,7},{7,3},{8,12},{12,8},{9,1... | collective-permute-start | bytes 3932168 | tf_op jit(solution)/shard_map/ppermute | solution.py:927
  237.4 51.7 %collective-permute-start.38 = (bf16[768,1024]{1,0:T(8,128)(2,1)}, bf16[768,1024]{1,0:T(8,128)(2,1)}, u32[]{:S(2)}, u32[]{:S(2)}) collective-permute-start(bf16[768,1024]{1,0:T(8,128)(2,1)} %add_convert_fusion.a_ref), channel_id=1, source_target_pairs={{0,8},{24,16},{1,9},{25,17},{2,10},{26,18},{3,11},{27,19},{4,12},{... | collective-permute-start | bytes 4718600 | tf_op jit(solution)/shard_map/ppermute | solution.py:939
  246.2 33.3 %collective-permute-start.28 = (bf16[128,2048]{1,0:T(8,128)(2,1)}, bf16[128,2048]{1,0:T(8,128)(2,1)}, u32[]{:S(2)}, u32[]{:S(2)}) collective-permute-start(bf16[128,2048]{1,0:T(8,128)(2,1)} %get-tuple-element.525), channel_id=1, source_target_pairs={{0,2},{2,0},{1,3},{3,1},{4,6},{6,4},{5,7},{7,5},{8,10},{10,8},{9,1... | collective-permute-start | bytes 1572872 | tf_op jit(solution)/shard_map/ppermute | solution.py:933
  250.7 61.4 %collective-permute-start.34 = (bf16[256,2816]{1,0:T(8,128)(2,1)}, bf16[256,2816]{1,0:T(8,128)(2,1)}, u32[]{:S(2)}, u32[]{:S(2)}) collective-permute-start(bf16[256,2816]{1,0:T(8,128)(2,1)} %convolution_convert_fusion.2), channel_id=1, source_target_pairs={{0,4},{4,0},{1,5},{5,1},{2,6},{6,2},{3,7},{7,3},{8,12},{12,8},{9,1... | collective-permute-start | bytes 4325384 | tf_op jit(solution)/shard_map/ppermute | solution.py:927
  289.1 29.1 %collective-permute-start.32 = (bf16[128,2048]{1,0:T(8,128)(2,1)S(1)}, bf16[128,2048]{1,0:T(8,128)(2,1)S(1)}, u32[]{:S(2)}, u32[]{:S(2)}) collective-permute-start(bf16[128,2048]{1,0:T(8,128)(2,1)S(1)} %get-tuple-element.583.refs_0_), channel_id=1, source_target_pairs={{0,1},{1,0},{2,3},{3,2},{4,5},{5,4},{6,7},{7,6},{8,9},{9,8},{10,11... | collective-permute-start | bytes 1572872 | tf_op jit(solution)/shard_map/ppermute | solution.py:930
  299.7 45.3 %collective-permute-start.41 = (bf16[640,1024]{1,0:T(8,128)(2,1)S(1)}, bf16[640,1024]{1,0:T(8,128)(2,1)S(1)}, u32[]{:S(2)}, u32[]{:S(2)}) collective-permute-start(bf16[640,1024]{1,0:T(8,128)(2,1)S(1)} %add_convert_fusion.2.a_ref), channel_id=1, source_target_pairs={{0,8},{24,16},{1,9},{25,17},{2,10},{26,18},{3,11},{27,19},{4,12},{... | collective-permute-start | bytes 3932168 | tf_op jit(solution)/shard_map/ppermute | solution.py:939
  301.1 36.4 %collective-permute-start.42 = (bf16[768,1024]{1,0:T(8,128)(2,1)S(1)}, bf16[768,1024]{1,0:T(8,128)(2,1)S(1)}, u32[]{:S(2)}, u32[]{:S(2)}) collective-permute-start(bf16[768,1024]{1,0:T(8,128)(2,1)S(1)} %shard_map.159.a_ref), channel_id=1, source_target_pairs={{8,16},{16,8},{9,17},{17,9},{10,18},{18,10},{11,19},{19,11},{12,20... | collective-permute-start | bytes 4718600 | tf_op jit(solution)/shard_map/ppermute | solution.py:942
  312.1 36.5 %collective-permute-start.39 = (bf16[128,512]{1,0:T(8,128)(2,1)S(1)}, bf16[128,512]{1,0:T(8,128)(2,1)S(1)}, u32[]{:S(2)}, u32[]{:S(2)}) collective-permute-start(bf16[128,512]{1,0:T(8,128)(2,1)S(1)} %get-tuple-element.578), channel_id=1, source_target_pairs={{4,0},{5,1},{6,2},{7,3},{12,8},{13,9},{14,10},{15,11},{20,16},{21,... | collective-permute-start | bytes 393224 | tf_op jit(solution)/shard_map/ppermute | solution.py:1227
  318.2 44.2 %collective-permute-start.44 = (bf16[256,2816]{1,0:T(8,128)(2,1)}, bf16[256,2816]{1,0:T(8,128)(2,1)}, u32[]{:S(2)}, u32[]{:S(2)}) collective-permute-start(bf16[256,2816]{1,0:T(8,128)(2,1)} %fusion.a_ref), channel_id=1, source_target_pairs={{0,8},{24,16},{1,9},{25,17},{2,10},{26,18},{3,11},{27,19},{4,12},{... | collective-permute-start | bytes 4325384 | tf_op jit(solution)/shard_map/ppermute | solution.py:939
  337.6 31.2 %collective-permute-start.43 = (bf16[512,1024]{1,0:T(8,128)(2,1)}, bf16[512,1024]{1,0:T(8,128)(2,1)}, u32[]{:S(2)}, u32[]{:S(2)}) collective-permute-start(bf16[512,1024]{1,0:T(8,128)(2,1)} %add_convert_fusion.4), channel_id=1, source_target_pairs={{0,4},{4,0},{1,5},{5,1},{2,6},{6,2},{3,7},{7,3},{8,12},{12,8},{9,1... | collective-permute-start | bytes 3145736 | tf_op jit(solution)/shard_map/ppermute | solution.py:927
  346.9 33.4 %collective-permute-start.49 = (bf16[640,1024]{1,0:T(8,128)(2,1)}, bf16[640,1024]{1,0:T(8,128)(2,1)}, u32[]{:S(2)}, u32[]{:S(2)}) collective-permute-start(bf16[640,1024]{1,0:T(8,128)(2,1)} %shard_map.165.a_ref), channel_id=1, source_target_pairs={{8,16},{16,8},{9,17},{17,9},{10,18},{18,10},{11,19},{19,11},{12,20... | collective-permute-start | bytes 3932168 | tf_op jit(solution)/shard_map/ppermute | solution.py:942
  353.9 45.8 %collective-permute-start.48 = (bf16[256,2816]{1,0:T(8,128)(2,1)}, bf16[256,2816]{1,0:T(8,128)(2,1)}, u32[]{:S(2)}, u32[]{:S(2)}) collective-permute-start(bf16[256,2816]{1,0:T(8,128)(2,1)} %convolution_convert_fusion.1), channel_id=1, source_target_pairs={{0,4},{4,0},{1,5},{5,1},{2,6},{6,2},{3,7},{7,3},{8,12},{12,8},{9,1... | collective-permute-start | bytes 4325384 | tf_op jit(solution)/shard_map/ppermute | solution.py:927
  366.4 47.1 %collective-permute-start.46 = (bf16[256,2816]{1,0:T(8,128)(2,1)}, bf16[256,2816]{1,0:T(8,128)(2,1)}, u32[]{:S(2)}, u32[]{:S(2)}) collective-permute-start(bf16[256,2816]{1,0:T(8,128)(2,1)} %shard_map.168.a_ref), channel_id=1, source_target_pairs={{8,16},{16,8},{9,17},{17,9},{10,18},{18,10},{11,19},{19,11},{12,20... | collective-permute-start | bytes 4325384 | tf_op jit(solution)/shard_map/ppermute | solution.py:942
  373.4 32.6 %collective-permute-start.47 = (bf16[512,1024]{1,0:T(8,128)(2,1)}, bf16[512,1024]{1,0:T(8,128)(2,1)}, u32[]{:S(2)}, u32[]{:S(2)}) collective-permute-start(bf16[512,1024]{1,0:T(8,128)(2,1)} %add_convert_fusion.3.a_ref), channel_id=1, source_target_pairs={{0,8},{24,16},{1,9},{25,17},{2,10},{26,18},{3,11},{27,19},{4,12},{... | collective-permute-start | bytes 3145736 | tf_op jit(solution)/shard_map/ppermute | solution.py:939
  384.3 207.8 %all-reduce.6.cloned.1.call-start = ((), (), s32[]{:S(2)}) async-start(), calls=%async_computation.1 | async-start | bytes 8388608 | tf_op jit(solution)/shard_map/psum | solution.py:1248
  384.3 42.7 %collective-permute-start.45 = (bf16[1024,640]{1,0:T(8,128)(2,1)}, bf16[1024,640]{1,0:T(8,128)(2,1)S(1)}, u32[]{:S(2)}, u32[]{:S(2)}) collective-permute-start(bf16[1024,640]{1,0:T(8,128)(2,1)} %fusion.23), channel_id=1, source_target_pairs={{0,4},{4,0},{1,5},{5,1},{2,6},{6,2},{3,7},{7,3},{8,12},{12,8},{9,1... | collective-permute-start | bytes 3932168 | tf_op jit(solution)/shard_map/ppermute | solution.py:927
  387.8 57.1 %collective-permute-start.55 = (bf16[768,1024]{1,0:T(8,128)(2,1)}, bf16[768,1024]{1,0:T(8,128)(2,1)S(1)}, u32[]{:S(2)}, u32[]{:S(2)}) collective-permute-start(bf16[768,1024]{1,0:T(8,128)(2,1)} %copy-done.64), channel_id=1, source_target_pairs={{8,0},{16,24},{9,1},{17,25},{10,2},{18,26},{11,3},{19,27},{12,4},{... | collective-permute-start | bytes 4718600 | tf_op jit(solution)/shard_map/ppermute | solution.py:945
  399.7 89.4 %collective-permute-start.61 = (bf16[640,1024]{1,0:T(8,128)(2,1)S(1)}, bf16[640,1024]{1,0:T(8,128)(2,1)S(1)}, u32[]{:S(2)}, u32[]{:S(2)}) collective-permute-start(bf16[640,1024]{1,0:T(8,128)(2,1)S(1)} %shard_map.169.a_ref), channel_id=1, source_target_pairs={{8,0},{16,24},{9,1},{17,25},{10,2},{18,26},{11,3},{19,27},{12,4},{... | collective-permute-start | bytes 3932168 | tf_op jit(solution)/shard_map/ppermute | solution.py:945
  406.0 34.1 %collective-permute-start.56 = (bf16[256,2816]{1,0:T(8,128)(2,1)S(1)}, bf16[256,2816]{1,0:T(8,128)(2,1)S(1)}, u32[]{:S(2)}, u32[]{:S(2)}) collective-permute-start(bf16[256,2816]{1,0:T(8,128)(2,1)S(1)} %fusion.1.a_ref), channel_id=1, source_target_pairs={{0,8},{24,16},{1,9},{25,17},{2,10},{26,18},{3,11},{27,19},{4,12},{... | collective-permute-start | bytes 4325384 | tf_op jit(solution)/shard_map/ppermute | solution.py:939
  413.5 36.4 %collective-permute-start.54 = (bf16[512,1024]{1,0:T(8,128)(2,1)S(1)}, bf16[512,1024]{1,0:T(8,128)(2,1)S(1)}, u32[]{:S(2)}, u32[]{:S(2)}) collective-permute-start(bf16[512,1024]{1,0:T(8,128)(2,1)S(1)} %shard_map.170.a_ref), channel_id=1, source_target_pairs={{8,16},{16,8},{9,17},{17,9},{10,18},{18,10},{11,19},{19,11},{12,20... | collective-permute-start | bytes 3145736 | tf_op jit(solution)/shard_map/ppermute | solution.py:942
  427.0 34.5 %collective-permute-start.53 = (bf16[256,2816]{1,0:T(8,128)(2,1)S(1)}, bf16[256,2816]{1,0:T(8,128)(2,1)S(1)}, u32[]{:S(2)}, u32[]{:S(2)}) collective-permute-start(bf16[256,2816]{1,0:T(8,128)(2,1)S(1)} %convolution_convert_fusion), channel_id=1, source_target_pairs={{0,4},{4,0},{1,5},{5,1},{2,6},{6,2},{3,7},{7,3},{8,12},{12,8},{9,1... | collective-permute-start | bytes 4325384 | tf_op jit(solution)/shard_map/ppermute | solution.py:927
  440.1 30.3 %collective-permute-start.52 = (bf16[1024,640]{1,0:T(8,128)(2,1)S(1)}, bf16[1024,640]{1,0:T(8,128)(2,1)S(1)}, u32[]{:S(2)}, u32[]{:S(2)}) collective-permute-start(bf16[1024,640]{1,0:T(8,128)(2,1)S(1)} %add_convert_fusion.1.a_ref), channel_id=1, source_target_pairs={{0,8},{24,16},{1,9},{25,17},{2,10},{26,18},{3,11},{27,19},{4,12},{... | collective-permute-start | bytes 3932168 | tf_op jit(solution)/shard_map/ppermute | solution.py:939
  445.0 39.6 %collective-permute-start.62 = (bf16[256,2816]{1,0:T(8,128)(2,1)S(1)}, bf16[256,2816]{1,0:T(8,128)(2,1)S(1)}, u32[]{:S(2)}, u32[]{:S(2)}) collective-permute-start(bf16[256,2816]{1,0:T(8,128)(2,1)S(1)} %shard_map.171.a_ref), channel_id=1, source_target_pairs={{8,0},{16,24},{9,1},{17,25},{10,2},{18,26},{11,3},{19,27},{12,4},{... | collective-permute-start | bytes 4325384 | tf_op jit(solution)/shard_map/ppermute | solution.py:945
  450.0 45.1 %collective-permute-start.59 = (bf16[128,2816]{1,0:T(8,128)(2,1)S(1)}, bf16[128,2816]{1,0:T(8,128)(2,1)S(1)}, u32[]{:S(2)}, u32[]{:S(2)}) collective-permute-start(bf16[128,2816]{1,0:T(8,128)(2,1)S(1)} %convolution_convert_fusion.4), channel_id=1, source_target_pairs={{0,4},{4,0},{1,5},{5,1},{2,6},{6,2},{3,7},{7,3},{8,12},{12,8},{9,1... | collective-permute-start | bytes 2162696 | tf_op jit(solution)/shard_map/ppermute | solution.py:927
  461.5 33.2 %collective-permute-start.60 = (bf16[256,2816]{1,0:T(8,128)(2,1)S(1)}, bf16[256,2816]{1,0:T(8,128)(2,1)S(1)}, u32[]{:S(2)}, u32[]{:S(2)}) collective-permute-start(bf16[256,2816]{1,0:T(8,128)(2,1)S(1)} %shard_map.172.a_ref), channel_id=1, source_target_pairs={{8,16},{16,8},{9,17},{17,9},{10,18},{18,10},{11,19},{19,11},{12,20... | collective-permute-start | bytes 4325384 | tf_op jit(solution)/shard_map/ppermute | solution.py:942
  470.4 32.3 %collective-permute-start.58 = (bf16[256,2816]{1,0:T(8,128)(2,1)S(1)}, bf16[256,2816]{1,0:T(8,128)(2,1)S(1)}, u32[]{:S(2)}, u32[]{:S(2)}) collective-permute-start(bf16[256,2816]{1,0:T(8,128)(2,1)S(1)} %fusion.2.a_ref), channel_id=1, source_target_pairs={{0,8},{24,16},{1,9},{25,17},{2,10},{26,18},{3,11},{27,19},{4,12},{... | collective-permute-start | bytes 4325384 | tf_op jit(solution)/shard_map/ppermute | solution.py:939
  493.4 47.7 %collective-permute-start.65 = (bf16[128,2816]{1,0:T(8,128)(2,1)}, bf16[128,2816]{1,0:T(8,128)(2,1)}, u32[]{:S(2)}, u32[]{:S(2)}) collective-permute-start(bf16[128,2816]{1,0:T(8,128)(2,1)} %convolution_convert_fusion.3), channel_id=1, source_target_pairs={{0,4},{4,0},{1,5},{5,1},{2,6},{6,2},{3,7},{7,3},{8,12},{12,8},{9,1... | collective-permute-start | bytes 2162696 | tf_op jit(solution)/shard_map/ppermute | solution.py:927
  504.4 46.3 %collective-permute-start.69 = (bf16[256,2816]{1,0:T(8,128)(2,1)}, bf16[256,2816]{1,0:T(8,128)(2,1)}, u32[]{:S(2)}, u32[]{:S(2)}) collective-permute-start(bf16[256,2816]{1,0:T(8,128)(2,1)} %shard_map.179.a_ref), channel_id=1, source_target_pairs={{8,16},{16,8},{9,17},{17,9},{10,18},{18,10},{11,19},{19,11},{12,20... | collective-permute-start | bytes 4325384 | tf_op jit(solution)/shard_map/ppermute | solution.py:942
  506.2 49.2 %collective-permute-start.68 = (bf16[512,1024]{1,0:T(8,128)(2,1)}, bf16[512,1024]{1,0:T(8,128)(2,1)S(1)}, u32[]{:S(2)}, u32[]{:S(2)}) collective-permute-start(bf16[512,1024]{1,0:T(8,128)(2,1)} %copy-done.70), channel_id=1, source_target_pairs={{8,0},{16,24},{9,1},{17,25},{10,2},{18,26},{11,3},{19,27},{12,4},{... | collective-permute-start | bytes 3145736 | tf_op jit(solution)/shard_map/ppermute | solution.py:945
  507.5 59.4 %collective-permute-start.63 = (bf16[256,2816]{1,0:T(8,128)(2,1)S(1)}, bf16[256,2816]{1,0:T(8,128)(2,1)S(1)}, u32[]{:S(2)}, u32[]{:S(2)}) collective-permute-start(bf16[256,2816]{1,0:T(8,128)(2,1)S(1)} %shard_map.178.a_ref), channel_id=1, source_target_pairs={{8,0},{16,24},{9,1},{17,25},{10,2},{18,26},{11,3},{19,27},{12,4},{... | collective-permute-start | bytes 4325384 | tf_op jit(solution)/shard_map/ppermute | solution.py:945
  508.8 35.9 %collective-permute-start.64 = (bf16[128,2816]{1,0:T(8,128)(2,1)}, bf16[128,2816]{1,0:T(8,128)(2,1)S(1)}, u32[]{:S(2)}, u32[]{:S(2)}) collective-permute-start(bf16[128,2816]{1,0:T(8,128)(2,1)} %fusion.3.a_ref), channel_id=1, source_target_pairs={{0,8},{24,16},{1,9},{25,17},{2,10},{26,18},{3,11},{27,19},{4,12},{... | collective-permute-start | bytes 2162696 | tf_op jit(solution)/shard_map/ppermute | solution.py:939
  541.1 77.2 %collective-permute-start.70 = (bf16[1024,640]{1,0:T(8,128)(2,1)}, bf16[1024,640]{1,0:T(8,128)(2,1)}, u32[]{:S(2)}, u32[]{:S(2)}) collective-permute-start(bf16[1024,640]{1,0:T(8,128)(2,1)} %shard_map.180.a_ref), channel_id=1, source_target_pairs={{8,0},{16,24},{9,1},{17,25},{10,2},{18,26},{11,3},{19,27},{12,4},{... | collective-permute-start | bytes 3932168 | tf_op jit(solution)/shard_map/ppermute | solution.py:945
  555.4 72.1 %collective-permute-start.75 = (bf16[256,2816]{1,0:T(8,128)(2,1)}, bf16[256,2816]{1,0:T(8,128)(2,1)}, u32[]{:S(2)}, u32[]{:S(2)}) collective-permute-start(bf16[256,2816]{1,0:T(8,128)(2,1)} %shard_map.183.a_ref), channel_id=1, source_target_pairs={{8,0},{16,24},{9,1},{17,25},{10,2},{18,26},{11,3},{19,27},{12,4},{... | collective-permute-start | bytes 4325384 | tf_op jit(solution)/shard_map/ppermute | solution.py:945
  562.3 47.4 %collective-permute-start.72 = (bf16[128,2816]{1,0:T(8,128)(2,1)}, bf16[128,2816]{1,0:T(8,128)(2,1)}, u32[]{:S(2)}, u32[]{:S(2)}) collective-permute-start(bf16[128,2816]{1,0:T(8,128)(2,1)} %shard_map.185.a_ref), channel_id=1, source_target_pairs={{8,16},{16,8},{9,17},{17,9},{10,18},{18,10},{11,19},{19,11},{12,20... | collective-permute-start | bytes 2162696 | tf_op jit(solution)/shard_map/ppermute | solution.py:942
  565.4 76.0 %collective-permute-start.74 = (bf16[128,2816]{1,0:T(8,128)(2,1)}, bf16[128,2816]{1,0:T(8,128)(2,1)}, u32[]{:S(2)}, u32[]{:S(2)}) collective-permute-start(bf16[128,2816]{1,0:T(8,128)(2,1)} %shard_map.186.a_ref), channel_id=1, source_target_pairs={{8,0},{16,24},{9,1},{17,25},{10,2},{18,26},{11,3},{19,27},{12,4},{... | collective-permute-start | bytes 2162696 | tf_op jit(solution)/shard_map/ppermute | solution.py:945
  612.1 41.2 %collective-permute-start.73 = (bf16[128,2816]{1,0:T(8,128)(2,1)S(1)}, bf16[128,2816]{1,0:T(8,128)(2,1)S(1)}, u32[]{:S(2)}, u32[]{:S(2)}) collective-permute-start(bf16[128,2816]{1,0:T(8,128)(2,1)S(1)} %shard_map.189.a_ref), channel_id=1, source_target_pairs={{8,0},{16,24},{9,1},{17,25},{10,2},{18,26},{11,3},{19,27},{12,4},{... | collective-permute-start | bytes 2162696 | tf_op jit(solution)/shard_map/ppermute | solution.py:945
  (149 other events, 1482.3 us)
Sparse Core Ops, SparseCore 0:
  384.4 86.1 all-reduce.3
  506.3 85.6 all-reduce.5

commit v3 on v2

--- a/solution.py
+++ b/solution.py
@@ -27,7 +27,7 @@
     return lax.dot_general(a, b, (((ca,), (cb,)), ((), ())), preferred_element_type=F32)
 
 
-def call(body, grid, ins, outs, shapes, scratch=(), scalars=0, alias=None, vmem=20):
+def call(body, grid, ins, outs, shapes, scratch=(), scalars=0, alias=None, vmem=16):
     return pl.pallas_call(
         body,
         out_shape=shapes,
@@ -444,7 +444,7 @@
 
 
 def by_rows(step, place, s, quarter, owned, blocks, vectors, outs, sums=0):
-    width = owned[0].shape[1]
+    width = (owned or blocks)[0].shape[1]
     half = width // 2
     tile = min(32, quarter)
     per = quarter // tile
@@ -569,20 +569,17 @@
     )(middle, a, b, *before)
 
 
-def spread_gate_up(w, place, blocks, apart, before):
+def spread_gate_up(w, place, blocks):
     rows, _, ff = w.shape
     block = min(128, rows)
     steps = rows // block if blocks is None else len(blocks)
 
-    def body(p, w_ref, *refs):
-        outs = refs[len(before) :]
+    def body(p, w_ref, o_ref):
         for j in range(ff // 128):
             for g in range(2):
-                outs[0][:, 256 * j + 128 * g : 256 * j + 128 * (g + 1)] = w_ref[
+                o_ref[:, 256 * j + 128 * g : 256 * j + 128 * (g + 1)] = w_ref[
                     :, g, 128 * j : 128 * (j + 1)
                 ]
-        if apart:
-            outs[1][...] = outs[0][...]
 
     def row(i, p):
         if blocks is None:
@@ -595,28 +592,22 @@
     return call(
         body,
         (steps,),
-        [pl.BlockSpec((block, 2, ff), lambda i, p: (row(i, p), 0, 0))]
-        + [pl.BlockSpec(memory_space=pl.ANY)] * len(before),
-        [pl.BlockSpec((block, 2 * ff), lambda i, p: (row(i, p), 0))]
-        + [pl.BlockSpec((block, 2 * ff), lambda i, p: (i, 0))] * apart,
-        [jax.ShapeDtypeStruct((rows, 2 * ff), BF16)]
-        + [jax.ShapeDtypeStruct((steps * block, 2 * ff), BF16)] * apart,
-        scalars=1,
-        alias={2 + k: k for k in range(len(before))},
-    )(place, w, *before)
+        [pl.BlockSpec((block, 2, ff), lambda i, p: (row(i, p), 0, 0))],
+        pl.BlockSpec((block, 2 * ff), lambda i, p: (i, 0)),
+        jax.ShapeDtypeStruct((steps * block, 2 * ff), BF16),
+        scalars=1,
+    )(place, w)
 
 
 def gate_up(pieces, parts, place):
     quarter, width = pieces[0].shape
     count = len(pieces)
     rows = count * quarter
-    own, rest = parts[0].array, parts[1:]
-    depth = own.shape[0]
-    ff = own.shape[1] // 2
+    ff = parts[0].array.shape[1] // 2
     tile = 128
 
     def body(p, *refs):
-        own_ref, *rest_refs = refs[count : count + len(parts)]
+        w_refs = refs[count : count + len(parts)]
         n_ref, act_ref, gu_ref, w_ref = refs[count + len(parts) :]
 
         @pl.when(pl.program_id(0) == 0)
@@ -624,13 +615,12 @@
             for k in range(count):
                 n_ref[k * quarter : (k + 1) * quarter] = refs[k][...]
 
-        gu = dot(n_ref[:, :depth], own_ref[...])
-        if rest:
-            for part, ref in zip(rest, rest_refs):
-                size = part.array.shape[0]
-                at = pl.multiple_of(part.start(width, p[2]) - depth, 128)
-                w_ref[pl.ds(at, size), :] = ref[...]
-            gu = gu + dot(n_ref[:, depth:], w_ref[...])
+        for part, ref in zip(parts, w_refs):
+            size = part.array.shape[0]
+            at = part.start(width, p[2])
+            at = at if part.late is None else pl.multiple_of(at, 128)
+            w_ref[pl.ds(at, size), :] = ref[...]
+        gu = dot(n_ref[...], w_ref[...])
         gate, up = gu[:, :tile], gu[:, tile:]
         sig = 1.0 / (1.0 + jnp.exp2(gate * (-LOG2E)))
         act_ref[...] = (gate * sig * up).astype(BF16)
@@ -651,7 +641,7 @@
             jax.ShapeDtypeStruct((rows, ff), BF16),
             jax.ShapeDtypeStruct((rows, 2 * ff), BF16),
         ],
-        scratch=[pltpu.VMEM((max(width - depth, 8), 2 * tile), BF16)],
+        scratch=[pltpu.VMEM((width, 2 * tile), BF16)],
         scalars=1,
         vmem=30,
     )(place, *pieces, *[x.array for x in parts])
@@ -734,7 +724,7 @@
         return pl.BlockSpec(shape, index, **once)
 
     def column(j, p):
-        c = j
+        c = parts[0].start(cols, p[2]) // tile + j
         for k in range(1, len(parts)):
             at = parts[k].start(cols, p[2]) // tile + j - bases[k]
             c = jnp.where(j >= bases[k], at, c)
@@ -793,7 +783,7 @@
         return pl.BlockSpec((tile, depth) if transposed else (depth, tile), index)
 
     def column(j, p):
-        c = j
+        c = parts[0].start(cols, p[2]) // tile + j
         for k in range(1, len(parts)):
             c = jnp.where(j >= bases[k], parts[k].start(cols, p[2]) // tile + j - bases[k], c)
         return (0, c)
@@ -851,7 +841,7 @@
     count = len(d2)
 
     def body(p, a_ref, b_ref, u_ref, g_ref, *refs):
-        o_ref, sum_ref = refs[count:]
+        o_ref = refs[count]
         i = pl.program_id(0)
         h = jnp.concatenate([a_ref[...], b_ref[...]], 1)
         inv = lax.rsqrt(jnp.mean(h * h, axis=-1, keepdims=True) + NORM_EPS)
@@ -864,16 +854,6 @@
             def _():
                 put_columns(o_ref, back + refs[s][...].astype(F32), p[1], half)
 
-        total = jnp.sum(mine * h * inv, axis=0, keepdims=True)
-
-        @pl.when(i == 0)
-        def _():
-            sum_ref[...] = total
-
-        @pl.when(i > 0)
-        def _():
-            sum_ref[...] += total
-
     def spec(s):
         return pl.BlockSpec((block, width), lambda i, p: (jnp.clip(i - s * per, 0, per - 1), 0))
 
@@ -887,13 +867,42 @@
             pl.BlockSpec((1, width), lambda i, p: (0, 0)),
         ]
         + [spec(s) for s in range(count)],
-        [
+        pl.BlockSpec((block, width), lambda i, p: (i, 0)),
+        jax.ShapeDtypeStruct((rows, width), F32),
+        scalars=1,
+    )(place, x, x, upstream, gain, *d2)
+
+
+def gain_rows(x, upstream, place, block):
+    rows, width = x.shape
+    half = width // 2
+
+    def body(p, a_ref, b_ref, u_ref, sum_ref):
+        i = pl.program_id(0)
+        h = jnp.concatenate([a_ref[...], b_ref[...]], 1)
+        inv = lax.rsqrt(jnp.mean(h * h, axis=-1, keepdims=True) + NORM_EPS)
+        total = jnp.sum(u_ref[...].astype(F32) * h * inv, axis=0, keepdims=True)
+
+        @pl.when(i == 0)
+        def _():
+            sum_ref[...] = total
+
+        @pl.when(i > 0)
+        def _():
+            sum_ref[...] += total
+
+    return call(
+        body,
+        (rows // block,),
+        [
+            pl.BlockSpec((block, half), lambda i, p: (i, p[1])),
+            pl.BlockSpec((block, half), lambda i, p: (i, 1 - p[1])),
             pl.BlockSpec((block, width), lambda i, p: (i, 0)),
-            pl.BlockSpec((1, width), lambda i, p: (0, 0)),
-        ],
-        [jax.ShapeDtypeStruct((rows, width), F32), jax.ShapeDtypeStruct((1, width), F32)],
-        scalars=1,
-    )(place, x, x, upstream, gain, *d2)
+        ],
+        pl.BlockSpec((1, width), lambda i, p: (0, 0)),
+        jax.ShapeDtypeStruct((1, width), F32),
+        scalars=1,
+    )(place, x, x, upstream)
 
 
 def per_device(
@@ -959,14 +968,16 @@
         gains = jnp.concatenate([norm_gains[0], swap_seq(norm_gains[0])], 1).astype(F32)
         qkv_parts = [Part(wq), Part(swap_seq(wq), half)]
         out_x = swap_seq(lax.dynamic_slice_in_dim(wo, pz * fourth, fourth, 1))
-        gu_own, gu_a = order(
-            lambda w, p: spread_gate_up(w, p, [lambda p: 4 * p[2]], 1, []), wg, place
-        )
+
+        def spread(*blocks):
+            return order(lambda w, p: spread_gate_up(w, p, list(blocks)), wg, place)
+
+        gu_a = spread(lambda p: 4 * p[2])
     else:
         gains = whole(norm_gains[0], 1).astype(F32)
         qkv_parts, out_parts = [Part(whole(wq, 0))], [Part(whole(wo, 1))]
         down_parts = [Part(whole(wd, 1))]
-        gu_parts = [Part(spread_gate_up(whole(wg, 0), place, None, 0, [])[0])]
+        gu_parts = [Part(spread_gate_up(whole(wg, 0), place, None))]
 
     first_row = si * length
     ids = jnp.arange(total, dtype=jnp.int32)
@@ -995,11 +1006,18 @@
 
     hidden = hidden_in.reshape(rows, width)
     d_hidden = cotangent.reshape(rows, width)
-    late_blocks = [lambda p, k=k: 4 * (1 - p[2]) + k for k in (0, 2, 3)]
     normed1 = order(lambda h, g, p: first_norm(h, g, p, 2 * quarter), hidden, gains[:1], place)
     if two:
-        gu_own = order(lambda w, p, b: spread_gate_up(w, p, late_blocks, 0, [b]), wg, place, gu_own)[0]
+        gu_c = spread(lambda p: 1, lambda p: 5)
     dhb = order(lambda d, p: local_cast(d, p, quarter), d_hidden, place)
+    own_h, own_d = [None] * seqs, [None] * seqs
+    for s in range(seqs):
+        own_h[s], own_d[s] = order(
+            lambda h, d, p, s=s: by_rows(
+                lambda h, d: (h, d), p, s, quarter, [h, d], [], [], [F32, F32]
+            ),
+            hidden, d_hidden, place,
+        )
     q_t, kv_t = order(
         lambda n, w, c, s: project_qkv(n, w, c, s, group),
         normed1, [x.array for x in qkv_parts], cos_t, sin_t,
@@ -1007,10 +1025,7 @@
     if two:
         kv_got = lax.ppermute(kv_t, "seq", [(0, 1)])
         gu_x = [swap_seq(*now(gu_a))]
-        blocks_b = [lambda p, k=k: 4 * p[2] + k for k in (2, 3)]
-        gu_own, gu_b = order(
-            lambda w, p, b: spread_gate_up(w, p, blocks_b, 1, [b]), wg, place, gu_own
-        )
+        gu_b = spread(lambda p: 4 * p[2] + 2, lambda p: 4 * p[2] + 3)
         out_z = swap_z(*now(out_x))
         all_kv = order(join_kv, kv_t, kv_got, place)
         out_parts = [Part(wo), Part(out_x, 0, 0), Part(out_z, 0, 1)]
@@ -1047,12 +1062,8 @@
         summed(keep, hold, s - 1)
         out_product(s)
     if two:
-        blocks_c = [lambda p: 1, lambda p: 5]
-        gu_own, gu_c = order(
-            lambda w, p, b: spread_gate_up(w, p, blocks_c, 1, [b]), wg, place, gu_own
-        )
-        gu_c = [swap_seq(gu_c[k * 128 : (k + 1) * 128]) for k in range(2)]
-        touch(order, gu_z[0])
+        own_c = [gu_c[k * 128 : (k + 1) * 128] for k in range(2)]
+        gu_c = [swap_seq(x) for x in now(*own_c)]
     summed(keep, hold, seqs - 1)
     if two:
         touch(order, gu_x[1])
@@ -1076,18 +1087,21 @@
     for s in range(seqs):
         h2[s], mine, extra[s] = order(
             lambda h, k, g, gain, p, s=s: by_rows(
-                second_norm, p, s, quarter, [h], [k, g], [gain], [F32, BF16, BF16]
+                second_norm, p, s, quarter, [], [h, k, g], [gain], [F32, BF16, BF16]
             ),
-            hidden, keep[s], hold[s], gains[1:], place,
+            own_h[s], keep[s], hold[s], gains[1:], place,
         )
         n2[s] = share(mine)
         if two and s == 0:
-            touch(order, gu_c[0])
+            gu_d = spread(*[lambda p, k=k: 4 * (1 - p[2]) + k for k in (0, 2, 3)])
+            touch(order, gu_z[0], gu_c[0])
             down_send = now(*down_send)
             down_x = swap_seq(down_send[0])
             down_c = [swap_seq(x) for x in down_send[1:]]
     if two:
-        gu_parts = [Part(gu_own)]
+        gu_parts = [Part(gu_a, -half, 0), Part(gu_b, 256 - half, 0)]
+        gu_parts += [Part(own_c[k], k * fourth + 128) for k in range(2)]
+        gu_parts += [Part(gu_d[:128], -half, 1), Part(gu_d[128:], 256 - half, 1)]
         gu_parts += [Part(gu_x[k], k * 256, 0) for k in range(2)]
         gu_parts += [Part(gu_z[k], k * 256, 1) for k in range(2)]
         gu_parts += [Part(gu_c[k], half + k * fourth + 128) for k in range(2)]
@@ -1178,9 +1192,13 @@
             return jnp.concatenate([a, jnp.where(first, c[0], c[1])])
 
         begin_down(1)
+        near = order(lambda a, c: pair(a, c, pz == 0), gu_a, own_c)
+        far = order(lambda a, c: pair(a, c, pz == 1), gu_d[:128], own_c)
         pair_x = order(lambda a, c: pair(a, c, pz == 0), gu_x[0], gu_c)
         pair_z = order(lambda a, c: pair(a, c, pz == 1), gu_z[0], gu_c)
-        gu_parts = [Part(gu_own), Part(pair_x, 0, 0), Part(gu_x[1], 256, 0)]
+        gu_parts = [Part(near, -half, 0), Part(gu_b, 256 - half, 0)]
+        gu_parts += [Part(far, -half, 1), Part(gu_d[128:], 256 - half, 1)]
+        gu_parts += [Part(pair_x, 0, 0), Part(gu_x[1], 256, 0)]
         gu_parts += [Part(pair_z, 0, 1), Part(gu_z[1], 256, 1)]
     dgu = order(gate_back, dhb, down_parts, gu, place)
     got = order(
@@ -1191,9 +1209,6 @@
     for s in range(seqs):
         summed(keep, hold, s)
     begin_gu(0)
-    delta = order(
-        lambda a, w, p, x: full_matmul(a, w, False, p, seqs, x), act, down_parts, place, extra
-    )
     d2, gain2 = [None] * seqs, []
 
     def second_back(d, k, g, x, gain):
@@ -1206,9 +1221,9 @@
     for s in range(seqs):
         mine, g2 = order(
             lambda d, k, g, x, gain, p, s=s: by_rows(
-                second_back, p, s, quarter, [d], [k, g, x], [gain], [BF16], 1
+                second_back, p, s, quarter, [], [d, k, g, x], [gain], [BF16], 1
             ),
-            d_hidden, keep[s], hold[s], h2[s], gains[1:], place,
+            own_d[s], keep[s], hold[s], h2[s], gains[1:], place,
         )
         gain2.append(g2)
         d2[s] = share(mine)
@@ -1227,7 +1242,6 @@
             dkv_got.append(lax.ppermute(early[s], "seq", [(1, 0)]))
         if s == 0:
             go("g0")
-    delta = lax.psum(lax.optimization_barrier((delta, d2[-1]))[0], "tp")
     begin(
         "out",
         into("out", lambda a, b, m, r: place_rows(a, b, m, 0, a.shape[0], r)),
@@ -1237,6 +1251,9 @@
         att, d2,
     )
     go("d0", "d1")
+    delta = order(
+        lambda a, w, p, x: full_matmul(a, w, False, p, seqs, x), act, down_parts, place, extra
+    )
     if not two:
         dkv = [lax.psum_scatter(x, "seq", scatter_dimension=1, tiled=True) for x in dkv]
     d_qkv = order(
@@ -1245,7 +1262,8 @@
     )
     begin_gu(1)
     d_n1 = order(lambda a, w, p: full_matmul(a, w, True, p, seqs, []), d_qkv, qkv_parts, place)
-    d_n1 = lax.psum(lax.optimization_barrier((d_n1, delta))[0], "tp")
+    d_part = d_n1
+    delta, d_n1 = lax.psum((delta, d_n1), "tp")
     go("g0", "out")
     begin(
         "qkv",
@@ -1253,31 +1271,31 @@
         lambda k, n, d: tdot(piece_of(n, k, 0, half), d, k),
         normed1, d_qkv,
     )
-    go("d1")
-    gain2 = order(lambda g: sum(g), gain2)
-    gain2 = order(lambda a, b: a + b, gain2, swap_core(gain2))
-    gain2 = order(lambda a, b: a + b, gain2, swap_y(gain2))
+    go("d0", "d1")
+    gain1 = order(lambda h, u, p: gain_rows(h, u, p, quarter), hidden, d_part, place)
     go("g1", "out", "g0")
     begin_gu(2)
-    go("qkv", "g1", "d0")
+    gain_sum = order(lambda a, b: jnp.concatenate([a, sum(b)]), gain1, gain2)
+    gain_sum = order(lambda a, b: a + b, gain_sum, swap_core(gain_sum))
+    gain_sum = order(lambda a, b: a + b, gain_sum, swap_y(gain_sum))
+
+    def gain_finish(a, b):
+        results["gain"] = [order(lambda a, b: jnp.where(middle, a, b), a, b)]
+
+    go("qkv", "d1", "g1", "out", "g0")
     begin_gu(3)
-    go("out", "g2", "qkv", "g0", "d1")
+    begin("gain", gain_finish, lambda k, g: piece_of(g, k, 0, half), gain_sum)
+    go("g2", "qkv", "g1", "out", "gain")
     begin_gu(4)
-    go("g1", "g3", "g2", "qkv")
+    go("g3", "g2", "qkv", "gain", "g1")
+    go("g4", "g3", "g2", "gain", "qkv")
+    go("g4", "g3", "g2", "gain", "g4")
     hidden_out = order(lambda h, d, p: add_columns(h, d, p, quarter), hidden, delta, place)
-    go("g4", "g3", "g2", "out")
-    go("g4", "g3", "g1")
-    grad_in, gain1 = order(
+    grad_in = order(
         lambda h, u, d, g, p: first_norm_back(h, u, d, g, p, quarter),
         hidden, d_n1, d2, gains[:1], place,
     )
-    gain_sum = order(lambda a, b: jnp.concatenate([a, b]), gain1, gain2)
-
-    def gain_finish(a, b):
-        results["gain"] = [order(lambda a, b: jnp.where(middle, a, b), a, b)]
-
-    begin("gain", gain_finish, lambda k, g: piece_of(g, k, 0, half), gain_sum)
-    go("g4", "gain", "qkv", "gain", "g2", "gain", "g3", "g4", "gain")
+    go("g3", "g4")
     if two:
         g_qkv, g_out, g_down = results["qkv"][0], results["out"][0], results["down"][0]
         g_gu, gain_own = results["gu"][0], results["gain"][0]

time: 671 us -> 656 us (0.978)
  waiting for transfers between devices: 144 us -> 116 us
  starting transfers between devices: 146 us -> 161 us
  local copies, waits for them, and re-layouts: 52.2 us -> 40.4 us
  Pallas kernels: 246 us -> 254 us
    ppermute x10, starting transfers between devices: 56.6 us -> 80.3 us  [hop_in(): return lax.ppermute(x, 'rep', [(0, 1), (3, 2)])]
    psum x2 -> x1, waiting for transfers between devices: 22.4 us -> 0.02 us  [per_device(): delta, d_n1 = lax.psum((delta, d_n1), 'tp')]
    ppermute x20, waiting for transfers between devices: 57.6 us -> 39.7 us  [swap_seq(): return lax.ppermute(x, 'seq', [(0, 1), (1, 0)])]
    unnamed x235, local copies, waits for them, and re-layouts: 49 us -> 34.3 us
    ppermute x9, waiting for transfers between devices: 12.2 us -> 24.8 us  [swap_y(): return lax.ppermute(x, 'tp', [(0, 2), (2, 0), (1, 3), (3, 1)])]
    ppermute x20, starting transfers between devices: 40.6 us -> 30.4 us  [swap_seq(): return lax.ppermute(x, 'seq', [(0, 1), (1, 0)])]
    pallas_call x4, Pallas kernels: 26.8 us -> 18.9 us  [spread_gate_up(): call(body, (steps,), [pl.BlockSpec((block, 2, ff), lambda i, p: (row(i, p...]
  transfers between devices with their start and end apart: 81 -> 80, of which waited for: 25 -> 23; matrix products, arithmetic and copies ran while one was open for 10% -> 10% of each run, Pallas kernels for 36% -> 38%
where the time goes in v3:
time: 656 us; the launch traced here: 645 us
  Pallas kernels  254 us (39%)
  starting transfers between devices  161 us (25%)
  waiting for transfers between devices  116 us (18%)
  matrix products  47.6 us (7%)
  local copies, waits for them, and re-layouts  40.4 us (6%)
  between operations  16.5 us (3%)
  other arithmetic  9.54 us (1%)
    ppermute x10, starting transfers between devices, hop_in(): return lax.ppermute(x, 'rep', [(0, 1), (3, 2)])  80.3 us
    dot_general x20, matrix products, dot(): lax.dot_general(a, b, (((ca,), (cb,)), ((), ())), preferred_element_type=...  47.6 us
    ppermute x20, waiting for transfers between devices, swap_seq(): return lax.ppermute(x, 'seq', [(0, 1), (1, 0)])  39.7 us
    pallas_call x3, Pallas kernels, split_matmul(): call(body, (sum(counts),), [pl.BlockSpec((rows, depth), lambda j, p: (0,...  34.8 us
    unnamed x235, local copies, waits for them, and re-layouts  34.3 us
    pallas_call x18, Pallas kernels, add_pair(): call(body, (4,), [spec, spec], spec, jax.ShapeDtypeStruct((rows, cols), B...  32.3 us
    ppermute x20, starting transfers between devices, swap_seq(): return lax.ppermute(x, 'seq', [(0, 1), (1, 0)])  30.4 us
    ppermute x10, waiting for transfers between devices, hop_in(): return lax.ppermute(x, 'rep', [(0, 1), (3, 2)])  25.3 us
  transfers between devices with their start and end apart: 80, of which 23 were waited for; matrix products, arithmetic and copies ran while one was open for 10% of the time, Pallas kernels for 38%

profile of v3, /device:TPU:0, one launch (start us, length us, event | category | flops | bytes accessed | tf_op | source)
XLA Modules:
  0.0 645.4 jit_solution(10023468258363537768)
XLA Ops:
  25.8 4.5 shard_map.137
  42.2 5.8 shard_map.141
  50.3 5.5 shard_map.142.refs_9_.refs_1_
  58.6 7.8 %shard_map.144 = (bf16[512,512]{1,0:T(8,128)(2,1)S(1)}, bf16[512,512]{1,0:T(8,128)(2,1)S(1)}, f32[8,512]{1,0:T(8,128)S(1)}) custom-call(s32[6]{0:T(128)S(1)} %pad_add_fusion.3.b_ref, bf16[2,512,512]{2,1,0:T(8,128)(2,1)S(1)} %get-tuple-element.611.q_ref, bf16[2,128,1024]{2,1,0:T(8,128)(2,1)S(1)} %shard_map.143.kv_ref, s32[2,1,512]{2,1,0:T(1,128)S(1)} %broadcast_in_dim.33.st_ref), custom_call_target="tpu_custom_call" | custom-call | flops 3000000000 | bytes 8000000 | tf_op jit(solution)/shard_map/pallas_call | solution.py:250
  70.8 6.5 %shard_map.145 = (bf16[256,2048]{1,0:T(8,128)(2,1)}, f32[256,2048]{1,0:T(8,128)S(1)}) custom-call(s32[3]{0:T(128)S(1)} %pad_add_fusion.2.p, bf16[512,512]{1,0:T(8,128)(2,1)S(1)} %get-tuple-element.659.a_ref, bf16[512,1024]{1,0:T(8,128)(2,1)S(1)} %bitcast.97, bf16[512,512]{1,0:T(8,128)(2,1)} %collective-permute-done.3.refs_1_, ...), custom_call_target="tpu_custom_call" | custom-call | flops 3000000000 | bytes 8000000 | tf_op jit(solution)/shard_map/pallas_call | solution.py:733
  83.8 7.8 %shard_map.146 = (bf16[512,512]{1,0:T(8,128)(2,1)S(1)}, bf16[512,512]{1,0:T(8,128)(2,1)S(1)}, f32[8,512]{1,0:T(8,128)S(1)}) custom-call(s32[6]{0:T(128)S(1)} %pad_add_fusion.5.b_ref, bf16[2,512,512]{2,1,0:T(8,128)(2,1)S(1)} %copy-done.77, bf16[2,128,1024]{2,1,0:T(8,128)(2,1)S(1)} %copy-done.82, s32[2,1,512]{2,1,0:T(1,128)S(1)} %broadcast_in_dim.33.st_ref), custom_call_target="tpu_custom_call" | custom-call | flops 3000000000 | bytes 8000000 | tf_op jit(solution)/shard_map/pallas_call | solution.py:250
  94.4 5.8 shard_map.148
  104.0 4.7 collective-permute-start.15
  109.4 5.0 collective-permute-done.9.refs_15_.refs_5_
  123.0 6.5 %shard_map.151 = bf16[384,2816]{1,0:T(8,128)(2,1)S(1)} custom-call(s32[3]{0:T(128)S(1)} %pad_add_fusion.2.p, bf16[1024,2,1408]{2,1,0:T(2,128)(2,1)S(1)} %bitcast.108), custom_call_target="tpu_custom_call" | custom-call | flops 3000000000 | bytes 8000000 | tf_op jit(solution)/shard_map/pallas_call | solution.py:592
  131.3 4.2 collective-permute-start.21
  140.5 4.6 collective-permute-done.20.refs_19_
  146.5 14.0 %collective-permute-done.21.refs_1_ = bf16[1408,256]{1,0:T(8,128)(2,1)} collective-permute-done((bf16[1408,256]{1,0:T(8,128)(2,1)S(1)}, bf16[1408,256]{1,0:T(8,128)(2,1)}, u32[]{:S(2)}, u32[]{:S(2)}) %collective-permute-start.21) | collective-permute-done | bytes 720928 | tf_op jit(solution)/shard_map/ppermute | solution.py:936
  167.8 20.3 %shard_map.153 = (bf16[1024,2048]{1,0:T(8,128)(2,1)S(1)}, bf16[1024,1408]{1,0:T(8,128)(2,1)S(1)}, bf16[1024,2816]{1,0:T(8,128)(2,1)}) custom-call(s32[3]{0:T(128)S(1)} %pad_add_fusion.2.p, bf16[128,2048]{1,0:T(8,128)(2,1)} %get-tuple-element.484.refs_0_, bf16[128,2048]{1,0:T(8,128)(2,1)} %collective-permute-done.10.refs_1_, ...), custom_call_target="tpu_custom_call" | custom-call | flops 3000000000 | bytes 8000000 | tf_op jit(solution)/shard_map/pallas_call | solution.py:629
  198.8 12.1 %shard_map.154.a_ref = bf16[1024,2816]{1,0:T(8,128)(2,1)S(1)} custom-call(s32[3]{0:T(128)S(1)} %pad_add_fusion.2.p, bf16[1024,2048]{1,0:T(8,128)(2,1)S(1)} %copy-done.8, bf16[1024,2816]{1,0:T(8,128)(2,1)S(1)} %bitcast.95, bf16[1408,1024]{1,0:T(8,128)(2,1)S(1)} %bitcast.92, bf16[1408,256]{1,0:T(8,128)(2,1)} %collective-permute-done.21.refs_1_, ...), custom_call_target="tpu_custom_call" | custom-call | flops 3000000000 | bytes 8000000 | tf_op jit(solution)/shard_map/pallas_call | solution.py:673
  210.9 22.4 %shard_map.155 = (bf16[256,2048]{1,0:T(8,128)(2,1)S(1)}, f32[256,2048]{1,0:T(8,128)S(1)}, bf16[256,2048]{1,0:T(8,128)(2,1)S(1)}, f32[256,2048]{1,0:T(8,128)S(1)}) custom-call(s32[3]{0:T(128)S(1)} %pad_add_fusion.2.p, bf16[1024,2816]{1,0:T(8,128)(2,1)S(1)} %shard_map.154.a_ref, bf16[256,2816]{1,0:T(8,128)(2,1)S(1)} %pad_maximum_fusion.refs_0_, ...), custom_call_target="tpu_custom_call" | custom-call | flops 3000000000 | bytes 8000000 | tf_op jit(solution)/shard_map/pallas_call | solution.py:733
  238.6 4.9 collective-permute-start.31
  250.2 9.1 %collective-permute-done.28.refs_2_ = bf16[128,2048]{1,0:T(8,128)(2,1)S(1)} collective-permute-done((bf16[128,2048]{1,0:T(8,128)(2,1)S(1)}, bf16[128,2048]{1,0:T(8,128)(2,1)S(1)}, u32[]{:S(2)}, u32[]{:S(2)}) %collective-permute-start.28) | collective-permute-done | bytes 524320 | tf_op jit(solution)/shard_map/ppermute | solution.py:942
  275.2 6.6 %collective-permute-done.34.refs_1_ = bf16[128,2048]{1,0:T(8,128)(2,1)} collective-permute-done((bf16[128,2048]{1,0:T(8,128)(2,1)}, bf16[128,2048]{1,0:T(8,128)(2,1)}, u32[]{:S(2)}, u32[]{:S(2)}) %collective-permute-start.34) | collective-permute-done | bytes 524320 | tf_op jit(solution)/shard_map/ppermute | solution.py:942
  286.9 4.6 collective-permute-done.37.refs_1_
  295.1 10.8 %shard_map.162 = (bf16[512,512]{1,0:T(8,128)(2,1)S(1)}, f32[128,1024]{1,0:T(8,128)S(1)}, bf16[128,512]{1,0:T(8,128)(2,1)S(1)}) custom-call(s32[6]{0:T(128)S(1)} %copy-done.56, bf16[2,512,512]{2,1,0:T(8,128)(2,1)S(1)} %copy-done.78, bf16[2,128,1024]{2,1,0:T(8,128)(2,1)S(1)} %copy-done.83, s32[2,1,512]{2,1,0:T(1,128)S(1)} %broadcast_in_dim.33.st_ref, ...), custom_call_target="tpu_custom_call" | custom-call | flops 3000000000 | bytes 8000000 | tf_op jit(solution)/shard_map/pallas_call | solution.py:347
  307.2 4.4 fusion.a_ref
  311.6 4.3 collective-permute-start.46
  318.0 10.3 %shard_map.164 = (bf16[512,512]{1,0:T(8,128)(2,1)S(1)}, f32[128,1024]{1,0:T(8,128)S(1)}, bf16[128,512]{1,0:T(8,128)(2,1)S(1)}) custom-call(s32[6]{0:T(128)S(1)} %copy-done.58, bf16[2,512,512]{2,1,0:T(8,128)(2,1)S(1)} %copy-done.78, bf16[2,128,1024]{2,1,0:T(8,128)(2,1)S(1)} %copy-done.83, s32[2,1,512]{2,1,0:T(1,128)S(1)} %broadcast_in_dim.33.st_ref, ...), custom_call_target="tpu_custom_call" | custom-call | flops 3000000000 | bytes 8000000 | tf_op jit(solution)/shard_map/pallas_call | solution.py:347
  332.7 4.6 collective-permute-start.45
  342.5 12.4 %shard_map.167 = bf16[1024,2048]{1,0:T(8,128)(2,1)S(1)} custom-call(s32[3]{0:T(128)S(1)} %pad_add_fusion.2.p, bf16[1024,1408]{1,0:T(8,128)(2,1)S(1)} %copy-done.34, bf16[1408,1024]{1,0:T(8,128)(2,1)S(1)} %bitcast.93, bf16[1408,256]{1,0:T(8,128)(2,1)} %collective-permute-done.21.refs_1_, bf16[1408,256]{1,0:T(8,128)(2,1)} %collective-permute-done.22.refs_2_, ...), custom_call_target="tpu_custom_call" | custom-call | flops 3000000000 | bytes 8000000 | tf_op jit(solution)/shard_map/pallas_call | solution.py:791
  359.6 4.4 convolution_convert_fusion.1
  363.9 7.9 %shard_map.169.u_ref = bf16[1024,2048]{1,0:T(8,128)(2,1)S(1)} custom-call(s32[3]{0:T(128)S(1)} %pad_add_fusion.2.p, bf16[1024,640]{1,0:T(8,128)(2,1)S(1)} %shard_map.168.a_ref, bf16[1024,640]{1,0:T(8,128)(2,1)S(1)} %bitcast.111, bf16[1024,640]{1,0:T(8,128)(2,1)} %collective-permute-done.1.refs_1_), custom_call_target="tpu_custom_call" | custom-call | flops 3000000000 | bytes 8000000 | tf_op jit(solution)/shard_map/pallas_call | solution.py:791
  383.3 11.0 %collective-permute-start.48 = (bf16[512,1024]{1,0:T(8,128)(2,1)}, bf16[512,1024]{1,0:T(8,128)(2,1)}, u32[]{:S(2)}, u32[]{:S(2)}) collective-permute-start(bf16[512,1024]{1,0:T(8,128)(2,1)} %add_convert_fusion.3.a_ref), channel_id=1, source_target_pairs={{0,8},{24,16},{1,9},{25,17},{2,10},{26,18},{3,11},{27,19},{4,12},{... | collective-permute-start | bytes 3145736 | tf_op jit(solution)/shard_map/ppermute | solution.py:948
  401.2 5.6 shard_map.171.refs_0_
  406.8 4.8 shard_map.172.a_ref
  417.1 4.9 fusion.1.a_ref
  422.0 6.7 %collective-permute-start.54 = (bf16[256,2816]{1,0:T(8,128)(2,1)S(1)}, bf16[256,2816]{1,0:T(8,128)(2,1)}, u32[]{:S(2)}, u32[]{:S(2)}) collective-permute-start(bf16[256,2816]{1,0:T(8,128)(2,1)S(1)} %fusion.1.a_ref), channel_id=1, source_target_pairs={{0,8},{24,16},{1,9},{25,17},{2,10},{26,18},{3,11},{27,19},{4,12},{... | collective-permute-start | bytes 4325384 | tf_op jit(solution)/shard_map/ppermute | solution.py:948
  454.8 6.0 collective-permute-start.60
  460.9 4.7 shard_map.176
  480.3 5.0 collective-permute-done.61
  488.4 7.4 %collective-permute-start.66 = (bf16[256,2816]{1,0:T(8,128)(2,1)S(1)}, bf16[256,2816]{1,0:T(8,128)(2,1)S(1)}, u32[]{:S(2)}, u32[]{:S(2)}) collective-permute-start(bf16[256,2816]{1,0:T(8,128)(2,1)S(1)} %fusion.2.a_ref), channel_id=1, source_target_pairs={{0,8},{24,16},{1,9},{25,17},{2,10},{26,18},{3,11},{27,19},{4,12},{... | collective-permute-start | bytes 4325384 | tf_op jit(solution)/shard_map/ppermute | solution.py:948
  497.3 7.4 %collective-permute-done.58.b_ref = bf16[512,1024]{1,0:T(8,128)(2,1)S(1)} collective-permute-done((bf16[512,1024]{1,0:T(8,128)(2,1)S(1)}, bf16[512,1024]{1,0:T(8,128)(2,1)S(1)}, u32[]{:S(2)}, u32[]{:S(2)}) %collective-permute-start.58) | collective-permute-done | bytes 1048608 | tf_op jit(solution)/shard_map/ppermute | solution.py:954
  509.9 13.0 %collective-permute-done.66.b_ref = bf16[256,2816]{1,0:T(8,128)(2,1)S(1)} collective-permute-done((bf16[256,2816]{1,0:T(8,128)(2,1)S(1)}, bf16[256,2816]{1,0:T(8,128)(2,1)S(1)}, u32[]{:S(2)}, u32[]{:S(2)}) %collective-permute-start.66) | collective-permute-done | bytes 1441824 | tf_op jit(solution)/shard_map/ppermute | solution.py:948
  524.1 6.3 collective-permute-start.64
  530.5 14.4 %collective-permute-start.72 = (bf16[128,2816]{1,0:T(8,128)(2,1)S(1)}, bf16[128,2816]{1,0:T(8,128)(2,1)S(1)}, u32[]{:S(2)}, u32[]{:S(2)}) collective-permute-start(bf16[128,2816]{1,0:T(8,128)(2,1)S(1)} %fusion.3.a_ref), channel_id=1, source_target_pairs={{0,8},{24,16},{1,9},{25,17},{2,10},{26,18},{3,11},{27,19},{4,12},{... | collective-permute-start | bytes 2162696 | tf_op jit(solution)/shard_map/ppermute | solution.py:948
  550.3 5.3 collective-permute-done.72.b_ref
  557.6 17.6 %collective-permute-start.68 = (bf16[128,2816]{1,0:T(8,128)(2,1)S(1)}, bf16[128,2816]{1,0:T(8,128)(2,1)S(1)}, u32[]{:S(2)}, u32[]{:S(2)}) collective-permute-start(bf16[128,2816]{1,0:T(8,128)(2,1)S(1)} %fusion.4.a_ref), channel_id=1, source_target_pairs={{0,8},{24,16},{1,9},{25,17},{2,10},{26,18},{3,11},{27,19},{4,12},{... | collective-permute-start | bytes 2162696 | tf_op jit(solution)/shard_map/ppermute | solution.py:948
  578.5 4.2 copy.25
  582.7 5.7 collective-permute-done.68.b_ref
  590.9 14.7 %collective-permute-done.75.b_ref = bf16[256,2816]{1,0:T(8,128)(2,1)S(1)} collective-permute-done((bf16[256,2816]{1,0:T(8,128)(2,1)S(1)}, bf16[256,2816]{1,0:T(8,128)(2,1)S(1)}, u32[]{:S(2)}, u32[]{:S(2)}) %collective-permute-start.75) | collective-permute-done | bytes 1441824 | tf_op jit(solution)/shard_map/ppermute | solution.py:954
  617.3 5.9 shard_map.193
  623.3 7.8 %shard_map.194 = f32[1024,2048]{1,0:T(8,128)} custom-call(s32[3]{0:T(128)S(1)} %pad_add_fusion.2.p, f32[1024,2048]{1,0:T(8,128)S(1)} %bitcast.81, f32[1024,2048]{1,0:T(8,128)S(1)} %bitcast.82, bf16[1024,2048]{1,0:T(8,128)(2,1)S(1)} %copy-done.24, f32[1,2048]{1,0:T(1,128)S(1)} %copy-done.50, bf16[512,2048]{1,0:T(8,128)(2,1)S(1)} %copy-done.16, ...), custom_call_target="tpu_custom_call" | custom-call | flops 3000000000 | bytes 8000000 | tf_op jit(solution)/shard_map/pallas_call | solution.py:860
  (486 shorter events, 248.7 us)
Async XLA Ops:
  10.2 32.0 %collective-permute-start.1 = (bf16[1024,640]{1,0:T(8,128)(2,1)}, bf16[1024,640]{1,0:T(8,128)(2,1)}, u32[]{:S(2)}, u32[]{:S(2)}) collective-permute-start(bf16[1024,640]{1,0:T(8,128)(2,1)} %bitcast.109), channel_id=1, source_target_pairs={{0,4},{4,0},{1,5},{5,1},{2,6},{6,2},{3,7},{7,3},{8,12},{12,8},{9,1... | collective-permute-start | bytes 3932168 | tf_op jit(solution)/shard_map/ppermute | solution.py:936
  11.3 44.5 %collective-permute-start.3 = (bf16[512,512]{1,0:T(8,128)(2,1)S(1)}, bf16[512,512]{1,0:T(8,128)(2,1)}, u32[]{:S(2)}, u32[]{:S(2)}) collective-permute-start(bf16[512,512]{1,0:T(8,128)(2,1)S(1)} %dynamic-slice_bitcast_fusion), channel_id=1, source_target_pairs={{0,4},{4,0},{1,5},{5,1},{2,6},{6,2},{3,7},{7,3},{8,12},{12,8},{9,1... | collective-permute-start | bytes 1572872 | tf_op jit(solution)/shard_map/ppermute | solution.py:936
  79.0 35.3 %collective-permute-start.9 = (bf16[256,2816]{1,0:T(8,128)(2,1)}, bf16[256,2816]{1,0:T(8,128)(2,1)}, u32[]{:S(2)}, u32[]{:S(2)}) collective-permute-start(bf16[256,2816]{1,0:T(8,128)(2,1)} %shard_map.142.refs_9_.refs_1_), channel_id=1, source_target_pairs={{0,4},{4,0},{1,5},{5,1},{2,6},{6,2},{3,7},{7,3},{8,12},{12,8},{9,1... | collective-permute-start | bytes 4325384 | tf_op jit(solution)/shard_map/ppermute | solution.py:936
  100.6 30.2 %collective-permute-start.14 = (bf16[128,2816]{1,0:T(8,128)(2,1)}, bf16[128,2816]{1,0:T(8,128)(2,1)S(1)}, u32[]{:S(2)}, u32[]{:S(2)}) collective-permute-start(bf16[128,2816]{1,0:T(8,128)(2,1)} %collective-permute-done.5.refs_14_), channel_id=1, source_target_pairs={{0,8},{8,0},{16,24},{24,16},{1,9},{9,1},{17,25},{25,17},{2,10},{10... | collective-permute-start | bytes 2162696 | tf_op jit(solution)/shard_map/ppermute | solution.py:945
  104.0 27.3 %collective-permute-start.15 = (bf16[128,2816]{1,0:T(8,128)(2,1)S(1)}, bf16[128,2816]{1,0:T(8,128)(2,1)S(1)}, u32[]{:S(2)}, u32[]{:S(2)}) collective-permute-start(bf16[128,2816]{1,0:T(8,128)(2,1)S(1)} %get-tuple-element.518.refs_10_), channel_id=1, source_target_pairs={{0,4},{4,0},{1,5},{5,1},{2,6},{6,2},{3,7},{7,3},{8,12},{12,8},{9,1... | collective-permute-start | bytes 2162696 | tf_op jit(solution)/shard_map/ppermute | solution.py:936
  108.7 36.4 %collective-permute-start.20 = (bf16[128,2816]{1,0:T(8,128)(2,1)S(1)}, bf16[128,2816]{1,0:T(8,128)(2,1)S(1)}, u32[]{:S(2)}, u32[]{:S(2)}) collective-permute-start(bf16[128,2816]{1,0:T(8,128)(2,1)S(1)} %get-tuple-element.519.refs_11_), channel_id=1, source_target_pairs={{0,4},{4,0},{1,5},{5,1},{2,6},{6,2},{3,7},{7,3},{8,12},{12,8},{9,1... | collective-permute-start | bytes 2162696 | tf_op jit(solution)/shard_map/ppermute | solution.py:936
  117.3 50.5 %collective-permute-start.19 = (bf16[256,2816]{1,0:T(8,128)(2,1)}, bf16[256,2816]{1,0:T(8,128)(2,1)}, u32[]{:S(2)}, u32[]{:S(2)}) collective-permute-start(bf16[256,2816]{1,0:T(8,128)(2,1)} %collective-permute-done.9.refs_15_.refs_5_), channel_id=1, source_target_pairs={{0,8},{8,0},{16,24},{24,16},{1,9},{9,1},{17,25},{25,17},{2,10},{10... | collective-permute-start | bytes 4325384 | tf_op jit(solution)/shard_map/ppermute | solution.py:945
  131.3 29.2 %collective-permute-start.21 = (bf16[1408,256]{1,0:T(8,128)(2,1)S(1)}, bf16[1408,256]{1,0:T(8,128)(2,1)}, u32[]{:S(2)}, u32[]{:S(2)}) collective-permute-start(bf16[1408,256]{1,0:T(8,128)(2,1)S(1)} %get-tuple-element.482), channel_id=1, source_target_pairs={{0,4},{4,0},{1,5},{5,1},{2,6},{6,2},{3,7},{7,3},{8,12},{12,8},{9,1... | collective-permute-start | bytes 2162696 | tf_op jit(solution)/shard_map/ppermute | solution.py:936
  163.9 33.0 %collective-permute-start.23 = (bf16[1408,256]{1,0:T(8,128)(2,1)}, bf16[1408,256]{1,0:T(8,128)(2,1)S(1)}, u32[]{:S(2)}, u32[]{:S(2)}) collective-permute-start(bf16[1408,256]{1,0:T(8,128)(2,1)} %get-tuple-element.506), channel_id=1, source_target_pairs={{0,4},{4,0},{1,5},{5,1},{2,6},{6,2},{3,7},{7,3},{8,12},{12,8},{9,1... | collective-permute-start | bytes 2162696 | tf_op jit(solution)/shard_map/ppermute | solution.py:936
  165.7 33.0 %collective-permute-start.24 = (bf16[1408,256]{1,0:T(8,128)(2,1)}, bf16[1408,256]{1,0:T(8,128)(2,1)}, u32[]{:S(2)}, u32[]{:S(2)}) collective-permute-start(bf16[1408,256]{1,0:T(8,128)(2,1)} %get-tuple-element.507), channel_id=1, source_target_pairs={{0,4},{4,0},{1,5},{5,1},{2,6},{6,2},{3,7},{7,3},{8,12},{12,8},{9,1... | collective-permute-start | bytes 2162696 | tf_op jit(solution)/shard_map/ppermute | solution.py:936
  166.0 32.7 %collective-permute-start.22 = (bf16[1408,256]{1,0:T(8,128)(2,1)}, bf16[1408,256]{1,0:T(8,128)(2,1)}, u32[]{:S(2)}, u32[]{:S(2)}) collective-permute-start(bf16[1408,256]{1,0:T(8,128)(2,1)} %collective-permute-done.21.refs_1_), channel_id=1, source_target_pairs={{0,8},{8,0},{16,24},{24,16},{1,9},{9,1},{17,25},{25,17},{2,10},{10... | collective-permute-start | bytes 2162696 | tf_op jit(solution)/shard_map/ppermute | solution.py:945
  191.6 44.0 %collective-permute-start.27 = (bf16[768,1024]{1,0:T(8,128)(2,1)}, bf16[768,1024]{1,0:T(8,128)(2,1)S(1)}, u32[]{:S(2)}, u32[]{:S(2)}) collective-permute-start(bf16[768,1024]{1,0:T(8,128)(2,1)} %fusion.17), channel_id=1, source_target_pairs={{0,4},{4,0},{1,5},{5,1},{2,6},{6,2},{3,7},{7,3},{8,12},{12,8},{9,1... | collective-permute-start | bytes 4718600 | tf_op jit(solution)/shard_map/ppermute | solution.py:936
  233.9 31.6 %collective-permute-start.25 = (bf16[640,1024]{1,0:T(8,128)(2,1)S(1)}, bf16[640,1024]{1,0:T(8,128)(2,1)S(1)}, u32[]{:S(2)}, u32[]{:S(2)}) collective-permute-start(bf16[640,1024]{1,0:T(8,128)(2,1)S(1)} %fusion.20), channel_id=1, source_target_pairs={{0,4},{4,0},{1,5},{5,1},{2,6},{6,2},{3,7},{7,3},{8,12},{12,8},{9,1... | collective-permute-start | bytes 3932168 | tf_op jit(solution)/shard_map/ppermute | solution.py:936
  238.6 43.2 %collective-permute-start.31 = (bf16[768,1024]{1,0:T(8,128)(2,1)}, bf16[768,1024]{1,0:T(8,128)(2,1)}, u32[]{:S(2)}, u32[]{:S(2)}) collective-permute-start(bf16[768,1024]{1,0:T(8,128)(2,1)} %add_convert_fusion.a_ref), channel_id=1, source_target_pairs={{0,8},{24,16},{1,9},{25,17},{2,10},{26,18},{3,11},{27,19},{4,12},{... | collective-permute-start | bytes 4718600 | tf_op jit(solution)/shard_map/ppermute | solution.py:948
  249.9 56.0 %collective-permute-start.40 = (bf16[256,2816]{1,0:T(8,128)(2,1)}, bf16[256,2816]{1,0:T(8,128)(2,1)}, u32[]{:S(2)}, u32[]{:S(2)}) collective-permute-start(bf16[256,2816]{1,0:T(8,128)(2,1)} %convolution_convert_fusion.2), channel_id=1, source_target_pairs={{0,4},{4,0},{1,5},{5,1},{2,6},{6,2},{3,7},{7,3},{8,12},{12,8},{9,1... | collective-permute-start | bytes 4325384 | tf_op jit(solution)/shard_map/ppermute | solution.py:936
  281.8 29.8 %collective-permute-start.38 = (bf16[128,2048]{1,0:T(8,128)(2,1)}, bf16[128,2048]{1,0:T(8,128)(2,1)S(1)}, u32[]{:S(2)}, u32[]{:S(2)}) collective-permute-start(bf16[128,2048]{1,0:T(8,128)(2,1)} %get-tuple-element.606.refs_0_), channel_id=1, source_target_pairs={{0,1},{1,0},{2,3},{3,2},{4,5},{5,4},{6,7},{7,6},{8,9},{9,8},{10,11... | collective-permute-start | bytes 1572872 | tf_op jit(solution)/shard_map/ppermute | solution.py:939
  285.3 53.9 %collective-permute-start.30 = (bf16[640,1024]{1,0:T(8,128)(2,1)S(1)}, bf16[640,1024]{1,0:T(8,128)(2,1)S(1)}, u32[]{:S(2)}, u32[]{:S(2)}) collective-permute-start(bf16[640,1024]{1,0:T(8,128)(2,1)S(1)} %copy-done.62), channel_id=1, source_target_pairs={{0,8},{24,16},{1,9},{25,17},{2,10},{26,18},{3,11},{27,19},{4,12},{... | collective-permute-start | bytes 3932168 | tf_op jit(solution)/shard_map/ppermute | solution.py:948
  291.5 41.2 %collective-permute-start.33 = (bf16[768,1024]{1,0:T(8,128)(2,1)S(1)}, bf16[768,1024]{1,0:T(8,128)(2,1)S(1)}, u32[]{:S(2)}, u32[]{:S(2)}) collective-permute-start(bf16[768,1024]{1,0:T(8,128)(2,1)S(1)} %shard_map.160.a_ref), channel_id=1, source_target_pairs={{8,16},{16,8},{9,17},{17,9},{10,18},{18,10},{11,19},{19,11},{12,20... | collective-permute-start | bytes 4718600 | tf_op jit(solution)/shard_map/ppermute | solution.py:951
  305.9 52.7 %collective-permute-start.41 = (bf16[128,512]{1,0:T(8,128)(2,1)S(1)}, bf16[128,512]{1,0:T(8,128)(2,1)S(1)}, u32[]{:S(2)}, u32[]{:S(2)}) collective-permute-start(bf16[128,512]{1,0:T(8,128)(2,1)S(1)} %get-tuple-element.601), channel_id=1, source_target_pairs={{4,0},{5,1},{6,2},{7,3},{12,8},{13,9},{14,10},{15,11},{20,16},{21,... | collective-permute-start | bytes 393224 | tf_op jit(solution)/shard_map/ppermute | solution.py:1242
  311.6 62.3 %collective-permute-start.46 = (bf16[256,2816]{1,0:T(8,128)(2,1)}, bf16[256,2816]{1,0:T(8,128)(2,1)}, u32[]{:S(2)}, u32[]{:S(2)}) collective-permute-start(bf16[256,2816]{1,0:T(8,128)(2,1)} %fusion.a_ref), channel_id=1, source_target_pairs={{0,8},{24,16},{1,9},{25,17},{2,10},{26,18},{3,11},{27,19},{4,12},{... | collective-permute-start | bytes 4325384 | tf_op jit(solution)/shard_map/ppermute | solution.py:948
  328.4 28.5 %collective-permute-start.42 = (bf16[128,512]{1,0:T(8,128)(2,1)S(1)}, bf16[128,512]{1,0:T(8,128)(2,1)S(1)}, u32[]{:S(2)}, u32[]{:S(2)}) collective-permute-start(bf16[128,512]{1,0:T(8,128)(2,1)S(1)} %get-tuple-element.624), channel_id=1, source_target_pairs={{4,0},{5,1},{6,2},{7,3},{12,8},{13,9},{14,10},{15,11},{20,16},{21,... | collective-permute-start | bytes 393224 | tf_op jit(solution)/shard_map/ppermute | solution.py:1242
  332.7 45.2 %collective-permute-start.45 = (bf16[512,1024]{1,0:T(8,128)(2,1)}, bf16[512,1024]{1,0:T(8,128)(2,1)}, u32[]{:S(2)}, u32[]{:S(2)}) collective-permute-start(bf16[512,1024]{1,0:T(8,128)(2,1)} %add_convert_fusion.4), channel_id=1, source_target_pairs={{0,4},{4,0},{1,5},{5,1},{2,6},{6,2},{3,7},{7,3},{8,12},{12,8},{9,1... | collective-permute-start | bytes 3145736 | tf_op jit(solution)/shard_map/ppermute | solution.py:936
  339.1 60.0 %collective-permute-start.44 = (bf16[768,1024]{1,0:T(8,128)(2,1)}, bf16[768,1024]{1,0:T(8,128)(2,1)}, u32[]{:S(2)}, u32[]{:S(2)}) collective-permute-start(bf16[768,1024]{1,0:T(8,128)(2,1)} %shard_map.165.a_ref), channel_id=1, source_target_pairs={{8,0},{16,24},{9,1},{17,25},{10,2},{18,26},{11,3},{19,27},{12,4},{... | collective-permute-start | bytes 4718600 | tf_op jit(solution)/shard_map/ppermute | solution.py:954
  356.9 50.0 %collective-permute-start.43 = (bf16[640,1024]{1,0:T(8,128)(2,1)}, bf16[640,1024]{1,0:T(8,128)(2,1)}, u32[]{:S(2)}, u32[]{:S(2)}) collective-permute-start(bf16[640,1024]{1,0:T(8,128)(2,1)} %shard_map.166.a_ref), channel_id=1, source_target_pairs={{8,16},{16,8},{9,17},{17,9},{10,18},{18,10},{11,19},{19,11},{12,20... | collective-permute-start | bytes 3932168 | tf_op jit(solution)/shard_map/ppermute | solution.py:951
  363.9 53.1 %collective-permute-start.49 = (bf16[256,2816]{1,0:T(8,128)(2,1)}, bf16[256,2816]{1,0:T(8,128)(2,1)}, u32[]{:S(2)}, u32[]{:S(2)}) collective-permute-start(bf16[256,2816]{1,0:T(8,128)(2,1)} %convolution_convert_fusion.1), channel_id=1, source_target_pairs={{0,4},{4,0},{1,5},{5,1},{2,6},{6,2},{3,7},{7,3},{8,12},{12,8},{9,1... | collective-permute-start | bytes 4325384 | tf_op jit(solution)/shard_map/ppermute | solution.py:936
  383.3 45.4 %collective-permute-start.48 = (bf16[512,1024]{1,0:T(8,128)(2,1)}, bf16[512,1024]{1,0:T(8,128)(2,1)}, u32[]{:S(2)}, u32[]{:S(2)}) collective-permute-start(bf16[512,1024]{1,0:T(8,128)(2,1)} %add_convert_fusion.3.a_ref), channel_id=1, source_target_pairs={{0,8},{24,16},{1,9},{25,17},{2,10},{26,18},{3,11},{27,19},{4,12},{... | collective-permute-start | bytes 3145736 | tf_op jit(solution)/shard_map/ppermute | solution.py:948
  394.3 38.2 %collective-permute-start.47 = (bf16[256,2816]{1,0:T(8,128)(2,1)}, bf16[256,2816]{1,0:T(8,128)(2,1)}, u32[]{:S(2)}, u32[]{:S(2)}) collective-permute-start(bf16[256,2816]{1,0:T(8,128)(2,1)} %shard_map.170.a_ref), channel_id=1, source_target_pairs={{8,16},{16,8},{9,17},{17,9},{10,18},{18,10},{11,19},{19,11},{12,20... | collective-permute-start | bytes 4325384 | tf_op jit(solution)/shard_map/ppermute | solution.py:951
  399.2 51.3 %collective-permute-start.56 = (bf16[1024,640]{1,0:T(8,128)(2,1)}, bf16[1024,640]{1,0:T(8,128)(2,1)}, u32[]{:S(2)}, u32[]{:S(2)}) collective-permute-start(bf16[1024,640]{1,0:T(8,128)(2,1)} %fusion.23), channel_id=1, source_target_pairs={{0,4},{4,0},{1,5},{5,1},{2,6},{6,2},{3,7},{7,3},{8,12},{12,8},{9,1... | collective-permute-start | bytes 3932168 | tf_op jit(solution)/shard_map/ppermute | solution.py:936
  411.7 43.1 %collective-permute-start.55 = (bf16[640,1024]{1,0:T(8,128)(2,1)}, bf16[640,1024]{1,0:T(8,128)(2,1)}, u32[]{:S(2)}, u32[]{:S(2)}) collective-permute-start(bf16[640,1024]{1,0:T(8,128)(2,1)} %shard_map.172.a_ref), channel_id=1, source_target_pairs={{8,0},{16,24},{9,1},{17,25},{10,2},{18,26},{11,3},{19,27},{12,4},{... | collective-permute-start | bytes 3932168 | tf_op jit(solution)/shard_map/ppermute | solution.py:954
  417.0 194.7 %all-reduce.4.cloned.1.call-start = ((), (), s32[]{:S(2)}) async-start(), calls=%async_computation | async-start | bytes 16777216 | tf_op jit(solution)/shard_map/psum | solution.py:1266
  422.0 43.6 %collective-permute-start.54 = (bf16[256,2816]{1,0:T(8,128)(2,1)S(1)}, bf16[256,2816]{1,0:T(8,128)(2,1)}, u32[]{:S(2)}, u32[]{:S(2)}) collective-permute-start(bf16[256,2816]{1,0:T(8,128)(2,1)S(1)} %fusion.1.a_ref), channel_id=1, source_target_pairs={{0,8},{24,16},{1,9},{25,17},{2,10},{26,18},{3,11},{27,19},{4,12},{... | collective-permute-start | bytes 4325384 | tf_op jit(solution)/shard_map/ppermute | solution.py:948
  436.5 37.8 %collective-permute-start.52 = (bf16[256,2816]{1,0:T(8,128)(2,1)}, bf16[256,2816]{1,0:T(8,128)(2,1)}, u32[]{:S(2)}, u32[]{:S(2)}) collective-permute-start(bf16[256,2816]{1,0:T(8,128)(2,1)} %shard_map.175.a_ref), channel_id=1, source_target_pairs={{8,0},{16,24},{9,1},{17,25},{10,2},{18,26},{11,3},{19,27},{12,4},{... | collective-permute-start | bytes 4325384 | tf_op jit(solution)/shard_map/ppermute | solution.py:954
  450.5 34.8 %collective-permute-start.61 = (bf16[256,2816]{1,0:T(8,128)(2,1)}, bf16[256,2816]{1,0:T(8,128)(2,1)S(1)}, u32[]{:S(2)}, u32[]{:S(2)}) collective-permute-start(bf16[256,2816]{1,0:T(8,128)(2,1)} %convolution_convert_fusion), channel_id=1, source_target_pairs={{0,4},{4,0},{1,5},{5,1},{2,6},{6,2},{3,7},{7,3},{8,12},{12,8},{9,1... | collective-permute-start | bytes 4325384 | tf_op jit(solution)/shard_map/ppermute | solution.py:936
  454.8 33.5 %collective-permute-start.60 = (bf16[1024,640]{1,0:T(8,128)(2,1)S(1)}, bf16[1024,640]{1,0:T(8,128)(2,1)S(1)}, u32[]{:S(2)}, u32[]{:S(2)}) collective-permute-start(bf16[1024,640]{1,0:T(8,128)(2,1)S(1)} %add_convert_fusion.1.a_ref), channel_id=1, source_target_pairs={{0,8},{24,16},{1,9},{25,17},{2,10},{26,18},{3,11},{27,19},{4,12},{... | collective-permute-start | bytes 3932168 | tf_op jit(solution)/shard_map/ppermute | solution.py:948
  467.9 28.3 %collective-permute-start.59 = (bf16[256,2816]{1,0:T(8,128)(2,1)S(1)}, bf16[256,2816]{1,0:T(8,128)(2,1)S(1)}, u32[]{:S(2)}, u32[]{:S(2)}) collective-permute-start(bf16[256,2816]{1,0:T(8,128)(2,1)S(1)} %shard_map.177.a_ref), channel_id=1, source_target_pairs={{8,16},{16,8},{9,17},{17,9},{10,18},{18,10},{11,19},{19,11},{12,20... | collective-permute-start | bytes 4325384 | tf_op jit(solution)/shard_map/ppermute | solution.py:951
  471.5 33.2 %collective-permute-start.58 = (bf16[512,1024]{1,0:T(8,128)(2,1)S(1)}, bf16[512,1024]{1,0:T(8,128)(2,1)S(1)}, u32[]{:S(2)}, u32[]{:S(2)}) collective-permute-start(bf16[512,1024]{1,0:T(8,128)(2,1)S(1)} %shard_map.178.a_ref), channel_id=1, source_target_pairs={{8,0},{16,24},{9,1},{17,25},{10,2},{18,26},{11,3},{19,27},{12,4},{... | collective-permute-start | bytes 3145736 | tf_op jit(solution)/shard_map/ppermute | solution.py:954
  479.3 29.6 %collective-permute-start.67 = (bf16[128,2816]{1,0:T(8,128)(2,1)S(1)}, bf16[128,2816]{1,0:T(8,128)(2,1)S(1)}, u32[]{:S(2)}, u32[]{:S(2)}) collective-permute-start(bf16[128,2816]{1,0:T(8,128)(2,1)S(1)} %convolution_convert_fusion.4), channel_id=1, source_target_pairs={{0,4},{4,0},{1,5},{5,1},{2,6},{6,2},{3,7},{7,3},{8,12},{12,8},{9,1... | collective-permute-start | bytes 2162696 | tf_op jit(solution)/shard_map/ppermute | solution.py:936
  488.4 34.6 %collective-permute-start.66 = (bf16[256,2816]{1,0:T(8,128)(2,1)S(1)}, bf16[256,2816]{1,0:T(8,128)(2,1)S(1)}, u32[]{:S(2)}, u32[]{:S(2)}) collective-permute-start(bf16[256,2816]{1,0:T(8,128)(2,1)S(1)} %fusion.2.a_ref), channel_id=1, source_target_pairs={{0,8},{24,16},{1,9},{25,17},{2,10},{26,18},{3,11},{27,19},{4,12},{... | collective-permute-start | bytes 4325384 | tf_op jit(solution)/shard_map/ppermute | solution.py:948
  496.1 34.4 %collective-permute-start.65 = (bf16[1024,640]{1,0:T(8,128)(2,1)S(1)}, bf16[1024,640]{1,0:T(8,128)(2,1)S(1)}, u32[]{:S(2)}, u32[]{:S(2)}) collective-permute-start(bf16[1024,640]{1,0:T(8,128)(2,1)S(1)} %shard_map.180.a_ref), channel_id=1, source_target_pairs={{8,16},{16,8},{9,17},{17,9},{10,18},{18,10},{11,19},{19,11},{12,20... | collective-permute-start | bytes 3932168 | tf_op jit(solution)/shard_map/ppermute | solution.py:951
  504.7 41.9 %collective-permute-start.63 = (bf16[256,2816]{1,0:T(8,128)(2,1)S(1)}, bf16[256,2816]{1,0:T(8,128)(2,1)S(1)}, u32[]{:S(2)}, u32[]{:S(2)}) collective-permute-start(bf16[256,2816]{1,0:T(8,128)(2,1)S(1)} %shard_map.181.a_ref), channel_id=1, source_target_pairs={{8,0},{16,24},{9,1},{17,25},{10,2},{18,26},{11,3},{19,27},{12,4},{... | collective-permute-start | bytes 4325384 | tf_op jit(solution)/shard_map/ppermute | solution.py:954
  508.8 40.5 %collective-permute-start.62 = (bf16[128,2816]{1,0:T(8,128)(2,1)S(1)}, bf16[128,2816]{1,0:T(8,128)(2,1)S(1)}, u32[]{:S(2)}, u32[]{:S(2)}) collective-permute-start(bf16[128,2816]{1,0:T(8,128)(2,1)S(1)} %convolution_convert_fusion.3), channel_id=1, source_target_pairs={{0,4},{4,0},{1,5},{5,1},{2,6},{6,2},{3,7},{7,3},{8,12},{12,8},{9,1... | collective-permute-start | bytes 2162696 | tf_op jit(solution)/shard_map/ppermute | solution.py:936
  523.4 32.5 %collective-permute-start.71 = (bf16[256,2816]{1,0:T(8,128)(2,1)S(1)}, bf16[256,2816]{1,0:T(8,128)(2,1)S(1)}, u32[]{:S(2)}, u32[]{:S(2)}) collective-permute-start(bf16[256,2816]{1,0:T(8,128)(2,1)S(1)} %shard_map.183.a_ref), channel_id=1, source_target_pairs={{8,16},{16,8},{9,17},{17,9},{10,18},{18,10},{11,19},{19,11},{12,20... | collective-permute-start | bytes 4325384 | tf_op jit(solution)/shard_map/ppermute | solution.py:951
  530.5 25.1 %collective-permute-start.72 = (bf16[128,2816]{1,0:T(8,128)(2,1)S(1)}, bf16[128,2816]{1,0:T(8,128)(2,1)S(1)}, u32[]{:S(2)}, u32[]{:S(2)}) collective-permute-start(bf16[128,2816]{1,0:T(8,128)(2,1)S(1)} %fusion.3.a_ref), channel_id=1, source_target_pairs={{0,8},{24,16},{1,9},{25,17},{2,10},{26,18},{3,11},{27,19},{4,12},{... | collective-permute-start | bytes 2162696 | tf_op jit(solution)/shard_map/ppermute | solution.py:948
  545.3 32.8 %collective-permute-start.69 = (bf16[1024,640]{1,0:T(8,128)(2,1)S(1)}, bf16[1024,640]{1,0:T(8,128)(2,1)S(1)}, u32[]{:S(2)}, u32[]{:S(2)}) collective-permute-start(bf16[1024,640]{1,0:T(8,128)(2,1)S(1)} %shard_map.184.a_ref), channel_id=1, source_target_pairs={{8,0},{16,24},{9,1},{17,25},{10,2},{18,26},{11,3},{19,27},{12,4},{... | collective-permute-start | bytes 3932168 | tf_op jit(solution)/shard_map/ppermute | solution.py:954
  556.3 49.3 %collective-permute-start.75 = (bf16[256,2816]{1,0:T(8,128)(2,1)S(1)}, bf16[256,2816]{1,0:T(8,128)(2,1)S(1)}, u32[]{:S(2)}, u32[]{:S(2)}) collective-permute-start(bf16[256,2816]{1,0:T(8,128)(2,1)S(1)} %shard_map.187.a_ref), channel_id=1, source_target_pairs={{8,0},{16,24},{9,1},{17,25},{10,2},{18,26},{11,3},{19,27},{12,4},{... | collective-permute-start | bytes 4325384 | tf_op jit(solution)/shard_map/ppermute | solution.py:954
  557.6 30.8 %collective-permute-start.68 = (bf16[128,2816]{1,0:T(8,128)(2,1)S(1)}, bf16[128,2816]{1,0:T(8,128)(2,1)S(1)}, u32[]{:S(2)}, u32[]{:S(2)}) collective-permute-start(bf16[128,2816]{1,0:T(8,128)(2,1)S(1)} %fusion.4.a_ref), channel_id=1, source_target_pairs={{0,8},{24,16},{1,9},{25,17},{2,10},{26,18},{3,11},{27,19},{4,12},{... | collective-permute-start | bytes 2162696 | tf_op jit(solution)/shard_map/ppermute | solution.py:948
  576.6 31.7 %collective-permute-start.74 = (f32[2,1024]{1,0:T(2,128)S(1)}, f32[2,1024]{1,0:T(2,128)S(1)}, u32[]{:S(2)}, u32[]{:S(2)}) collective-permute-start(f32[2,1024]{1,0:T(2,128)S(1)} %add.169), channel_id=1, source_target_pairs={{8,0},{16,24},{9,1},{17,25},{10,2},{18,26},{11,3},{19,27},{12,4},{... | collective-permute-start | bytes 24584 | tf_op jit(solution)/shard_map/ppermute | solution.py:954
  589.6 41.4 %collective-permute-start.78 = (bf16[128,2816]{1,0:T(8,128)(2,1)S(1)}, bf16[128,2816]{1,0:T(8,128)(2,1)S(1)}, u32[]{:S(2)}, u32[]{:S(2)}) collective-permute-start(bf16[128,2816]{1,0:T(8,128)(2,1)S(1)} %shard_map.190.a_ref), channel_id=1, source_target_pairs={{8,0},{16,24},{9,1},{17,25},{10,2},{18,26},{11,3},{19,27},{12,4},{... | collective-permute-start | bytes 2162696 | tf_op jit(solution)/shard_map/ppermute | solution.py:954
  (148 other events, 1428.8 us)
Sparse Core Ops, SparseCore 0:
  449.9 155.4 all-reduce.3

commit v4 on v3

--- a/solution.py
+++ b/solution.py
@@ -1291,11 +1291,12 @@
     go("g4", "g3", "g2", "gain", "qkv")
     go("g4", "g3", "g2", "gain", "g4")
     hidden_out = order(lambda h, d, p: add_columns(h, d, p, quarter), hidden, delta, place)
+    go("g3")
     grad_in = order(
         lambda h, u, d, g, p: first_norm_back(h, u, d, g, p, quarter),
         hidden, d_n1, d2, gains[:1], place,
     )
-    go("g3", "g4")
+    go("g4")
     if two:
         g_qkv, g_out, g_down = results["qkv"][0], results["out"][0], results["down"][0]
         g_gu, gain_own = results["gu"][0], results["gain"][0]

time: 656 us -> 660 us (level)
    unnamed x235 -> x237, local copies, waits for them, and re-layouts: 34.3 us -> 39.2 us
  transfers between devices with their start and end apart: 80 -> 80, of which waited for: 23 -> 21; matrix products, arithmetic and copies ran while one was open for 10% -> 10% of each run, Pallas kernels for 38% -> 38%
where the time goes in v4:
time: 660 us; the launch traced here: 649 us
  Pallas kernels  254 us (38%)
  starting transfers between devices  163 us (25%)
  waiting for transfers between devices  114 us (17%)
  matrix products  47.6 us (7%)
  local copies, waits for them, and re-layouts  45.2 us (7%)
  between operations  16.5 us (2%)
  other arithmetic  9.54 us (1%)
    ppermute x10, starting transfers between devices, hop_in(): return lax.ppermute(x, 'rep', [(0, 1), (3, 2)])  76.3 us
    dot_general x20, matrix products, dot(): lax.dot_general(a, b, (((ca,), (cb,)), ((), ())), preferred_element_type=...  47.6 us
    unnamed x237, local copies, waits for them, and re-layouts  39.2 us
    ppermute x20, waiting for transfers between devices, swap_seq(): return lax.ppermute(x, 'seq', [(0, 1), (1, 0)])  38.5 us
    ppermute x20, starting transfers between devices, swap_seq(): return lax.ppermute(x, 'seq', [(0, 1), (1, 0)])  36.5 us
    pallas_call x3, Pallas kernels, split_matmul(): call(body, (sum(counts),), [pl.BlockSpec((rows, depth), lambda j, p: (0,...  34.8 us
    pallas_call x18, Pallas kernels, add_pair(): call(body, (4,), [spec, spec], spec, jax.ShapeDtypeStruct((rows, cols), B...  32.3 us
    ppermute x10, waiting for transfers between devices, hop_in(): return lax.ppermute(x, 'rep', [(0, 1), (3, 2)])  27.1 us
  transfers between devices with their start and end apart: 80, of which 21 were waited for; matrix products, arithmetic and copies ran while one was open for 10% of the time, Pallas kernels for 38%

profile of v4, /device:TPU:0, one launch (start us, length us, event | category | flops | bytes accessed | tf_op | source)
XLA Modules:
  0.0 648.8 jit_solution(2444703239696597080)
XLA Ops:
  25.8 4.5 shard_map.137
  42.2 5.8 shard_map.141
  50.3 5.5 shard_map.142.refs_9_.refs_1_
  58.6 7.8 %shard_map.144 = (bf16[512,512]{1,0:T(8,128)(2,1)S(1)}, bf16[512,512]{1,0:T(8,128)(2,1)S(1)}, f32[8,512]{1,0:T(8,128)S(1)}) custom-call(s32[6]{0:T(128)S(1)} %pad_add_fusion.3.b_ref, bf16[2,512,512]{2,1,0:T(8,128)(2,1)S(1)} %get-tuple-element.611.q_ref, bf16[2,128,1024]{2,1,0:T(8,128)(2,1)S(1)} %shard_map.143.kv_ref, s32[2,1,512]{2,1,0:T(1,128)S(1)} %broadcast_in_dim.33.st_ref), custom_call_target="tpu_custom_call" | custom-call | flops 3000000000 | bytes 8000000 | tf_op jit(solution)/shard_map/pallas_call | solution.py:250
  70.8 6.5 %shard_map.145 = (bf16[256,2048]{1,0:T(8,128)(2,1)}, f32[256,2048]{1,0:T(8,128)S(1)}) custom-call(s32[3]{0:T(128)S(1)} %pad_add_fusion.2.p, bf16[512,512]{1,0:T(8,128)(2,1)S(1)} %get-tuple-element.659.a_ref, bf16[512,1024]{1,0:T(8,128)(2,1)S(1)} %bitcast.97, bf16[512,512]{1,0:T(8,128)(2,1)} %collective-permute-done.3.refs_1_, ...), custom_call_target="tpu_custom_call" | custom-call | flops 3000000000 | bytes 8000000 | tf_op jit(solution)/shard_map/pallas_call | solution.py:733
  84.1 7.8 %shard_map.146 = (bf16[512,512]{1,0:T(8,128)(2,1)S(1)}, bf16[512,512]{1,0:T(8,128)(2,1)S(1)}, f32[8,512]{1,0:T(8,128)S(1)}) custom-call(s32[6]{0:T(128)S(1)} %pad_add_fusion.5.b_ref, bf16[2,512,512]{2,1,0:T(8,128)(2,1)S(1)} %copy-done.78, bf16[2,128,1024]{2,1,0:T(8,128)(2,1)S(1)} %copy-done.83, s32[2,1,512]{2,1,0:T(1,128)S(1)} %broadcast_in_dim.33.st_ref), custom_call_target="tpu_custom_call" | custom-call | flops 3000000000 | bytes 8000000 | tf_op jit(solution)/shard_map/pallas_call | solution.py:250
  94.7 5.8 shard_map.148
  104.0 4.7 collective-permute-start.15
  109.4 5.2 collective-permute-done.9.refs_15_.refs_5_
  123.0 6.5 shard_map.151
  131.3 4.7 collective-permute-start.21
  141.0 4.3 collective-permute-done.20.refs_19_
  146.7 14.0 %collective-permute-done.21.refs_1_ = bf16[1408,256]{1,0:T(8,128)(2,1)} collective-permute-done((bf16[1408,256]{1,0:T(8,128)(2,1)S(1)}, bf16[1408,256]{1,0:T(8,128)(2,1)}, u32[]{:S(2)}, u32[]{:S(2)}) %collective-permute-start.21) | collective-permute-done | bytes 720928 | tf_op jit(solution)/shard_map/ppermute | solution.py:936
  167.8 20.3 %shard_map.153 = (bf16[1024,2048]{1,0:T(8,128)(2,1)S(1)}, bf16[1024,1408]{1,0:T(8,128)(2,1)S(1)}, bf16[1024,2816]{1,0:T(8,128)(2,1)}) custom-call(s32[3]{0:T(128)S(1)} %pad_add_fusion.2.p, bf16[128,2048]{1,0:T(8,128)(2,1)} %get-tuple-element.484.refs_0_, bf16[128,2048]{1,0:T(8,128)(2,1)} %collective-permute-done.10.refs_1_, ...), custom_call_target="tpu_custom_call" | custom-call | flops 3000000000 | bytes 8000000 | tf_op jit(solution)/shard_map/pallas_call | solution.py:629
  199.0 12.1 %shard_map.154.a_ref = bf16[1024,2816]{1,0:T(8,128)(2,1)S(1)} custom-call(s32[3]{0:T(128)S(1)} %pad_add_fusion.2.p, bf16[1024,2048]{1,0:T(8,128)(2,1)S(1)} %copy-done.9, bf16[1024,2816]{1,0:T(8,128)(2,1)S(1)} %bitcast.95, bf16[1408,1024]{1,0:T(8,128)(2,1)S(1)} %bitcast.92, bf16[1408,256]{1,0:T(8,128)(2,1)} %collective-permute-done.21.refs_1_, ...), custom_call_target="tpu_custom_call" | custom-call | flops 3000000000 | bytes 8000000 | tf_op jit(solution)/shard_map/pallas_call | solution.py:673
  211.1 22.4 %shard_map.155 = (bf16[256,2048]{1,0:T(8,128)(2,1)S(1)}, f32[256,2048]{1,0:T(8,128)S(1)}, bf16[256,2048]{1,0:T(8,128)(2,1)S(1)}, f32[256,2048]{1,0:T(8,128)S(1)}) custom-call(s32[3]{0:T(128)S(1)} %pad_add_fusion.2.p, bf16[1024,2816]{1,0:T(8,128)(2,1)S(1)} %shard_map.154.a_ref, bf16[256,2816]{1,0:T(8,128)(2,1)S(1)} %pad_maximum_fusion.refs_0_, ...), custom_call_target="tpu_custom_call" | custom-call | flops 3000000000 | bytes 8000000 | tf_op jit(solution)/shard_map/pallas_call | solution.py:733
  238.8 4.7 collective-permute-start.31
  250.2 9.1 %collective-permute-done.28.refs_2_ = bf16[128,2048]{1,0:T(8,128)(2,1)S(1)} collective-permute-done((bf16[128,2048]{1,0:T(8,128)(2,1)S(1)}, bf16[128,2048]{1,0:T(8,128)(2,1)S(1)}, u32[]{:S(2)}, u32[]{:S(2)}) %collective-permute-start.28) | collective-permute-done | bytes 524320 | tf_op jit(solution)/shard_map/ppermute | solution.py:942
  275.2 6.6 %collective-permute-done.34.refs_1_ = bf16[128,2048]{1,0:T(8,128)(2,1)} collective-permute-done((bf16[128,2048]{1,0:T(8,128)(2,1)}, bf16[128,2048]{1,0:T(8,128)(2,1)}, u32[]{:S(2)}, u32[]{:S(2)}) %collective-permute-start.34) | collective-permute-done | bytes 524320 | tf_op jit(solution)/shard_map/ppermute | solution.py:942
  286.9 4.6 collective-permute-done.37.refs_1_
  295.1 10.8 %shard_map.162 = (bf16[512,512]{1,0:T(8,128)(2,1)S(1)}, f32[128,1024]{1,0:T(8,128)S(1)}, bf16[128,512]{1,0:T(8,128)(2,1)S(1)}) custom-call(s32[6]{0:T(128)S(1)} %copy-done.57, bf16[2,512,512]{2,1,0:T(8,128)(2,1)S(1)} %copy-done.79, bf16[2,128,1024]{2,1,0:T(8,128)(2,1)S(1)} %copy-done.84, s32[2,1,512]{2,1,0:T(1,128)S(1)} %broadcast_in_dim.33.st_ref, ...), custom_call_target="tpu_custom_call" | custom-call | flops 3000000000 | bytes 8000000 | tf_op jit(solution)/shard_map/pallas_call | solution.py:347
  307.2 4.4 fusion.a_ref
  311.6 4.4 collective-permute-start.46
  318.1 10.3 %shard_map.164 = (bf16[512,512]{1,0:T(8,128)(2,1)S(1)}, f32[128,1024]{1,0:T(8,128)S(1)}, bf16[128,512]{1,0:T(8,128)(2,1)S(1)}) custom-call(s32[6]{0:T(128)S(1)} %copy-done.59, bf16[2,512,512]{2,1,0:T(8,128)(2,1)S(1)} %copy-done.79, bf16[2,128,1024]{2,1,0:T(8,128)(2,1)S(1)} %copy-done.84, s32[2,1,512]{2,1,0:T(1,128)S(1)} %broadcast_in_dim.33.st_ref, ...), custom_call_target="tpu_custom_call" | custom-call | flops 3000000000 | bytes 8000000 | tf_op jit(solution)/shard_map/pallas_call | solution.py:347
  332.8 8.9 %collective-permute-start.45 = (bf16[512,1024]{1,0:T(8,128)(2,1)}, bf16[512,1024]{1,0:T(8,128)(2,1)}, u32[]{:S(2)}, u32[]{:S(2)}) collective-permute-start(bf16[512,1024]{1,0:T(8,128)(2,1)} %add_convert_fusion.4), channel_id=1, source_target_pairs={{0,4},{4,0},{1,5},{5,1},{2,6},{6,2},{3,7},{7,3},{8,12},{12,8},{9,1... | collective-permute-start | bytes 3145736 | tf_op jit(solution)/shard_map/ppermute | solution.py:936
  346.8 12.4 %shard_map.167 = bf16[1024,2048]{1,0:T(8,128)(2,1)S(1)} custom-call(s32[3]{0:T(128)S(1)} %pad_add_fusion.2.p, bf16[1024,1408]{1,0:T(8,128)(2,1)S(1)} %copy-done.35, bf16[1408,1024]{1,0:T(8,128)(2,1)S(1)} %bitcast.93, bf16[1408,256]{1,0:T(8,128)(2,1)} %collective-permute-done.21.refs_1_, bf16[1408,256]{1,0:T(8,128)(2,1)} %collective-permute-done.22.refs_2_, ...), custom_call_target="tpu_custom_call" | custom-call | flops 3000000000 | bytes 8000000 | tf_op jit(solution)/shard_map/pallas_call | solution.py:791
  363.9 4.4 convolution_convert_fusion.1
  368.3 8.0 %shard_map.169.u_ref = bf16[1024,2048]{1,0:T(8,128)(2,1)S(1)} custom-call(s32[3]{0:T(128)S(1)} %pad_add_fusion.2.p, bf16[1024,640]{1,0:T(8,128)(2,1)S(1)} %shard_map.168.a_ref, bf16[1024,640]{1,0:T(8,128)(2,1)S(1)} %bitcast.111, bf16[1024,640]{1,0:T(8,128)(2,1)} %collective-permute-done.1.refs_1_), custom_call_target="tpu_custom_call" | custom-call | flops 3000000000 | bytes 8000000 | tf_op jit(solution)/shard_map/pallas_call | solution.py:791
  387.7 7.3 %collective-permute-start.48 = (bf16[512,1024]{1,0:T(8,128)(2,1)}, bf16[512,1024]{1,0:T(8,128)(2,1)}, u32[]{:S(2)}, u32[]{:S(2)}) collective-permute-start(bf16[512,1024]{1,0:T(8,128)(2,1)} %add_convert_fusion.3.a_ref), channel_id=1, source_target_pairs={{0,8},{24,16},{1,9},{25,17},{2,10},{26,18},{3,11},{27,19},{4,12},{... | collective-permute-start | bytes 3145736 | tf_op jit(solution)/shard_map/ppermute | solution.py:948
  401.8 5.6 shard_map.171.refs_0_
  407.5 4.9 shard_map.172.a_ref
  417.7 4.9 fusion.1.a_ref
  422.6 6.7 %collective-permute-start.54 = (bf16[256,2816]{1,0:T(8,128)(2,1)S(1)}, bf16[256,2816]{1,0:T(8,128)(2,1)}, u32[]{:S(2)}, u32[]{:S(2)}) collective-permute-start(bf16[256,2816]{1,0:T(8,128)(2,1)S(1)} %fusion.1.a_ref), channel_id=1, source_target_pairs={{0,8},{24,16},{1,9},{25,17},{2,10},{26,18},{3,11},{27,19},{4,12},{... | collective-permute-start | bytes 4325384 | tf_op jit(solution)/shard_map/ppermute | solution.py:948
  451.3 4.2 add_convert_fusion.1.a_ref
  455.4 7.7 %collective-permute-start.60 = (bf16[1024,640]{1,0:T(8,128)(2,1)S(1)}, bf16[1024,640]{1,0:T(8,128)(2,1)S(1)}, u32[]{:S(2)}, u32[]{:S(2)}) collective-permute-start(bf16[1024,640]{1,0:T(8,128)(2,1)S(1)} %add_convert_fusion.1.a_ref), channel_id=1, source_target_pairs={{0,8},{24,16},{1,9},{25,17},{2,10},{26,18},{3,11},{27,19},{4,12},{... | collective-permute-start | bytes 3932168 | tf_op jit(solution)/shard_map/ppermute | solution.py:948
  463.1 4.7 shard_map.176
  490.3 6.0 collective-permute-start.66
  497.9 7.4 %collective-permute-done.58.b_ref = bf16[512,1024]{1,0:T(8,128)(2,1)S(1)} collective-permute-done((bf16[512,1024]{1,0:T(8,128)(2,1)S(1)}, bf16[512,1024]{1,0:T(8,128)(2,1)S(1)}, u32[]{:S(2)}, u32[]{:S(2)}) %collective-permute-start.58) | collective-permute-done | bytes 1048608 | tf_op jit(solution)/shard_map/ppermute | solution.py:954
  510.6 13.4 %collective-permute-done.66.b_ref = bf16[256,2816]{1,0:T(8,128)(2,1)S(1)} collective-permute-done((bf16[256,2816]{1,0:T(8,128)(2,1)S(1)}, bf16[256,2816]{1,0:T(8,128)(2,1)S(1)}, u32[]{:S(2)}, u32[]{:S(2)}) %collective-permute-start.66) | collective-permute-done | bytes 1441824 | tf_op jit(solution)/shard_map/ppermute | solution.py:948
  525.2 6.8 %collective-permute-start.64 = (f32[2,1024]{1,0:T(2,128)S(1)}, f32[2,1024]{1,0:T(2,128)S(1)}, u32[]{:S(2)}, u32[]{:S(2)}) collective-permute-start(f32[2,1024]{1,0:T(2,128)S(1)} %slice_add_fusion), channel_id=1, source_target_pairs={{0,8},{24,16},{1,9},{25,17},{2,10},{26,18},{3,11},{27,19},{4,12},{... | collective-permute-start | bytes 24584 | tf_op jit(solution)/shard_map/ppermute | solution.py:948
  532.0 13.6 %collective-permute-start.72 = (bf16[128,2816]{1,0:T(8,128)(2,1)S(1)}, bf16[128,2816]{1,0:T(8,128)(2,1)S(1)}, u32[]{:S(2)}, u32[]{:S(2)}) collective-permute-start(bf16[128,2816]{1,0:T(8,128)(2,1)S(1)} %fusion.3.a_ref), channel_id=1, source_target_pairs={{0,8},{24,16},{1,9},{25,17},{2,10},{26,18},{3,11},{27,19},{4,12},{... | collective-permute-start | bytes 2162696 | tf_op jit(solution)/shard_map/ppermute | solution.py:948
  551.0 5.3 collective-permute-done.72.b_ref
  558.2 17.6 %collective-permute-start.68 = (bf16[128,2816]{1,0:T(8,128)(2,1)S(1)}, bf16[128,2816]{1,0:T(8,128)(2,1)S(1)}, u32[]{:S(2)}, u32[]{:S(2)}) collective-permute-start(bf16[128,2816]{1,0:T(8,128)(2,1)S(1)} %fusion.4.a_ref), channel_id=1, source_target_pairs={{0,8},{24,16},{1,9},{25,17},{2,10},{26,18},{3,11},{27,19},{4,12},{... | collective-permute-start | bytes 2162696 | tf_op jit(solution)/shard_map/ppermute | solution.py:948
  579.1 4.2 copy.25
  583.3 5.7 collective-permute-done.68.b_ref
  591.6 14.7 %collective-permute-done.75.b_ref = bf16[256,2816]{1,0:T(8,128)(2,1)S(1)} collective-permute-done((bf16[256,2816]{1,0:T(8,128)(2,1)S(1)}, bf16[256,2816]{1,0:T(8,128)(2,1)S(1)}, u32[]{:S(2)}, u32[]{:S(2)}) %collective-permute-start.75) | collective-permute-done | bytes 1441824 | tf_op jit(solution)/shard_map/ppermute | solution.py:954
  617.9 5.9 shard_map.193
  630.6 7.7 %shard_map.195 = f32[1024,2048]{1,0:T(8,128)} custom-call(s32[3]{0:T(128)S(1)} %pad_add_fusion.2.p, f32[1024,2048]{1,0:T(8,128)S(1)} %bitcast.81, f32[1024,2048]{1,0:T(8,128)S(1)} %bitcast.82, bf16[1024,2048]{1,0:T(8,128)(2,1)S(1)} %copy-done.25, f32[1,2048]{1,0:T(1,128)S(1)} %copy-done.51, bf16[512,2048]{1,0:T(8,128)(2,1)S(1)} %copy-done.17, ...), custom_call_target="tpu_custom_call" | custom-call | flops 3000000000 | bytes 8000000 | tf_op jit(solution)/shard_map/pallas_call | solution.py:860
  (488 shorter events, 251.8 us)
Async XLA Ops:
  10.2 32.0 %collective-permute-start.1 = (bf16[1024,640]{1,0:T(8,128)(2,1)}, bf16[1024,640]{1,0:T(8,128)(2,1)}, u32[]{:S(2)}, u32[]{:S(2)}) collective-permute-start(bf16[1024,640]{1,0:T(8,128)(2,1)} %bitcast.109), channel_id=1, source_target_pairs={{0,4},{4,0},{1,5},{5,1},{2,6},{6,2},{3,7},{7,3},{8,12},{12,8},{9,1... | collective-permute-start | bytes 3932168 | tf_op jit(solution)/shard_map/ppermute | solution.py:936
  11.3 44.5 %collective-permute-start.3 = (bf16[512,512]{1,0:T(8,128)(2,1)S(1)}, bf16[512,512]{1,0:T(8,128)(2,1)}, u32[]{:S(2)}, u32[]{:S(2)}) collective-permute-start(bf16[512,512]{1,0:T(8,128)(2,1)S(1)} %dynamic-slice_bitcast_fusion), channel_id=1, source_target_pairs={{0,4},{4,0},{1,5},{5,1},{2,6},{6,2},{3,7},{7,3},{8,12},{12,8},{9,1... | collective-permute-start | bytes 1572872 | tf_op jit(solution)/shard_map/ppermute | solution.py:936
  79.0 35.6 %collective-permute-start.9 = (bf16[256,2816]{1,0:T(8,128)(2,1)}, bf16[256,2816]{1,0:T(8,128)(2,1)}, u32[]{:S(2)}, u32[]{:S(2)}) collective-permute-start(bf16[256,2816]{1,0:T(8,128)(2,1)} %shard_map.142.refs_9_.refs_1_), channel_id=1, source_target_pairs={{0,4},{4,0},{1,5},{5,1},{2,6},{6,2},{3,7},{7,3},{8,12},{12,8},{9,1... | collective-permute-start | bytes 4325384 | tf_op jit(solution)/shard_map/ppermute | solution.py:936
  100.9 29.9 %collective-permute-start.14 = (bf16[128,2816]{1,0:T(8,128)(2,1)}, bf16[128,2816]{1,0:T(8,128)(2,1)S(1)}, u32[]{:S(2)}, u32[]{:S(2)}) collective-permute-start(bf16[128,2816]{1,0:T(8,128)(2,1)} %collective-permute-done.5.refs_14_), channel_id=1, source_target_pairs={{0,8},{8,0},{16,24},{24,16},{1,9},{9,1},{17,25},{25,17},{2,10},{10... | collective-permute-start | bytes 2162696 | tf_op jit(solution)/shard_map/ppermute | solution.py:945
  104.0 27.3 %collective-permute-start.15 = (bf16[128,2816]{1,0:T(8,128)(2,1)S(1)}, bf16[128,2816]{1,0:T(8,128)(2,1)S(1)}, u32[]{:S(2)}, u32[]{:S(2)}) collective-permute-start(bf16[128,2816]{1,0:T(8,128)(2,1)S(1)} %get-tuple-element.518.refs_10_), channel_id=1, source_target_pairs={{0,4},{4,0},{1,5},{5,1},{2,6},{6,2},{3,7},{7,3},{8,12},{12,8},{9,1... | collective-permute-start | bytes 2162696 | tf_op jit(solution)/shard_map/ppermute | solution.py:936
  108.7 36.6 %collective-permute-start.20 = (bf16[128,2816]{1,0:T(8,128)(2,1)S(1)}, bf16[128,2816]{1,0:T(8,128)(2,1)S(1)}, u32[]{:S(2)}, u32[]{:S(2)}) collective-permute-start(bf16[128,2816]{1,0:T(8,128)(2,1)S(1)} %get-tuple-element.519.refs_11_), channel_id=1, source_target_pairs={{0,4},{4,0},{1,5},{5,1},{2,6},{6,2},{3,7},{7,3},{8,12},{12,8},{9,1... | collective-permute-start | bytes 2162696 | tf_op jit(solution)/shard_map/ppermute | solution.py:936
  117.3 50.4 %collective-permute-start.19 = (bf16[256,2816]{1,0:T(8,128)(2,1)}, bf16[256,2816]{1,0:T(8,128)(2,1)}, u32[]{:S(2)}, u32[]{:S(2)}) collective-permute-start(bf16[256,2816]{1,0:T(8,128)(2,1)} %collective-permute-done.9.refs_15_.refs_5_), channel_id=1, source_target_pairs={{0,8},{8,0},{16,24},{24,16},{1,9},{9,1},{17,25},{25,17},{2,10},{10... | collective-permute-start | bytes 4325384 | tf_op jit(solution)/shard_map/ppermute | solution.py:945
  131.3 29.4 %collective-permute-start.21 = (bf16[1408,256]{1,0:T(8,128)(2,1)S(1)}, bf16[1408,256]{1,0:T(8,128)(2,1)}, u32[]{:S(2)}, u32[]{:S(2)}) collective-permute-start(bf16[1408,256]{1,0:T(8,128)(2,1)S(1)} %get-tuple-element.482), channel_id=1, source_target_pairs={{0,4},{4,0},{1,5},{5,1},{2,6},{6,2},{3,7},{7,3},{8,12},{12,8},{9,1... | collective-permute-start | bytes 2162696 | tf_op jit(solution)/shard_map/ppermute | solution.py:936
  164.1 32.8 %collective-permute-start.23 = (bf16[1408,256]{1,0:T(8,128)(2,1)}, bf16[1408,256]{1,0:T(8,128)(2,1)S(1)}, u32[]{:S(2)}, u32[]{:S(2)}) collective-permute-start(bf16[1408,256]{1,0:T(8,128)(2,1)} %get-tuple-element.506), channel_id=1, source_target_pairs={{0,4},{4,0},{1,5},{5,1},{2,6},{6,2},{3,7},{7,3},{8,12},{12,8},{9,1... | collective-permute-start | bytes 2162696 | tf_op jit(solution)/shard_map/ppermute | solution.py:936
  165.9 33.0 %collective-permute-start.24 = (bf16[1408,256]{1,0:T(8,128)(2,1)}, bf16[1408,256]{1,0:T(8,128)(2,1)}, u32[]{:S(2)}, u32[]{:S(2)}) collective-permute-start(bf16[1408,256]{1,0:T(8,128)(2,1)} %get-tuple-element.507), channel_id=1, source_target_pairs={{0,4},{4,0},{1,5},{5,1},{2,6},{6,2},{3,7},{7,3},{8,12},{12,8},{9,1... | collective-permute-start | bytes 2162696 | tf_op jit(solution)/shard_map/ppermute | solution.py:936
  166.2 32.7 %collective-permute-start.22 = (bf16[1408,256]{1,0:T(8,128)(2,1)}, bf16[1408,256]{1,0:T(8,128)(2,1)}, u32[]{:S(2)}, u32[]{:S(2)}) collective-permute-start(bf16[1408,256]{1,0:T(8,128)(2,1)} %collective-permute-done.21.refs_1_), channel_id=1, source_target_pairs={{0,8},{8,0},{16,24},{24,16},{1,9},{9,1},{17,25},{25,17},{2,10},{10... | collective-permute-start | bytes 2162696 | tf_op jit(solution)/shard_map/ppermute | solution.py:945
  191.6 44.2 %collective-permute-start.27 = (bf16[768,1024]{1,0:T(8,128)(2,1)}, bf16[768,1024]{1,0:T(8,128)(2,1)S(1)}, u32[]{:S(2)}, u32[]{:S(2)}) collective-permute-start(bf16[768,1024]{1,0:T(8,128)(2,1)} %fusion.17), channel_id=1, source_target_pairs={{0,4},{4,0},{1,5},{5,1},{2,6},{6,2},{3,7},{7,3},{8,12},{12,8},{9,1... | collective-permute-start | bytes 4718600 | tf_op jit(solution)/shard_map/ppermute | solution.py:936
  234.1 31.6 %collective-permute-start.25 = (bf16[640,1024]{1,0:T(8,128)(2,1)S(1)}, bf16[640,1024]{1,0:T(8,128)(2,1)S(1)}, u32[]{:S(2)}, u32[]{:S(2)}) collective-permute-start(bf16[640,1024]{1,0:T(8,128)(2,1)S(1)} %fusion.20), channel_id=1, source_target_pairs={{0,4},{4,0},{1,5},{5,1},{2,6},{6,2},{3,7},{7,3},{8,12},{12,8},{9,1... | collective-permute-start | bytes 3932168 | tf_op jit(solution)/shard_map/ppermute | solution.py:936
  238.8 43.0 %collective-permute-start.31 = (bf16[768,1024]{1,0:T(8,128)(2,1)}, bf16[768,1024]{1,0:T(8,128)(2,1)}, u32[]{:S(2)}, u32[]{:S(2)}) collective-permute-start(bf16[768,1024]{1,0:T(8,128)(2,1)} %add_convert_fusion.a_ref), channel_id=1, source_target_pairs={{0,8},{24,16},{1,9},{25,17},{2,10},{26,18},{3,11},{27,19},{4,12},{... | collective-permute-start | bytes 4718600 | tf_op jit(solution)/shard_map/ppermute | solution.py:948
  249.9 56.0 %collective-permute-start.40 = (bf16[256,2816]{1,0:T(8,128)(2,1)}, bf16[256,2816]{1,0:T(8,128)(2,1)}, u32[]{:S(2)}, u32[]{:S(2)}) collective-permute-start(bf16[256,2816]{1,0:T(8,128)(2,1)} %convolution_convert_fusion.2), channel_id=1, source_target_pairs={{0,4},{4,0},{1,5},{5,1},{2,6},{6,2},{3,7},{7,3},{8,12},{12,8},{9,1... | collective-permute-start | bytes 4325384 | tf_op jit(solution)/shard_map/ppermute | solution.py:936
  281.8 29.8 %collective-permute-start.38 = (bf16[128,2048]{1,0:T(8,128)(2,1)}, bf16[128,2048]{1,0:T(8,128)(2,1)S(1)}, u32[]{:S(2)}, u32[]{:S(2)}) collective-permute-start(bf16[128,2048]{1,0:T(8,128)(2,1)} %get-tuple-element.606.refs_0_), channel_id=1, source_target_pairs={{0,1},{1,0},{2,3},{3,2},{4,5},{5,4},{6,7},{7,6},{8,9},{9,8},{10,11... | collective-permute-start | bytes 1572872 | tf_op jit(solution)/shard_map/ppermute | solution.py:939
  285.3 58.3 %collective-permute-start.30 = (bf16[640,1024]{1,0:T(8,128)(2,1)S(1)}, bf16[640,1024]{1,0:T(8,128)(2,1)S(1)}, u32[]{:S(2)}, u32[]{:S(2)}) collective-permute-start(bf16[640,1024]{1,0:T(8,128)(2,1)S(1)} %copy-done.63), channel_id=1, source_target_pairs={{0,8},{24,16},{1,9},{25,17},{2,10},{26,18},{3,11},{27,19},{4,12},{... | collective-permute-start | bytes 3932168 | tf_op jit(solution)/shard_map/ppermute | solution.py:948
  291.5 41.3 %collective-permute-start.33 = (bf16[768,1024]{1,0:T(8,128)(2,1)S(1)}, bf16[768,1024]{1,0:T(8,128)(2,1)S(1)}, u32[]{:S(2)}, u32[]{:S(2)}) collective-permute-start(bf16[768,1024]{1,0:T(8,128)(2,1)S(1)} %shard_map.160.a_ref), channel_id=1, source_target_pairs={{8,16},{16,8},{9,17},{17,9},{10,18},{18,10},{11,19},{19,11},{12,20... | collective-permute-start | bytes 4718600 | tf_op jit(solution)/shard_map/ppermute | solution.py:951
  305.9 57.1 %collective-permute-start.41 = (bf16[128,512]{1,0:T(8,128)(2,1)S(1)}, bf16[128,512]{1,0:T(8,128)(2,1)S(1)}, u32[]{:S(2)}, u32[]{:S(2)}) collective-permute-start(bf16[128,512]{1,0:T(8,128)(2,1)S(1)} %get-tuple-element.601), channel_id=1, source_target_pairs={{4,0},{5,1},{6,2},{7,3},{12,8},{13,9},{14,10},{15,11},{20,16},{21,... | collective-permute-start | bytes 393224 | tf_op jit(solution)/shard_map/ppermute | solution.py:1242
  311.6 66.7 %collective-permute-start.46 = (bf16[256,2816]{1,0:T(8,128)(2,1)}, bf16[256,2816]{1,0:T(8,128)(2,1)}, u32[]{:S(2)}, u32[]{:S(2)}) collective-permute-start(bf16[256,2816]{1,0:T(8,128)(2,1)} %fusion.a_ref), channel_id=1, source_target_pairs={{0,8},{24,16},{1,9},{25,17},{2,10},{26,18},{3,11},{27,19},{4,12},{... | collective-permute-start | bytes 4325384 | tf_op jit(solution)/shard_map/ppermute | solution.py:948
  328.4 32.8 %collective-permute-start.42 = (bf16[128,512]{1,0:T(8,128)(2,1)S(1)}, bf16[128,512]{1,0:T(8,128)(2,1)S(1)}, u32[]{:S(2)}, u32[]{:S(2)}) collective-permute-start(bf16[128,512]{1,0:T(8,128)(2,1)S(1)} %get-tuple-element.624), channel_id=1, source_target_pairs={{4,0},{5,1},{6,2},{7,3},{12,8},{13,9},{14,10},{15,11},{20,16},{21,... | collective-permute-start | bytes 393224 | tf_op jit(solution)/shard_map/ppermute | solution.py:1242
  332.8 49.5 %collective-permute-start.45 = (bf16[512,1024]{1,0:T(8,128)(2,1)}, bf16[512,1024]{1,0:T(8,128)(2,1)}, u32[]{:S(2)}, u32[]{:S(2)}) collective-permute-start(bf16[512,1024]{1,0:T(8,128)(2,1)} %add_convert_fusion.4), channel_id=1, source_target_pairs={{0,4},{4,0},{1,5},{5,1},{2,6},{6,2},{3,7},{7,3},{8,12},{12,8},{9,1... | collective-permute-start | bytes 3145736 | tf_op jit(solution)/shard_map/ppermute | solution.py:936
  343.5 56.3 %collective-permute-start.44 = (bf16[768,1024]{1,0:T(8,128)(2,1)}, bf16[768,1024]{1,0:T(8,128)(2,1)}, u32[]{:S(2)}, u32[]{:S(2)}) collective-permute-start(bf16[768,1024]{1,0:T(8,128)(2,1)} %shard_map.165.a_ref), channel_id=1, source_target_pairs={{8,0},{16,24},{9,1},{17,25},{10,2},{18,26},{11,3},{19,27},{12,4},{... | collective-permute-start | bytes 4718600 | tf_op jit(solution)/shard_map/ppermute | solution.py:954
  361.2 46.2 %collective-permute-start.43 = (bf16[640,1024]{1,0:T(8,128)(2,1)}, bf16[640,1024]{1,0:T(8,128)(2,1)}, u32[]{:S(2)}, u32[]{:S(2)}) collective-permute-start(bf16[640,1024]{1,0:T(8,128)(2,1)} %shard_map.166.a_ref), channel_id=1, source_target_pairs={{8,16},{16,8},{9,17},{17,9},{10,18},{18,10},{11,19},{19,11},{12,20... | collective-permute-start | bytes 3932168 | tf_op jit(solution)/shard_map/ppermute | solution.py:951
  368.3 49.4 %collective-permute-start.49 = (bf16[256,2816]{1,0:T(8,128)(2,1)}, bf16[256,2816]{1,0:T(8,128)(2,1)}, u32[]{:S(2)}, u32[]{:S(2)}) collective-permute-start(bf16[256,2816]{1,0:T(8,128)(2,1)} %convolution_convert_fusion.1), channel_id=1, source_target_pairs={{0,4},{4,0},{1,5},{5,1},{2,6},{6,2},{3,7},{7,3},{8,12},{12,8},{9,1... | collective-permute-start | bytes 4325384 | tf_op jit(solution)/shard_map/ppermute | solution.py:936
  387.7 41.7 %collective-permute-start.48 = (bf16[512,1024]{1,0:T(8,128)(2,1)}, bf16[512,1024]{1,0:T(8,128)(2,1)}, u32[]{:S(2)}, u32[]{:S(2)}) collective-permute-start(bf16[512,1024]{1,0:T(8,128)(2,1)} %add_convert_fusion.3.a_ref), channel_id=1, source_target_pairs={{0,8},{24,16},{1,9},{25,17},{2,10},{26,18},{3,11},{27,19},{4,12},{... | collective-permute-start | bytes 3145736 | tf_op jit(solution)/shard_map/ppermute | solution.py:948
  394.9 38.2 %collective-permute-start.47 = (bf16[256,2816]{1,0:T(8,128)(2,1)}, bf16[256,2816]{1,0:T(8,128)(2,1)}, u32[]{:S(2)}, u32[]{:S(2)}) collective-permute-start(bf16[256,2816]{1,0:T(8,128)(2,1)} %shard_map.170.a_ref), channel_id=1, source_target_pairs={{8,16},{16,8},{9,17},{17,9},{10,18},{18,10},{11,19},{19,11},{12,20... | collective-permute-start | bytes 4325384 | tf_op jit(solution)/shard_map/ppermute | solution.py:951
  399.8 51.3 %collective-permute-start.56 = (bf16[1024,640]{1,0:T(8,128)(2,1)}, bf16[1024,640]{1,0:T(8,128)(2,1)}, u32[]{:S(2)}, u32[]{:S(2)}) collective-permute-start(bf16[1024,640]{1,0:T(8,128)(2,1)} %fusion.23), channel_id=1, source_target_pairs={{0,4},{4,0},{1,5},{5,1},{2,6},{6,2},{3,7},{7,3},{8,12},{12,8},{9,1... | collective-permute-start | bytes 3932168 | tf_op jit(solution)/shard_map/ppermute | solution.py:936
  412.3 43.1 %collective-permute-start.55 = (bf16[640,1024]{1,0:T(8,128)(2,1)}, bf16[640,1024]{1,0:T(8,128)(2,1)}, u32[]{:S(2)}, u32[]{:S(2)}) collective-permute-start(bf16[640,1024]{1,0:T(8,128)(2,1)} %shard_map.172.a_ref), channel_id=1, source_target_pairs={{8,0},{16,24},{9,1},{17,25},{10,2},{18,26},{11,3},{19,27},{12,4},{... | collective-permute-start | bytes 3932168 | tf_op jit(solution)/shard_map/ppermute | solution.py:954
  417.6 194.7 %all-reduce.4.cloned.1.call-start = ((), (), s32[]{:S(2)}) async-start(), calls=%async_computation | async-start | bytes 16777216 | tf_op jit(solution)/shard_map/psum | solution.py:1266
  422.6 45.2 %collective-permute-start.54 = (bf16[256,2816]{1,0:T(8,128)(2,1)S(1)}, bf16[256,2816]{1,0:T(8,128)(2,1)}, u32[]{:S(2)}, u32[]{:S(2)}) collective-permute-start(bf16[256,2816]{1,0:T(8,128)(2,1)S(1)} %fusion.1.a_ref), channel_id=1, source_target_pairs={{0,8},{24,16},{1,9},{25,17},{2,10},{26,18},{3,11},{27,19},{4,12},{... | collective-permute-start | bytes 4325384 | tf_op jit(solution)/shard_map/ppermute | solution.py:948
  437.1 38.4 %collective-permute-start.52 = (bf16[256,2816]{1,0:T(8,128)(2,1)}, bf16[256,2816]{1,0:T(8,128)(2,1)}, u32[]{:S(2)}, u32[]{:S(2)}) collective-permute-start(bf16[256,2816]{1,0:T(8,128)(2,1)} %shard_map.175.a_ref), channel_id=1, source_target_pairs={{8,0},{16,24},{9,1},{17,25},{10,2},{18,26},{11,3},{19,27},{12,4},{... | collective-permute-start | bytes 4325384 | tf_op jit(solution)/shard_map/ppermute | solution.py:954
  451.2 34.8 %collective-permute-start.61 = (bf16[256,2816]{1,0:T(8,128)(2,1)}, bf16[256,2816]{1,0:T(8,128)(2,1)S(1)}, u32[]{:S(2)}, u32[]{:S(2)}) collective-permute-start(bf16[256,2816]{1,0:T(8,128)(2,1)} %convolution_convert_fusion), channel_id=1, source_target_pairs={{0,4},{4,0},{1,5},{5,1},{2,6},{6,2},{3,7},{7,3},{8,12},{12,8},{9,1... | collective-permute-start | bytes 4325384 | tf_op jit(solution)/shard_map/ppermute | solution.py:936
  455.4 34.9 %collective-permute-start.60 = (bf16[1024,640]{1,0:T(8,128)(2,1)S(1)}, bf16[1024,640]{1,0:T(8,128)(2,1)S(1)}, u32[]{:S(2)}, u32[]{:S(2)}) collective-permute-start(bf16[1024,640]{1,0:T(8,128)(2,1)S(1)} %add_convert_fusion.1.a_ref), channel_id=1, source_target_pairs={{0,8},{24,16},{1,9},{25,17},{2,10},{26,18},{3,11},{27,19},{4,12},{... | collective-permute-start | bytes 3932168 | tf_op jit(solution)/shard_map/ppermute | solution.py:948
  470.1 26.6 %collective-permute-start.59 = (bf16[256,2816]{1,0:T(8,128)(2,1)S(1)}, bf16[256,2816]{1,0:T(8,128)(2,1)S(1)}, u32[]{:S(2)}, u32[]{:S(2)}) collective-permute-start(bf16[256,2816]{1,0:T(8,128)(2,1)S(1)} %shard_map.177.a_ref), channel_id=1, source_target_pairs={{8,16},{16,8},{9,17},{17,9},{10,18},{18,10},{11,19},{19,11},{12,20... | collective-permute-start | bytes 4325384 | tf_op jit(solution)/shard_map/ppermute | solution.py:951
  473.7 31.6 %collective-permute-start.58 = (bf16[512,1024]{1,0:T(8,128)(2,1)S(1)}, bf16[512,1024]{1,0:T(8,128)(2,1)S(1)}, u32[]{:S(2)}, u32[]{:S(2)}) collective-permute-start(bf16[512,1024]{1,0:T(8,128)(2,1)S(1)} %shard_map.178.a_ref), channel_id=1, source_target_pairs={{8,0},{16,24},{9,1},{17,25},{10,2},{18,26},{11,3},{19,27},{12,4},{... | collective-permute-start | bytes 3145736 | tf_op jit(solution)/shard_map/ppermute | solution.py:954
  480.6 29.1 %collective-permute-start.67 = (bf16[128,2816]{1,0:T(8,128)(2,1)S(1)}, bf16[128,2816]{1,0:T(8,128)(2,1)S(1)}, u32[]{:S(2)}, u32[]{:S(2)}) collective-permute-start(bf16[128,2816]{1,0:T(8,128)(2,1)S(1)} %convolution_convert_fusion.4), channel_id=1, source_target_pairs={{0,4},{4,0},{1,5},{5,1},{2,6},{6,2},{3,7},{7,3},{8,12},{12,8},{9,1... | collective-permute-start | bytes 2162696 | tf_op jit(solution)/shard_map/ppermute | solution.py:936
  490.3 33.7 %collective-permute-start.66 = (bf16[256,2816]{1,0:T(8,128)(2,1)S(1)}, bf16[256,2816]{1,0:T(8,128)(2,1)S(1)}, u32[]{:S(2)}, u32[]{:S(2)}) collective-permute-start(bf16[256,2816]{1,0:T(8,128)(2,1)S(1)} %fusion.2.a_ref), channel_id=1, source_target_pairs={{0,8},{24,16},{1,9},{25,17},{2,10},{26,18},{3,11},{27,19},{4,12},{... | collective-permute-start | bytes 4325384 | tf_op jit(solution)/shard_map/ppermute | solution.py:948
  496.8 35.2 %collective-permute-start.65 = (bf16[1024,640]{1,0:T(8,128)(2,1)S(1)}, bf16[1024,640]{1,0:T(8,128)(2,1)S(1)}, u32[]{:S(2)}, u32[]{:S(2)}) collective-permute-start(bf16[1024,640]{1,0:T(8,128)(2,1)S(1)} %shard_map.180.a_ref), channel_id=1, source_target_pairs={{8,16},{16,8},{9,17},{17,9},{10,18},{18,10},{11,19},{19,11},{12,20... | collective-permute-start | bytes 3932168 | tf_op jit(solution)/shard_map/ppermute | solution.py:951
  505.3 41.9 %collective-permute-start.63 = (bf16[256,2816]{1,0:T(8,128)(2,1)S(1)}, bf16[256,2816]{1,0:T(8,128)(2,1)S(1)}, u32[]{:S(2)}, u32[]{:S(2)}) collective-permute-start(bf16[256,2816]{1,0:T(8,128)(2,1)S(1)} %shard_map.181.a_ref), channel_id=1, source_target_pairs={{8,0},{16,24},{9,1},{17,25},{10,2},{18,26},{11,3},{19,27},{12,4},{... | collective-permute-start | bytes 4325384 | tf_op jit(solution)/shard_map/ppermute | solution.py:954
  509.5 40.5 %collective-permute-start.62 = (bf16[128,2816]{1,0:T(8,128)(2,1)S(1)}, bf16[128,2816]{1,0:T(8,128)(2,1)S(1)}, u32[]{:S(2)}, u32[]{:S(2)}) collective-permute-start(bf16[128,2816]{1,0:T(8,128)(2,1)S(1)} %convolution_convert_fusion.3), channel_id=1, source_target_pairs={{0,4},{4,0},{1,5},{5,1},{2,6},{6,2},{3,7},{7,3},{8,12},{12,8},{9,1... | collective-permute-start | bytes 2162696 | tf_op jit(solution)/shard_map/ppermute | solution.py:936
  524.4 32.1 %collective-permute-start.71 = (bf16[256,2816]{1,0:T(8,128)(2,1)S(1)}, bf16[256,2816]{1,0:T(8,128)(2,1)S(1)}, u32[]{:S(2)}, u32[]{:S(2)}) collective-permute-start(bf16[256,2816]{1,0:T(8,128)(2,1)S(1)} %shard_map.183.a_ref), channel_id=1, source_target_pairs={{8,16},{16,8},{9,17},{17,9},{10,18},{18,10},{11,19},{19,11},{12,20... | collective-permute-start | bytes 4325384 | tf_op jit(solution)/shard_map/ppermute | solution.py:951
  545.9 32.8 %collective-permute-start.69 = (bf16[1024,640]{1,0:T(8,128)(2,1)S(1)}, bf16[1024,640]{1,0:T(8,128)(2,1)S(1)}, u32[]{:S(2)}, u32[]{:S(2)}) collective-permute-start(bf16[1024,640]{1,0:T(8,128)(2,1)S(1)} %shard_map.184.a_ref), channel_id=1, source_target_pairs={{8,0},{16,24},{9,1},{17,25},{10,2},{18,26},{11,3},{19,27},{12,4},{... | collective-permute-start | bytes 3932168 | tf_op jit(solution)/shard_map/ppermute | solution.py:954
  556.9 49.3 %collective-permute-start.75 = (bf16[256,2816]{1,0:T(8,128)(2,1)S(1)}, bf16[256,2816]{1,0:T(8,128)(2,1)S(1)}, u32[]{:S(2)}, u32[]{:S(2)}) collective-permute-start(bf16[256,2816]{1,0:T(8,128)(2,1)S(1)} %shard_map.187.a_ref), channel_id=1, source_target_pairs={{8,0},{16,24},{9,1},{17,25},{10,2},{18,26},{11,3},{19,27},{12,4},{... | collective-permute-start | bytes 4325384 | tf_op jit(solution)/shard_map/ppermute | solution.py:954
  558.2 30.8 %collective-permute-start.68 = (bf16[128,2816]{1,0:T(8,128)(2,1)S(1)}, bf16[128,2816]{1,0:T(8,128)(2,1)S(1)}, u32[]{:S(2)}, u32[]{:S(2)}) collective-permute-start(bf16[128,2816]{1,0:T(8,128)(2,1)S(1)} %fusion.4.a_ref), channel_id=1, source_target_pairs={{0,8},{24,16},{1,9},{25,17},{2,10},{26,18},{3,11},{27,19},{4,12},{... | collective-permute-start | bytes 2162696 | tf_op jit(solution)/shard_map/ppermute | solution.py:948
  577.2 31.7 %collective-permute-start.74 = (f32[2,1024]{1,0:T(2,128)S(1)}, f32[2,1024]{1,0:T(2,128)S(1)}, u32[]{:S(2)}, u32[]{:S(2)}) collective-permute-start(f32[2,1024]{1,0:T(2,128)S(1)} %add.169), channel_id=1, source_target_pairs={{8,0},{16,24},{9,1},{17,25},{10,2},{18,26},{11,3},{19,27},{12,4},{... | collective-permute-start | bytes 24584 | tf_op jit(solution)/shard_map/ppermute | solution.py:954
  590.3 33.6 %collective-permute-start.77 = (bf16[128,2816]{1,0:T(8,128)(2,1)S(1)}, bf16[128,2816]{1,0:T(8,128)(2,1)S(1)}, u32[]{:S(2)}, u32[]{:S(2)}) collective-permute-start(bf16[128,2816]{1,0:T(8,128)(2,1)S(1)} %shard_map.190.a_ref), channel_id=1, source_target_pairs={{8,0},{16,24},{9,1},{17,25},{10,2},{18,26},{11,3},{19,27},{12,4},{... | collective-permute-start | bytes 2162696 | tf_op jit(solution)/shard_map/ppermute | solution.py:954
  611.0 27.3 %collective-permute-start.78 = (bf16[128,2816]{1,0:T(8,128)(2,1)}, bf16[128,2816]{1,0:T(8,128)(2,1)}, u32[]{:S(2)}, u32[]{:S(2)}) collective-permute-start(bf16[128,2816]{1,0:T(8,128)(2,1)} %shard_map.192.a_ref), channel_id=1, source_target_pairs={{8,0},{16,24},{9,1},{17,25},{10,2},{18,26},{11,3},{19,27},{12,4},{... | collective-permute-start | bytes 2162696 | tf_op jit(solution)/shard_map/ppermute | solution.py:954
  (149 other events, 1411.6 us)
Sparse Core Ops, SparseCore 0:
  450.5 155.6 all-reduce.3
